TPU v7x, 256 devices: a whole 4x4x8 slice. The times are simulated.
256 devices in a mesh: grp: 2 (over x_lo), gx: 16 (over z, x_hi), gy: 8 (over y, core).
Axes of the slice: x: 4 (x_hi: 2, x_lo: 2; x = x_hi * 2 + x_lo), y: 4, z: 8, core: 2. Of those that a mesh axis runs over, the one named last changes fastest.
Arguments:
- theta_anomaly: float32 [768, 128, 128], P(('grp', 'gx'), 'gy'), may hold values from -4 to 4
- humidity_ratio: float32 [768, 128, 128], P(('grp', 'gx'), 'gy'), may hold values from 0.6 to 1.4
- zonal_velocity: float32 [768, 128, 128], P(('grp', 'gx'), 'gy'), may hold values from -1.8 to 1.8
- meridional_velocity: float32 [768, 128, 128], P(('grp', 'gx'), 'gy'), may hold values from -1.8 to 1.8
- vertical_velocity: float32 [768, 128, 128], P(('grp', 'gx'), 'gy'), may hold values from -1.8 to 1.8
- patch_processor_map: int32 [32, 8, 8], P(('grp', 'gx'), 'gy'), may hold values from 0 to 15, as said below
- particle_bucket_population: int32 [32, 8, 16], P(('grp', 'gx'), 'gy'), may hold values from 0 to 1024, as said below
- particle_size_quadratic: float32 [32, 8, 16, 1024], P(('grp', 'gx'), 'gy'), may hold values from 0.25 to 4
- represented_number: float32 [32, 8, 16, 1024], P(('grp', 'gx'), 'gy'), may hold values from 0.5 to 2
- particle_location_number: int32 [32, 8, 16, 1024], P(('grp', 'gx'), 'gy'), may hold values from 48 to 6095, as said below
Outputs:
- final_temperature: float32 [768, 128, 128], P(('grp', 'gx'), 'gy')
- final_vapour: float32 [768, 128, 128], P(('grp', 'gx'), 'gy')
- final_east: float32 [768, 128, 128], P(('grp', 'gx'), 'gy')
- final_north: float32 [768, 128, 128], P(('grp', 'gx'), 'gy')
- final_vertical: float32 [768, 128, 128], P(('grp', 'gx'), 'gy')
- final_size_quadratic: float32 [32, 8, 16, 1024], P(('grp', 'gx'), 'gy')
Inputs may be any that keep to these rules, and one draw needn't show every extreme that they name: `patch_processor_map`: entry [a, y, b] is the index along gx of the device in the same row (same grp half, same gy) that holds the droplets of column block b of device (a, y). Different blocks of one device go to different owners, so one device sends at most 1 block to one owner; in every row some owner holds 1 block from every device of the row. `particle_bucket_population`: entry [a, y, r] counts the live droplets of slot r = s x 1 + t of the owner (a, y); they are the first ones of the slot. A slot that receives no block has none; every slot of an owner that holds 1 block from every device is full. `particle_location_number`: the cell within the slot's block, column 128 + level, with levels from 48 to 79. Within a slot the live droplets are sorted by column, and so are the others.
All inputs are finite; a program needn't handle non-finite values.
Results may differ from a plain program's by a relative error of at most 0.0003.
Values sent between devices are 32-bit elements; how exact they have to be, the bound alone decides.
No kernel may reach another device: no remote copies, remote signals or barrier semaphores. Data moves between devices by JAX's collectives and lax.ppermute only.
A program may use at most 64 MiB of HBM per device.

v0:
```python
import jax
import jax.numpy as jnp
from jax import lax
from jax.sharding import PartitionSpec as P

NBD = 8
NSUB = 4
ITERS = 4


TIME_INCREMENT = 0.15
THERMAL_LIFT = 0.5
HUMID_LIFT = 0.3
HELMHOLTZ = 0.001
CLAUSIUS_FACTOR = 0.2
GROWTH = 0.5
GROWTH_SLOPE = 0.1
SUB_STEP = 0.25
CURVATURE = 0.05
FLOOR_SQUARE = 0.04
CONDENSE = 0.2
PHASE_WARMING = 2.5


def with_halo(block, sides, width):
    for axis, dim in sides:
        count = lax.axis_size(axis)
        forward = [(i, i + 1) for i in range(count - 1)]
        forward.append((count - 1, 0))
        backward = [(target, source) for source, target in forward]
        low = lax.ppermute(
            lax.slice_in_dim(block, block.shape[dim] - width, None, axis=dim), axis, forward
        )
        high = lax.ppermute(lax.slice_in_dim(block, 0, width, axis=dim), axis, backward)
        block = jnp.concatenate([low, block, high], axis=dim)
    return block


def surround(stacked):
    return with_halo(stacked, ((("grp", "gx"), 1), ("gy", 2)), 1)


def beside(padded):
    return (
        padded[:, 2:, 1:-1, :],
        padded[:, :-2, 1:-1, :],
        padded[:, 1:-1, 2:, :],
        padded[:, 1:-1, :-2, :],
    )


def level_above(values):
    return jnp.concatenate([values[..., 1:], jnp.zeros_like(values[..., :1])], axis=-1)


def level_below(values):
    return jnp.concatenate([jnp.zeros_like(values[..., :1]), values[..., :-1]], axis=-1)


def profiles(layer_altitudes):
    heights = jnp.arange(layer_altitudes, dtype=jnp.float32)
    midpoint_mass_per_volume = jnp.exp(-(heights + 0.5) / layer_altitudes)
    interface_mass_per_volume = jnp.where(
        heights < layer_altitudes - 1, jnp.exp(-(heights + 1.0) / layer_altitudes), 0.0
    )
    return (midpoint_mass_per_volume, interface_mass_per_volume)


def operate(values, midpoint_mass_per_volume, interface_mass_per_volume):
    east_side, west_side, north_side, south_side = beside(surround(values[None]))
    return (
        midpoint_mass_per_volume
        * ((4.0 + HELMHOLTZ) * values - east_side[0] - west_side[0] - north_side[0] - south_side[0])
        + interface_mass_per_volume * (values - level_above(values))
        + level_below(interface_mass_per_volume) * (values - level_below(values))
    )


def squares(residual):
    return lax.psum(jnp.sum(residual * residual), ("grp", "gx", "gy"))


def solve_pressure(right_side, midpoint_mass_per_volume, interface_mass_per_volume):
    potential = jnp.zeros_like(right_side)
    residual = right_side
    direction = right_side
    norm_now = squares(residual)
    for iteration in range(ITERS):
        applied = operate(direction, midpoint_mass_per_volume, interface_mass_per_volume)
        step_length = norm_now / lax.psum(jnp.sum(direction * applied), ("grp", "gx", "gy"))
        potential = potential + step_length * direction
        residual = residual - step_length * applied
        norm_next = squares(residual)
        direction = residual + norm_next / norm_now * direction
        norm_now = norm_next
    return potential


def momentum_update(
    theta_anomaly,
    humidity_ratio,
    zonal_velocity,
    meridional_velocity,
    vertical_velocity,
    midpoint_mass_per_volume,
    interface_mass_per_volume,
):
    raised_airmass = vertical_velocity + TIME_INCREMENT * (
        THERMAL_LIFT * theta_anomaly + HUMID_LIFT * humidity_ratio
    )
    east_side, west_side, north_side, south_side = beside(
        surround(jnp.stack([zonal_velocity, meridional_velocity]))
    )
    divergence = midpoint_mass_per_volume * (
        (east_side[0] - west_side[0]) * 0.5 + (north_side[1] - south_side[1]) * 0.5
    ) + 0.5 * (
        level_above(midpoint_mass_per_volume * raised_airmass)
        - level_below(midpoint_mass_per_volume * raised_airmass)
    )
    potential = solve_pressure(
        -divergence / TIME_INCREMENT, midpoint_mass_per_volume, interface_mass_per_volume
    )
    pot_east, pot_west, pot_north, pot_south = beside(surround(potential[None]))
    zonal_velocity = zonal_velocity - TIME_INCREMENT * 0.5 * (pot_east[0] - pot_west[0])
    meridional_velocity = meridional_velocity - TIME_INCREMENT * 0.5 * (pot_north[0] - pot_south[0])
    vertical_velocity = raised_airmass - TIME_INCREMENT * 0.5 * (
        level_above(potential) - level_below(potential)
    )
    scalar_quantities = jnp.stack([theta_anomaly, humidity_ratio])
    tra_east, tra_west, tra_north, tra_south = beside(surround(scalar_quantities))
    lower_level = jnp.concatenate(
        [scalar_quantities[..., :1], scalar_quantities[..., :-1]], axis=-1
    )
    upper_level = jnp.concatenate(
        [scalar_quantities[..., 1:], scalar_quantities[..., -1:]], axis=-1
    )
    tendency = (
        jnp.maximum(zonal_velocity, 0.0) * (scalar_quantities - tra_west)
        + jnp.minimum(zonal_velocity, 0.0) * (tra_east - scalar_quantities)
        + jnp.maximum(meridional_velocity, 0.0) * (scalar_quantities - tra_south)
        + jnp.minimum(meridional_velocity, 0.0) * (tra_north - scalar_quantities)
        + jnp.maximum(vertical_velocity, 0.0) * (scalar_quantities - lower_level)
        + jnp.minimum(vertical_velocity, 0.0) * (upper_level - scalar_quantities)
    )
    moved = scalar_quantities - TIME_INCREMENT * tendency
    return (moved[0], moved[1], zonal_velocity, meridional_velocity, vertical_velocity)


def grow_droplets(supersat_ratio, warmth, particle_size_quadratic, represented_number, alive_mask):
    growth_rate = GROWTH * jnp.exp(GROWTH_SLOPE * warmth)
    square_now = particle_size_quadratic
    for substep in range(NSUB):
        square_now = jnp.maximum(
            square_now
            + 2.0 * SUB_STEP * growth_rate * (supersat_ratio - CURVATURE / jnp.sqrt(square_now)),
            FLOOR_SQUARE,
        )
    grown_square = jnp.where(alive_mask, square_now, particle_size_quadratic)
    mass_change = jnp.where(
        alive_mask,
        represented_number
        * (
            grown_square * jnp.sqrt(grown_square)
            - particle_size_quadratic * jnp.sqrt(particle_size_quadratic)
        ),
        0.0,
    )
    return (grown_square, mass_change)


def grow_rows(columns, radius_squared_rows, mult_rows, local_cell, alive_mask):
    row_count = columns.shape[0]
    thermal_couple = columns.reshape(row_count, 2, -1)
    cells_per = thermal_couple.shape[2]
    supersat_ratio = jnp.take_along_axis(thermal_couple[:, 0], local_cell, axis=1)
    warmth = jnp.take_along_axis(thermal_couple[:, 1], local_cell, axis=1)
    grown_square, mass_change = grow_droplets(
        supersat_ratio, warmth, radius_squared_rows, mult_rows, alive_mask
    )
    flat_cell = local_cell + cells_per * jnp.arange(row_count, dtype=jnp.int32)[:, None]
    liquid_content = CONDENSE * jax.ops.segment_sum(
        mass_change.reshape(-1), flat_cell.reshape(-1), num_segments=row_count * cells_per
    )
    return (grown_square, liquid_content.reshape(row_count, cells_per))


def into_patches(values):
    domain_length_east, domain_length_north, layer_depth = values.shape
    shaped = values.reshape(domain_length_east, NBD, domain_length_north // NBD, layer_depth)
    return shaped.transpose(1, 0, 2, 3).reshape(NBD, -1)


def from_blocks(blocks, domain_length_east, domain_length_north, layer_depth):
    shaped = blocks.reshape(NBD, domain_length_east, domain_length_north // NBD, layer_depth)
    return shaped.transpose(1, 0, 2, 3).reshape(
        domain_length_east, domain_length_north, layer_depth
    )


def routing_plan(owner_row, slots, row_count):
    row_index = jnp.arange(row_count, dtype=jnp.int32)[:, None]
    block_index = jnp.arange(owner_row.shape[0], dtype=jnp.int32)[None, :]
    matches = (owner_row[None, :] == row_index // slots) & (
        block_index % slots == row_index % slots
    )
    return matches.astype(jnp.float32)


def on_device(
    theta_anomaly,
    humidity_ratio,
    zonal_velocity,
    meridional_velocity,
    vertical_velocity,
    patch_processor_map,
    particle_bucket_population,
    particle_size_quadratic,
    represented_number,
    particle_location_number,
):
    domain_length_east, domain_length_north, layer_altitudes = theta_anomaly.shape
    midpoint_mass_per_volume, interface_mass_per_volume = profiles(layer_altitudes)
    radius_squared_rows = particle_size_quadratic[0, 0]
    mult_rows = represented_number[0, 0]
    cell_rows = particle_location_number[0, 0]
    count_rows = particle_bucket_population[0, 0]
    row_count = radius_squared_rows.shape[0]
    slots = row_count // lax.axis_size("gx")
    routing = routing_plan(patch_processor_map[0, 0], slots, row_count)
    layer_low = 0
    layer_depth = layer_altitudes - layer_low
    local_cell = (
        cell_rows // layer_altitudes * layer_depth + cell_rows % layer_altitudes - layer_low
    )
    alive_mask = (
        jnp.arange(radius_squared_rows.shape[1], dtype=jnp.int32)[None, :] < count_rows[:, None]
    )
    advected_theta, advected_humidity, zonal_velocity, meridional_velocity, vertical_velocity = (
        momentum_update(
            theta_anomaly,
            humidity_ratio,
            zonal_velocity,
            meridional_velocity,
            vertical_velocity,
            midpoint_mass_per_volume,
            interface_mass_per_volume,
        )
    )
    supersat_ratio = advected_humidity * jnp.exp(-CLAUSIUS_FACTOR * advected_theta) - 1.0
    thermal_couple = jnp.stack(
        [into_patches(supersat_ratio), into_patches(advected_theta)], axis=1
    ).reshape(NBD, -1)
    columns = jnp.dot(routing, thermal_couple, precision=lax.Precision.HIGHEST)
    arrived_columns = lax.all_to_all(columns, "gx", split_axis=0, concat_axis=0, tiled=True)
    radius_squared_rows, owner_rows = grow_rows(
        arrived_columns, radius_squared_rows, mult_rows, local_cell, alive_mask
    )
    condensed_rows = lax.all_to_all(owner_rows, "gx", split_axis=0, concat_axis=0, tiled=True)
    liquid_content = from_blocks(
        jnp.dot(routing.T, condensed_rows, precision=lax.Precision.HIGHEST),
        domain_length_east,
        domain_length_north,
        layer_depth,
    )
    theta_anomaly = advected_theta + PHASE_WARMING * liquid_content
    humidity_ratio = advected_humidity - liquid_content
    return (
        theta_anomaly,
        humidity_ratio,
        zonal_velocity,
        meridional_velocity,
        vertical_velocity,
        radius_squared_rows[None, None],
    )


def solution(mesh):
    placed = (
        P(("grp", "gx"), "gy", None),
        P(("grp", "gx"), "gy", None),
        P(("grp", "gx"), "gy", None),
        P(("grp", "gx"), "gy", None),
        P(("grp", "gx"), "gy", None),
        P(("grp", "gx"), "gy", None),
        P(("grp", "gx"), "gy", None),
        P(("grp", "gx"), "gy", None, None),
        P(("grp", "gx"), "gy", None, None),
        P(("grp", "gx"), "gy", None, None),
    )
    return jax.shard_map(
        on_device,
        mesh=mesh,
        in_specs=placed,
        out_specs=(
            P(("grp", "gx"), "gy", None),
            P(("grp", "gx"), "gy", None),
            P(("grp", "gx"), "gy", None),
            P(("grp", "gx"), "gy", None),
            P(("grp", "gx"), "gy", None),
            P(("grp", "gx"), "gy", None, None),
        ),
        check_vma=False,
    )
```

profile of v0, /device:TPU:1, one launch (start us, length us, event | category | flops | bytes accessed | tf_op | source)
XLA Modules:
  0.0 1049.9 jit_solution(11866780198976958518)
XLA Ops:
  0.7 0.8 pad_maximum_fusion.74
  1.5 8.6 collective-permute-start
  10.1 1.1 copy_bitcast_fusion.3
  11.9 4.8 collective-permute-start.23
  17.0 0.7 copy-done
  17.8 1.5 collective-permute-start.2
  19.3 1.2 collective-permute-start.3
  20.5 1.5 collective-permute-done.2
  22.2 3.3 collective-permute-start.4
  25.6 0.7 collective-permute-done.4
  26.3 5.0 collective-permute-done.5
  31.4 4.5 collective-permute-start.6
  36.0 0.7 collective-permute-done.6
  37.1 0.8 multiply_reduce_fusion.5
  37.9 73.7 %all-reduce.12 = (f32[]{:T(128)}, f32[]{:T(128)}) all-reduce(f32[]{:T(128)} %get-tuple-element.38, f32[]{:T(128)} %get-tuple-element.37), channel_id=1, replica_groups=mesh['grp'=2,'gx'=16,'gy'=8] {'grp','gx','gy'}, use_global_device_ids=true, to_apply=%region_1.2 | all-reduce | flops 2 | bytes 16 | tf_op jit(solution)/shard_map/psum | solution.py:80
  112.9 0.7 multiply_reduce_fusion.4
  113.6 74.4 %psum.58 = f32[]{:T(128)} all-reduce(f32[]{:T(128)} %multiply_reduce_fusion.4), channel_id=1, replica_groups=mesh['grp'=2,'gx'=16,'gy'=8] {'grp','gx','gy'}, use_global_device_ids=true, to_apply=%region_5.6 | all-reduce | flops 1 | bytes 8 | tf_op jit(solution)/shard_map/psum | solution.py:80
  189.5 3.0 collective-permute-start.8
  192.7 0.9 collective-permute-done.8
  193.6 4.7 collective-permute-done.9
  198.3 2.1 collective-permute-start.10
  200.5 0.9 collective-permute-done.10
  201.6 0.8 multiply_reduce_fusion.3
  202.3 73.6 %psum.59 = f32[]{:T(128)} all-reduce(f32[]{:T(128)} %get-tuple-element.53), channel_id=1, replica_groups=mesh['grp'=2,'gx'=16,'gy'=8] {'grp','gx','gy'}, use_global_device_ids=true, to_apply=%region_7.8 | all-reduce | flops 1 | bytes 8 | tf_op jit(solution)/shard_map/psum | solution.py:90
  277.3 0.7 multiply_reduce_fusion.2
  277.9 74.4 %psum.60 = f32[]{:T(128)} all-reduce(f32[]{:T(128)} %get-tuple-element.51), channel_id=1, replica_groups=mesh['grp'=2,'gx'=16,'gy'=8] {'grp','gx','gy'}, use_global_device_ids=true, to_apply=%region_9.10 | all-reduce | flops 1 | bytes 8 | tf_op jit(solution)/shard_map/psum | solution.py:80
  353.7 3.0 collective-permute-start.12
  356.8 0.9 fusion.3
  357.6 0.7 copy.105
  358.3 4.2 collective-permute-done.13
  362.6 2.1 collective-permute-start.14
  364.8 0.9 collective-permute-done.14
  365.9 0.8 multiply_reduce_fusion.1
  366.6 73.6 %psum.61 = f32[]{:T(128)} all-reduce(f32[]{:T(128)} %get-tuple-element.49), channel_id=1, replica_groups=mesh['grp'=2,'gx'=16,'gy'=8] {'grp','gx','gy'}, use_global_device_ids=true, to_apply=%region_11.12 | all-reduce | flops 1 | bytes 8 | tf_op jit(solution)/shard_map/psum | solution.py:90
  441.6 0.7 multiply_reduce_fusion
  442.3 1.5 copy.104
  443.9 74.4 %psum.62 = f32[]{:T(128)} all-reduce(f32[]{:T(128)} %multiply_reduce_fusion), channel_id=1, replica_groups=mesh['grp'=2,'gx'=16,'gy'=8] {'grp','gx','gy'}, use_global_device_ids=true, to_apply=%region_13.14 | all-reduce | flops 1 | bytes 8 | tf_op jit(solution)/shard_map/psum | solution.py:80
  519.7 3.0 collective-permute-start.16
  522.8 0.7 pad_maximum_fusion.69
  523.4 2.2 collective-permute-start.26
  525.7 2.9 collective-permute-done.17
  528.6 2.1 collective-permute-start.18
  530.8 0.9 collective-permute-done.18
  531.9 0.8 fusion.38
  532.6 74.9 %psum.63 = f32[]{:T(128)} all-reduce(f32[]{:T(128)} %fusion.38), channel_id=1, replica_groups=mesh['grp'=2,'gx'=16,'gy'=8] {'grp','gx','gy'}, use_global_device_ids=true, to_apply=%region_15.16 | all-reduce | flops 1 | bytes 8 | tf_op jit(solution)/shard_map/psum | solution.py:90
  609.1 2.8 collective-permute-start.20
  612.3 0.9 collective-permute-done.20
  613.2 4.5 collective-permute-done.21
  617.8 2.1 collective-permute-start.24
  620.0 0.9 collective-permute-done.24
  622.2 0.7 copy-done.4
  622.8 1.2 fusion.10
  625.6 1.7 copy.93
  627.3 4.3 all-to-all-start
  632.2 19.9 %all-to-all-done = f32[16,1,12288]{2,1,0:T(1,128)S(1)} async-done(((f32[16,1,12288]{2,1,0:T(1,128)}), f32[16,1,12288]{2,1,0:T(1,128)S(1)}, u32[]{:S(2)}, u32[]{:S(2)}) %all-to-all-start) | async-done | bytes 786464 | tf_op jit(solution)/shard_map/all_to_all | solution.py:254
  652.1 1.9 reduce
  654.0 0.7 reshape.224
  655.4 129.7 %gather_fusion = f32[16384]{0:T(1024)S(1)} fusion(f32[16,6144]{1,0:T(8,128)S(1)} %bitcast.261, s32[16384]{0:T(1024)S(1)} %bitcast.262), kind=kCustom, calls=%fused_computation.clone | custom fusion | bytes 262144 | tf_op jit(solution)/shard_map/jit(take_along_axis)/gather | solution.py:176
  785.3 129.7 %gather_fusion.1 = f32[16384]{0:T(1024)S(1)} fusion(f32[16,6144]{1,0:T(8,128)S(1)} %bitcast.260, s32[16384]{0:T(1024)S(1)} %bitcast.263), kind=kCustom, calls=%fused_computation.1.clone | custom fusion | bytes 262144 | tf_op jit(solution)/shard_map/jit(take_along_axis)/gather | solution.py:175
  915.1 0.8 fusion.99
  916.0 112.9 %scatter_custom_fusion = f32[98304]{0:T(1024)S(1)} fusion(s32[16384]{0:T(1024)S(1)} %bitcast.291, f32[16384]{0:T(1024)S(1)} %bitcast.292, f32[]{:T(128)} %constant.104.clone.1), kind=kCustom, calls=%fused_computation.183 | custom fusion | flops 16384 | bytes 393220 | tf_op jit(solution)/shard_map/scatter-add | solution.py:181
  1029.0 18.6 %all_to_all.21 = f32[16,1,6144]{2,1,0:T(1,128)S(1)} all-to-all(f32[16,1,6144]{2,1,0:T(1,128)S(1)} %bitcast.284), channel_id=1, replica_groups=mesh['grp'=2,'gx'=16,'gy'=8] {'gx'}, dimensions={0} | all-to-all | bytes 786432 | tf_op jit(solution)/shard_map/all_to_all | solution.py:258
  1048.5 0.7 copy.98
  1049.2 0.7 copy.99
  (140 shorter events, 9.0 us)
Async XLA Ops:
  0.6 16.1 %copy-start.2 = (f32[24,16,128]{2,1,0:T(8,128)S(1)}, f32[24,16,128]{2,1,0:T(8,128)}, u32[]{:S(2)}) copy-start(f32[24,16,128]{2,1,0:T(8,128)} %param.13) | copy-start | bytes 589828
  0.6 16.0 %copy-start.3 = (f32[24,16,128]{2,1,0:T(8,128)S(1)}, f32[24,16,128]{2,1,0:T(8,128)}, u32[]{:S(2)}) copy-start(f32[24,16,128]{2,1,0:T(8,128)} %param.12) | copy-start | bytes 589828
  0.7 16.0 %copy-start.6 = (f32[24,16,128]{2,1,0:T(8,128)S(1)}, f32[24,16,128]{2,1,0:T(8,128)}, u32[]{:S(2)}) copy-start(f32[24,16,128]{2,1,0:T(8,128)} %param.16) | copy-start | bytes 589828
  1.5 15.5 %collective-permute-start = (f32[2,1,16,128]{3,2,1,0:T(8,128)S(1)}, f32[2,1,16,128]{3,2,1,0:T(8,128)S(1)}, u32[]{:S(2)}, u32[]{:S(2)}) collective-permute-start(f32[2,1,16,128]{3,2,1,0:T(8,128)S(1)} %get-tuple-element.69), channel_id=1, source_target_pairs={{8,0},{16,8},{24,16},{32,24},{40,32},{48,40},{56,48},{64,56},{72,6... | collective-permute-start | bytes 49160 | tf_op jit(solution)/shard_map/ppermute | solution.py:34
  10.1 6.9 collective-permute-start.1
  11.9 510.9 %collective-permute-start.22 = (f32[2,1,16,128]{3,1,2,0:T(1,128)}, f32[2,1,16,128]{3,1,2,0:T(1,128)S(1)}, u32[]{:S(2)}, u32[]{:S(2)}) collective-permute-start(f32[2,1,16,128]{3,1,2,0:T(1,128)} %get-tuple-element.74), channel_id=1, source_target_pairs={{0,8},{8,16},{16,24},{24,32},{32,40},{40,48},{48,56},{56,64},{64,7... | collective-permute-start | bytes 49160 | tf_op jit(solution)/shard_map/ppermute | solution.py:31
  11.9 510.9 %collective-permute-start.23 = (f32[2,1,16,128]{3,1,2,0:T(1,128)}, f32[2,1,16,128]{3,1,2,0:T(1,128)}, u32[]{:S(2)}, u32[]{:S(2)}) collective-permute-start(f32[2,1,16,128]{3,1,2,0:T(1,128)} %get-tuple-element.75), channel_id=1, source_target_pairs={{8,0},{16,8},{24,16},{32,24},{40,32},{48,40},{56,48},{64,56},{72,6... | collective-permute-start | bytes 49160 | tf_op jit(solution)/shard_map/ppermute | solution.py:34
  16.7 184.9 %copy-start.15 = (f32[128]{0:T(128)}, f32[128]{0:T(128)S(1)}, u32[]{:S(2)}) copy-start(f32[128]{0:T(128)S(1)} %multiply_exponential_fusion) | copy-start | bytes 1540
  16.7 0.9 copy-start
  16.7 1.0 copy-start.1
  16.9 184.6 %copy-start.18 = (f32[128]{0:T(128)}, f32[128]{0:T(128)S(1)}, u32[]{:S(2)}) copy-start(f32[128]{0:T(128)S(1)} %compare_select_fusion.4) | copy-start | bytes 1540
  17.8 4.2 collective-permute-start.2
  19.3 2.7 collective-permute-start.3
  22.2 4.1 collective-permute-start.4
  25.5 5.8 collective-permute-start.5
  25.6 176.0 %copy-start.21 = (f32[128]{0:T(128)}, f32[128]{0:T(128)S(1)}, u32[]{:S(2)}) copy-start(f32[128]{0:T(128)S(1)} %pad_maximum_fusion.91) | copy-start | bytes 1540
  31.4 5.4 collective-permute-start.6
  35.9 1.2 collective-permute-start.7
  189.5 4.1 collective-permute-start.8
  192.4 5.8 collective-permute-start.9
  198.3 3.1 collective-permute-start.10
  200.4 1.2 collective-permute-start.11
  353.7 4.6 collective-permute-start.12
  356.7 5.8 collective-permute-start.13
  357.6 8.3 copy-start.16
  357.6 8.3 copy-start.19
  357.6 8.3 copy-start.22
  362.6 3.1 collective-permute-start.14
  364.7 1.2 collective-permute-start.15
  519.7 12.2 %copy-start.17 = (f32[128]{0:T(128)S(1)}, f32[128]{0:T(128)}, u32[]{:S(2)}) copy-start(f32[128]{0:T(128)} %copy-done.15) | copy-start | bytes 1540
  519.7 12.2 %copy-start.20 = (f32[128]{0:T(128)S(1)}, f32[128]{0:T(128)}, u32[]{:S(2)}) copy-start(f32[128]{0:T(128)} %copy-done.18) | copy-start | bytes 1540
  519.7 12.2 %copy-start.23 = (f32[128]{0:T(128)S(1)}, f32[128]{0:T(128)}, u32[]{:S(2)}) copy-start(f32[128]{0:T(128)} %copy-done.21) | copy-start | bytes 1540
  519.7 6.0 collective-permute-start.16
  522.7 5.8 collective-permute-start.17
  523.4 98.7 %collective-permute-start.26 = (f32[2,26,1,128]{3,1,2,0:T(8,128)S(1)}, f32[2,26,1,128]{3,1,2,0:T(8,128)S(1)}, u32[]{:S(2)}, u32[]{:S(2)}) collective-permute-start(f32[2,26,1,128]{3,1,2,0:T(8,128)S(1)} %get-tuple-element.64), channel_id=1, source_target_pairs={{0,1},{1,2},{2,3},{3,4},{4,5},{5,6},{6,7},{7,0},{8,9},{9,10},{10,1... | collective-permute-start | bytes 79880 | tf_op jit(solution)/shard_map/ppermute | solution.py:31
  525.7 96.5 %collective-permute-start.27 = (f32[2,26,1,128]{3,1,2,0:T(8,128)S(1)}, f32[2,26,1,128]{3,1,2,0:T(8,128)S(1)}, u32[]{:S(2)}, u32[]{:S(2)}) collective-permute-start(f32[2,26,1,128]{3,1,2,0:T(8,128)S(1)} %get-tuple-element.65), channel_id=1, source_target_pairs={{1,0},{2,1},{3,2},{4,3},{5,4},{6,5},{7,6},{0,7},{9,8},{10,9},{11,1... | collective-permute-start | bytes 79880 | tf_op jit(solution)/shard_map/ppermute | solution.py:34
  528.6 3.1 collective-permute-start.18
  530.7 1.2 collective-permute-start.19
  608.9 3.3 copy-start.7
  609.1 4.1 collective-permute-start.20
  611.9 5.8 collective-permute-start.21
  612.3 8.8 copy-start.5
  617.8 3.1 collective-permute-start.24
  619.9 1.2 collective-permute-start.25
  621.2 0.7 copy-start.8
  621.2 0.8 copy-start.9
  621.8 1.0 copy-start.4
  624.3 0.7 copy-start.24
  627.3 4.3 copy-start.11
  627.3 4.3 copy-start.12
  627.3 4.8 copy-start.10
  627.3 24.8 %all-to-all-start = ((f32[16,1,12288]{2,1,0:T(1,128)}), f32[16,1,12288]{2,1,0:T(1,128)S(1)}, u32[]{:S(2)}, u32[]{:S(2)}) async-start(f32[16,1,12288]{2,1,0:T(1,128)} %copy.93), calls=%async_computation | async-start | bytes 1572864 | tf_op jit(solution)/shard_map/all_to_all | solution.py:254
  785.3 129.8 %copy-start.13 = (f32[1,1,16,1024]{3,2,1,0:T(8,128)S(1)}, f32[1,1,16,1024]{3,2,1,0:T(8,128)}, u32[]{:S(2)}) copy-start(f32[1,1,16,1024]{3,2,1,0:T(8,128)} %param.19) | copy-start | bytes 196612
  785.3 129.8 %copy-start.14 = (f32[1,1,16,1024]{3,2,1,0:T(8,128)S(1)}, f32[1,1,16,1024]{3,2,1,0:T(8,128)}, u32[]{:S(2)}) copy-start(f32[1,1,16,1024]{3,2,1,0:T(8,128)} %param.20) | copy-start | bytes 196612
  785.3 129.8 %copy-start.25 = (s32[1,1,16]{2,1,0:T(1,128)S(1)}, s32[1,1,16]{2,1,0:T(1,128)}, u32[]{:S(2)}) copy-start(s32[1,1,16]{2,1,0:T(1,128)} %param.18) | copy-start | bytes 196
where the time goes:
time: 1060 us; the launch traced here: 1050 us
  blocking collectives  538 us (51%)
  local copies, waits for them, and re-layouts  272 us (26%)
  other arithmetic  127 us (12%)
  starting transfers between devices  51.1 us (5%)
  waiting for transfers between devices  50.5 us (5%)
  between operations  10.8 us (1%)
    psum x4, blocking collectives, squares(): return lax.psum(jnp.sum(residual * residual), ('grp', 'gx', 'gy'))  297 us
    psum x3, blocking collectives, solve_pressure(): lax.psum(jnp.sum(direction * applied), ('grp', 'gx', 'gy'))  222 us
    gather x2, local copies, waits for them, and re-layouts, grow_rows(): warmth = jnp.take_along_axis(thermal_couple[:, 1], local_cell, axis=1)  130 us
    gather x2, local copies, waits for them, and re-layouts, grow_rows(): jnp.take_along_axis(thermal_couple[:, 0], local_cell, axis=1)  130 us
    scatter-add x1, other arithmetic, grow_rows(): jax.ops.segment_sum(mass_change.reshape(-1), flat_cell.reshape(-1), num_s...  113 us
    ppermute x14, starting transfers between devices, with_halo(): lax.ppermute(lax.slice_in_dim(block, 0, width, axis=dim), axis, backward)  43 us
    ppermute x14, waiting for transfers between devices, with_halo(): lax.ppermute(lax.slice_in_dim(block, block.shape[dim] - width, None, axis...  22.2 us
  transfers between devices with their start and end apart: 29, of which 20 were waited for; matrix products, arithmetic and copies ran while one was open for 1% of the time, Pallas kernels for 0%

commit v1 on v0

v1 whole, which is shorter than its diff:
```python
import functools

import jax
import jax.numpy as jnp
from jax import lax
from jax.experimental import pallas as pl
from jax.experimental.pallas import tpu as pltpu
from jax.sharding import PartitionSpec as P

TIME_INCREMENT = 0.15
THERMAL_LIFT = 0.5
HUMID_LIFT = 0.3
HELMHOLTZ = 0.001
CLAUSIUS_FACTOR = 0.2
GROWTH = 0.5
GROWTH_SLOPE = 0.1
SUB_STEP = 0.25
CURVATURE = 0.05
FLOOR_SQUARE = 0.04
CONDENSE = 0.2
PHASE_WARMING = 2.5

NSUB = 4
ITERS = 4
NBD = 8
CX = 24
CY = 16
LEVELS = 128
KLO = 48
BAND = 32
EX = 32
EY = 24
SLOT_ROWS = 16
DPB = 1024
CHUNKS = DPB // LEVELS
PARCEL = 32
SCALE = 1.0 / 6.0
VMEM_LIMIT = 24 * 1024 * 1024

f32 = jnp.float32
bf16 = jnp.bfloat16


def iota(shape, axis):
    return lax.broadcasted_iota(jnp.int32, shape, axis)


def vertical_profiles():
    level = iota((1, LEVELS), 1)
    height = level.astype(f32)
    centre = jnp.exp(-(height + 0.5) / LEVELS)
    face = jnp.where(level < LEVELS - 1, jnp.exp(-(height + 1.0) / LEVELS), 0.0)
    face_below = jnp.where(level > 0, jnp.exp(-height / LEVELS), 0.0)
    return level, centre, face, face_below


def turn(values, by, axis):
    return pltpu.roll(values, by % values.shape[axis], axis)


def lifted_row(i, theta, humidity, vertical):
    return vertical[i] + TIME_INCREMENT * (THERMAL_LIFT * theta[i] + HUMID_LIFT * humidity[i])


def right_side_kernel(theta, humidity, zonal, meridional, vertical, partial, to_south, to_north):
    level, centre, _, _ = vertical_profiles()
    sub = iota((CY, LEVELS), 0)
    sub8 = iota((8, LEVELS), 0)
    for i in range(CX):
        weighted = centre * lifted_row(i, theta, humidity, vertical)
        rise = jnp.where(level < LEVELS - 1, turn(weighted, -1, 1), 0.0) - jnp.where(
            level > 0, turn(weighted, 1, 1), 0.0
        )
        if i == 0:
            across = zonal[1]
        elif i == CX - 1:
            across = -zonal[CX - 2]
        else:
            across = zonal[i + 1] - zonal[i - 1]
        wind = meridional[i]
        along = jnp.where(sub < CY - 1, turn(wind, -1, 0), 0.0) - jnp.where(
            sub > 0, turn(wind, 1, 0), 0.0
        )
        right = (centre * (across * 0.5 + along * 0.5) + 0.5 * rise) * (-1.0 / TIME_INCREMENT)
        partial[i] = right
        warm = theta[i]
        damp = humidity[i]
        to_south[i] = jnp.where(
            sub8 < 4,
            right[0:8],
            jnp.where(sub8 == 4, wind[0:1], jnp.where(sub8 == 5, warm[0:1], damp[0:1])),
        )
        to_north[i] = jnp.where(
            sub8 >= 4,
            right[8:16],
            jnp.where(sub8 == 0, wind[15:16], jnp.where(sub8 == 1, warm[15:16], damp[15:16])),
        )
    for place, i in ((CX, 0), (CX + 1, CX - 1)):
        to_south[place] = zonal[i, 0:8]
        to_north[place] = zonal[i, 8:16]


def joined(north, south):
    return jnp.where(iota((8, LEVELS), 0) < 4, north, south)


def completed_row(i, partial, meridional, from_north, from_south, third):
    sub8 = iota((8, LEVELS), 0)
    north = from_north[i]
    south = from_south[i]
    wind = meridional[i]
    low = partial[i, 0:8] + jnp.where(sub8 == 0, third * south[0:1], 0.0)
    high = partial[i, 8:16] - jnp.where(sub8 == 7, third * north[4:5], 0.0)
    halo = (
        joined(north, south)
        + jnp.where(sub8 == 0, third * wind[15:16], 0.0)
        - jnp.where(sub8 == 7, third * wind[0:1], 0.0)
    )
    return low, high, halo


def side_kernel(
    partial, from_north, from_south, theta, humidity, zonal, meridional, to_west, to_east
):
    _, centre, _, _ = vertical_profiles()
    third = centre * (0.5 / TIME_INCREMENT)
    for target, first, edge, place in ((to_west, 0, 0, CX), (to_east, CX - 4, CX - 1, CX + 1)):
        for t in range(4):
            low, high, halo = completed_row(
                first + t, partial, meridional, from_north, from_south, third
            )
            target[t, 0:8] = low
            target[t, 8:16] = high
            target[t, 16:24] = halo
        target[4, 0:16] = zonal[edge]
        target[4, 16:24] = joined(from_north[place], from_south[place])
        target[5, 0:16] = theta[edge]
        target[5, 16:24] = jnp.zeros((8, LEVELS), f32)
        target[6, 0:16] = humidity[edge]
        target[6, 16:24] = jnp.zeros((8, LEVELS), f32)


def power_kernel(
    counts,
    partial,
    from_north,
    from_south,
    meridional,
    to_west,
    to_east,
    from_east,
    from_west,
    squares,
    numbers,
    cells,
    powers,
    parcels,
):
    _, centre, face, face_below = vertical_profiles()
    third = centre * (0.5 / TIME_INCREMENT)
    for i in range(4, CX - 4):
        low, high, halo = completed_row(i, partial, meridional, from_north, from_south, third)
        powers[0, i, 0:8] = low
        powers[0, i, 8:16] = high
        powers[0, i, 16:24] = halo
    for t in range(4):
        west = to_west[t]
        east = to_east[t]
        far_east = from_east[t]
        far_west = from_west[t]
        if t == 0:
            west = west + third * from_west[4]
            far_east = far_east + third * to_east[4]
        if t == 3:
            east = east - third * from_east[4]
            far_west = far_west - third * to_west[4]
        powers[0, t] = west
        powers[0, CX - 4 + t] = east
        powers[0, CX + t] = far_east
        powers[0, CX + 4 + t] = far_west
    here = ((4.0 + HELMHOLTZ) * centre + face + face_below) * SCALE
    beside = centre * SCALE
    above = face * SCALE
    below = face_below * SCALE

    def applied(j, i):
        values = powers[j, i]
        lateral = (
            powers[j, (i + 1) % EX]
            + powers[j, (i - 1) % EX]
            + turn(values, -1, 0)
            + turn(values, 1, 0)
        )
        return (
            here * values
            - beside * lateral
            - above * turn(values, -1, 1)
            - below * turn(values, 1, 1)
        )

    for j in range(ITERS - 1):
        reach = ITERS - 1 - j
        for i in range(-reach, CX + reach):
            powers[j + 1, i % EX] = applied(j, i % EX)
    sums = [jnp.zeros((8, LEVELS), f32) for _ in range(2 * ITERS)]
    for i in range(CX):
        rows = [powers[j, i, 0:16] for j in range(ITERS)]
        rows.append(applied(ITERS - 1, i)[0:16])
        for k in range(2 * ITERS):
            product = rows[k // 2] * rows[(k + 1) // 2]
            sums[k] = sums[k] + (product[0:8] + product[8:16])
    sub8 = iota((8, LEVELS), 0)
    packed = jnp.zeros((8, LEVELS), f32)
    for k in range(2 * ITERS):
        packed = jnp.where(sub8 == k, jnp.sum(sums[k], axis=0, keepdims=True), packed)
    for r in range(SLOT_ROWS):
        parcels[PARCEL * r + 24 : PARCEL * r + 32] = packed
    row = iota((SLOT_ROWS, LEVELS), 0)
    lane = iota((SLOT_ROWS, LEVELS), 1)
    live = jnp.zeros((SLOT_ROWS, LEVELS), jnp.int32)
    for r in range(SLOT_ROWS):
        live = jnp.where(row == r, counts[r], live)
    for s in range(CHUNKS):
        part = slice(LEVELS * s, LEVELS * (s + 1))
        parcels[pl.ds(s, SLOT_ROWS, stride=PARCEL), :] = squares[:, part]
        parcels[pl.ds(8 + s, SLOT_ROWS, stride=PARCEL), :] = jnp.where(
            lane + LEVELS * s < live, numbers[:, part], 0.0
        )
        parcels[pl.ds(16 + s, SLOT_ROWS, stride=PARCEL), :] = cells[:, part].astype(f32)


def two_sum(a, b):
    s = a + b
    t = s - a
    return s, (a - (s - t)) + (b - t)


def quick_sum(a, b):
    s = a + b
    return s, b - (s - a)


def split(a):
    t = a * 4097.0
    high = t - (t - a)
    return high, a - high


def two_product(a, b):
    p = a * b
    ah, al = split(a)
    bh, bl = split(b)
    return p, ((ah * bh - p) + ah * bl + al * bh) + al * bl


def pair_add(a, b):
    s, e = two_sum(a[0], b[0])
    return quick_sum(s, e + (a[1] + b[1]))


def pair_mul(a, b):
    p, e = two_product(a[0], b[0])
    return quick_sum(p, e + (a[0] * b[1] + a[1] * b[0]))


def pair_sub_mul(a, b, c):
    p = pair_mul(b, c)
    return pair_add(a, (-p[0], -p[1]))


def pair_inverse(a):
    guess = 1.0 / a[0]
    p = pair_mul(a, (guess, jnp.zeros_like(guess)))
    rest = (1.0 - p[0]) - p[1]
    return quick_sum(guess, guess * rest)


def coefficients(totals):
    high = totals[0]
    low = jnp.zeros_like(high)
    for t in range(1, totals.shape[0]):
        high, e = two_sum(high, totals[t])
        low = low + e
    by = LEVELS // 2
    high, low = quick_sum(high, low)
    while by:
        high, low = pair_add((high, low), (turn(high, by, 1), turn(low, by, 1)))
        by //= 2
    moment = []
    for k in range(2 * ITERS):
        moment.append(
            (
                jnp.broadcast_to(high[k : k + 1], (8, LEVELS)),
                jnp.broadcast_to(low[k : k + 1], (8, LEVELS)),
            )
        )
    matrix = [[moment[i + j + 1] for j in range(ITERS)] for i in range(ITERS)]
    side = [moment[i] for i in range(ITERS)]
    inverse = []
    for k in range(ITERS):
        inverse.append(pair_inverse(matrix[k][k]))
        for i in range(k + 1, ITERS):
            factor = pair_mul(matrix[k][i], inverse[k])
            for j in range(i, ITERS):
                matrix[i][j] = pair_sub_mul(matrix[i][j], factor, matrix[k][j])
            side[i] = pair_sub_mul(side[i], factor, side[k])
    result = [None] * ITERS
    for k in reversed(range(ITERS)):
        rest = side[k]
        for j in range(k + 1, ITERS):
            rest = pair_sub_mul(rest, matrix[k][j], result[j])
        result[k] = pair_mul(rest, inverse[k])
    return [(r[0] + r[1])[0:1] * SCALE for r in result]


def halves(values):
    high = values.astype(bf16).astype(f32)
    return high, values - high


def step_kernel(
    owners,
    totals,
    powers,
    arrived,
    theta,
    humidity,
    zonal,
    meridional,
    vertical,
    from_north,
    from_south,
    from_east,
    from_west,
    new_theta,
    new_humidity,
    new_zonal,
    new_meridional,
    new_vertical,
    returned,
    potential,
    excess,
    warmth,
    vapour,
    picked_excess,
    picked_warmth,
    mass,
    condensed,
):
    level, _, _, _ = vertical_profiles()
    sub = iota((CY, LEVELS), 0)
    weights = coefficients(totals)
    for t in range(CX + 2):
        i = (t - 1) % EX
        total = weights[0] * powers[0, i]
        for j in range(1, ITERS):
            total = total + weights[j] * powers[j, i]
        potential[t] = total
    half = TIME_INCREMENT * 0.5
    for i in range(CX):
        here = potential[i + 1]
        east = zonal[i] - half * (potential[i + 2, 0:16] - potential[i, 0:16])
        north = meridional[i] - half * (turn(here, -1, 0)[0:16] - turn(here, 1, 0)[0:16])
        mid = here[0:16]
        up = lifted_row(i, theta, humidity, vertical) - half * (
            jnp.where(level < LEVELS - 1, turn(mid, -1, 1), 0.0)
            - jnp.where(level > 0, turn(mid, 1, 1), 0.0)
        )
        new_zonal[i] = east
        new_meridional[i] = north
        new_vertical[i] = up
        moved = []
        for f, (field, side, in_north, in_south) in enumerate(
            ((theta, 5, 5, 1), (humidity, 6, 6, 2))
        ):
            values = field[i]
            f_e = field[i + 1] if i < CX - 1 else from_east[side, 0:16]
            f_w = field[i - 1] if i > 0 else from_west[side, 0:16]
            f_n = jnp.where(
                sub < CY - 1, turn(values, -1, 0), from_north[i, in_north : in_north + 1]
            )
            f_s = jnp.where(sub > 0, turn(values, 1, 0), from_south[i, in_south : in_south + 1])
            f_t = jnp.where(level < LEVELS - 1, turn(values, -1, 1), values)
            f_b = jnp.where(level > 0, turn(values, 1, 1), values)
            tendency = (
                jnp.maximum(east, 0.0) * (values - f_w)
                + jnp.minimum(east, 0.0) * (f_e - values)
                + jnp.maximum(north, 0.0) * (values - f_s)
                + jnp.minimum(north, 0.0) * (f_n - values)
                + jnp.maximum(up, 0.0) * (values - f_b)
                + jnp.minimum(up, 0.0) * (f_t - values)
            )
            moved.append(values - TIME_INCREMENT * tendency)
        rows = slice(CY * i, CY * (i + 1))
        warmth[rows] = moved[0]
        vapour[rows] = moved[1]
        excess[rows] = moved[1] * jnp.exp(-CLAUSIUS_FACTOR * moved[0]) - 1.0

    lane = iota((2 * CX, LEVELS), 1)
    height = iota((BAND, 2 * LEVELS), 0)
    place = iota((2 * CX, 2 * LEVELS), 0)

    def band(field, b):
        values = jnp.concatenate(
            [
                field[pl.ds(2 * b, CX, stride=CY), :],
                field[pl.ds(2 * b + 1, CX, stride=CY), :],
            ],
            axis=0,
        )
        high, low = halves(values)
        both = jnp.where(lane < BAND, turn(high, -KLO, 1), turn(low, BAND - KLO, 1))
        return both[:, : 2 * BAND].astype(bf16)

    def chunk(values, t):
        return jnp.concatenate([values[2 * t : 2 * t + 1], values[2 * t + 1 : 2 * t + 2]], axis=1)

    def where_at(b):
        cell = arrived[owners[b], 16:24].astype(jnp.int32)
        column = lax.shift_right_logical(cell, 7)
        return (
            jnp.bitwise_and(cell, LEVELS - 1) - KLO,
            jnp.bitwise_and(column, 1) * CX + lax.shift_right_logical(column, 1),
        )

    for b in range(NBD):
        table = jnp.concatenate([band(excess, b), band(warmth, b)], axis=0)
        heights, places = where_at(b)
        for t in range(CHUNKS // 2):
            hot = jnp.where(height == chunk(heights, t), 1.0, 0.0).astype(bf16)
            found = jnp.dot(
                table, jnp.concatenate([hot, hot], axis=0), preferred_element_type=f32
            )
            mine = place == chunk(places, t)
            for target, part in ((picked_excess, found[: 2 * CX]), (picked_warmth, found[2 * CX :])):
                value = jnp.sum(jnp.where(mine, part, 0.0), axis=0, keepdims=True)
                row = CHUNKS * b + 2 * t
                target[row : row + 1] = value[:, :LEVELS]
                target[row + 1 : row + 2] = value[:, LEVELS:]
    returned[...] = jnp.zeros(returned.shape, f32)
    for b in range(NBD):
        rows = slice(CHUNKS * b, CHUNKS * (b + 1))
        owner = owners[b]
        old = arrived[owner, 0:8]
        number = arrived[owner, 8:16]
        oversaturation = picked_excess[rows]
        rate = GROWTH * jnp.exp(GROWTH_SLOPE * picked_warmth[rows])
        now = old
        for substep in range(NSUB):
            now = jnp.maximum(
                now + 2.0 * SUB_STEP * rate * (oversaturation - CURVATURE / jnp.sqrt(now)),
                FLOOR_SQUARE,
            )
        mass[rows] = jnp.where(
            number > 0.0, number * (now * jnp.sqrt(now) - old * jnp.sqrt(old)), 0.0
        )
        returned[owner] = now
    for b in range(NBD):
        heights, places = where_at(b)
        gained = mass[CHUNKS * b : CHUNKS * (b + 1)]
        total = jnp.zeros((4 * CX, BAND), f32)
        for t in range(CHUNKS // 2):
            hot = jnp.where(height == chunk(heights, t), 1.0, 0.0).astype(bf16)
            mine = place == chunk(places, t)
            high, low = halves(chunk(gained, t))
            spread = jnp.concatenate(
                [
                    jnp.where(mine, high, 0.0).astype(bf16),
                    jnp.where(mine, low, 0.0).astype(bf16),
                ],
                axis=0,
            )
            total = total + lax.dot_general(
                spread, hot, (((1,), (1,)), ((), ())), preferred_element_type=f32
            )
        liquid = CONDENSE * (total[: 2 * CX] + total[2 * CX :])
        liquid = jnp.concatenate([liquid, jnp.zeros((2 * CX, LEVELS - BAND), f32)], axis=1)
        liquid = turn(liquid, KLO, 1)
        condensed[pl.ds(2 * b, CX, stride=CY), :] = liquid[:CX]
        condensed[pl.ds(2 * b + 1, CX, stride=CY), :] = liquid[CX:]
    for i in range(CX):
        rows = slice(CY * i, CY * (i + 1))
        new_theta[i] = warmth[rows] + PHASE_WARMING * condensed[rows]
        new_humidity[i] = vapour[rows] - condensed[rows]


def size_kernel(counts, returned, squares, new_squares):
    row = iota((SLOT_ROWS, LEVELS), 0)
    lane = iota((SLOT_ROWS, LEVELS), 1)
    live = jnp.zeros((SLOT_ROWS, LEVELS), jnp.int32)
    for r in range(SLOT_ROWS):
        live = jnp.where(row == r, counts[r], live)
    for s in range(CHUNKS):
        part = slice(LEVELS * s, LEVELS * (s + 1))
        new_squares[:, part] = jnp.where(
            lane + LEVELS * s < live,
            returned[pl.ds(s, SLOT_ROWS, stride=CHUNKS), :],
            squares[:, part],
        )


def local(kernel, outs, scalars, operands, scratch=(), cost=(1_000_000, 1_000_000)):
    whole = pl.BlockSpec(memory_space=pltpu.VMEM)
    single = len(outs) == 1
    return pl.pallas_call(
        kernel,
        out_shape=outs[0] if single else outs,
        in_specs=[pl.BlockSpec(memory_space=pltpu.SMEM)] * len(scalars) + [whole] * len(operands),
        out_specs=whole if single else [whole] * len(outs),
        scratch_shapes=list(scratch),
        compiler_params=pltpu.CompilerParams(vmem_limit_bytes=VMEM_LIMIT),
        cost_estimate=pl.CostEstimate(flops=cost[0], bytes_accessed=cost[1], transcendentals=0),
    )(*scalars, *operands)


def shape(*dims):
    return jax.ShapeDtypeStruct(dims, f32)


def ring(axes, step):
    count = lax.axis_size(axes)
    return [(i, (i + step) % count) for i in range(count)]


def on_device(
    theta, humidity, zonal, meridional, vertical, owner_map, population, squares, numbers, cells
):
    owners = owner_map.reshape(NBD)
    counts = population.reshape(SLOT_ROWS)
    squares = squares.reshape(SLOT_ROWS, DPB)
    numbers = numbers.reshape(SLOT_ROWS, DPB)
    cells = cells.reshape(SLOT_ROWS, DPB)
    tiles = ("grp", "gx")
    tile = shape(CX, CY, LEVELS)
    partial, to_south, to_north = local(
        right_side_kernel,
        [tile, shape(CX + 2, 8, LEVELS), shape(CX + 2, 8, LEVELS)],
        [],
        [theta, humidity, zonal, meridional, vertical],
    )
    from_north = lax.ppermute(to_south, "gy", ring("gy", -1))
    from_south = lax.ppermute(to_north, "gy", ring("gy", 1))
    to_west, to_east = local(
        side_kernel,
        [shape(7, EY, LEVELS), shape(7, EY, LEVELS)],
        [],
        [partial, from_north, from_south, theta, humidity, zonal, meridional],
    )
    from_east = lax.ppermute(to_west, tiles, ring(tiles, -1))
    from_west = lax.ppermute(to_east, tiles, ring(tiles, 1))
    powers, parcels = local(
        power_kernel,
        [shape(ITERS, EX, EY, LEVELS), shape(SLOT_ROWS * PARCEL, LEVELS)],
        [counts],
        [
            partial,
            from_north,
            from_south,
            meridional,
            to_west,
            to_east,
            from_east,
            from_west,
            squares,
            numbers,
            cells,
        ],
    )
    parcels = parcels.reshape(SLOT_ROWS, PARCEL, LEVELS)
    arrived = lax.all_to_all(parcels, "gx", split_axis=0, concat_axis=0, tiled=True)
    shared = jnp.broadcast_to(jnp.sum(arrived[:, 24:], axis=0)[None], (16, 8, LEVELS))
    totals = lax.all_to_all(shared, ("grp", "gy"), split_axis=0, concat_axis=0, tiled=True)
    flat = (CX * CY, LEVELS)
    picked = (NBD * CHUNKS, LEVELS)
    new_theta, new_humidity, new_zonal, new_meridional, new_vertical, returned = local(
        step_kernel,
        [tile] * 5 + [shape(SLOT_ROWS, CHUNKS, LEVELS)],
        [owners],
        [
            totals,
            powers,
            arrived,
            theta,
            humidity,
            zonal,
            meridional,
            vertical,
            from_north,
            from_south,
            from_east,
            from_west,
        ],
        [pltpu.VMEM((CX + 2, EY, LEVELS), f32)]
        + [pltpu.VMEM(flat, f32)] * 3
        + [pltpu.VMEM(picked, f32)] * 3
        + [pltpu.VMEM(flat, f32)],
    )
    returned = lax.all_to_all(returned, "gx", split_axis=0, concat_axis=0, tiled=True)
    new_squares = local(
        size_kernel,
        [shape(SLOT_ROWS, DPB)],
        [counts],
        [returned.reshape(SLOT_ROWS * CHUNKS, LEVELS), squares],
    )
    return (
        new_theta,
        new_humidity,
        new_zonal,
        new_meridional,
        new_vertical,
        new_squares[None, None],
    )


def solution(mesh):
    field = P(("grp", "gx"), "gy", None)
    slots = P(("grp", "gx"), "gy", None, None)
    return jax.shard_map(
        on_device,
        mesh=mesh,
        in_specs=(field,) * 7 + (slots,) * 3,
        out_specs=(field,) * 5 + (slots,),
        check_vma=False,
    )
```

time: 1060 us -> 75.5 us (0.07)
  blocking collectives: 538 us -> 42.5 us
  local copies, waits for them, and re-layouts: 272 us -> 4.67 us
  other arithmetic: 127 us -> 0.02 us
  waiting for transfers between devices: 50.5 us -> 8.49 us
  starting transfers between devices: 51.1 us -> 11.1 us
    psum x7 -> x0, blocking collectives: 519 us -> none  [the longest x4 297 us: squares(): return lax.psum(jnp.sum(residual * residual), ('grp', 'gx', 'gy'))]
    gather x4 -> x0, local copies, waits for them, and re-layouts: 260 us -> none  [the longest x2 130 us: grow_rows(): warmth = jnp.take_along_axis(thermal_couple[:, 1], local_cell, axis=1)]
    scatter-add x1 -> x0, other arithmetic: 113 us -> none  [grow_rows(): jax.ops.segment_sum(mass_change.reshape(-1), flat_cell.reshape(-1), num_s...]
    ppermute x28 -> x4, starting transfers between devices: 46.8 us -> 11.1 us  [the longest x1 7.85 us: on_device(): from_east = lax.ppermute(to_west, tiles, ring(tiles, -1))]
    all_to_all x1 -> x3, blocking collectives: 18.6 us -> 42.5 us  [the longest x1 16.3 us: on_device(): lax.all_to_all(shared, ('grp', 'gy'), split_axis=0, concat_axis=0, tiled=...]
    ppermute x28 -> x4, waiting for transfers between devices: 30.6 us -> 8.49 us  [the longest x1 5.13 us: on_device(): from_west = lax.ppermute(to_east, tiles, ring(tiles, 1))]
    all_to_all x1 -> x0, waiting for transfers between devices: 19.9 us -> none  [on_device(): lax.all_to_all(columns, 'gx', split_axis=0, concat_axis=0, tiled=True)]
  transfers between devices with their start and end apart: 29 -> 4, of which waited for: 20 -> 3; matrix products, arithmetic and copies ran while one was open for 1% -> 0% of each run, Pallas kernels for 0% -> 0%
where the time goes in v1:
time: 75.5 us; the launch traced here: 75.1 us
  blocking collectives  42.5 us (56%)
  starting transfers between devices  11.1 us (15%)
  waiting for transfers between devices  8.49 us (11%)
  Pallas kernels  7.59 us (10%)
  local copies, waits for them, and re-layouts  4.67 us (6%)
    all_to_all x1, blocking collectives, on_device(): lax.all_to_all(shared, ('grp', 'gy'), split_axis=0, concat_axis=0, tiled=...  16.3 us
    all_to_all x1, blocking collectives, on_device(): lax.all_to_all(parcels, 'gx', split_axis=0, concat_axis=0, tiled=True)  14.1 us
    all_to_all x1, blocking collectives, on_device(): lax.all_to_all(returned, 'gx', split_axis=0, concat_axis=0, tiled=True)  12.2 us
    ppermute x1, starting transfers between devices, on_device(): from_east = lax.ppermute(to_west, tiles, ring(tiles, -1))  7.85 us
    pallas_call x5, Pallas kernels, local(): pl.pallas_call(kernel, out_shape=outs[0] if single else outs, in_specs=[p...  7.59 us
    ppermute x1, waiting for transfers between devices, on_device(): from_west = lax.ppermute(to_east, tiles, ring(tiles, 1))  5.13 us
    unnamed x28, local copies, waits for them, and re-layouts  4.66 us
    ppermute x1, starting transfers between devices, on_device(): from_north = lax.ppermute(to_south, 'gy', ring('gy', -1))  3.25 us
  transfers between devices with their start and end apart: 4, of which 3 were waited for; matrix products, arithmetic and copies ran while one was open for 0% of the time, Pallas kernels for 0%

profile of v1, /device:TPU:1, one launch (start us, length us, event | category | flops | bytes accessed | tf_op | source)
XLA Modules:
  0.0 75.1 jit_solution(6213458221842051103)
XLA Ops:
  0.6 0.0 copy-start
  0.6 0.9 %copy-done = f32[24,16,128]{2,1,0:T(8,128)S(1)} copy-done((f32[24,16,128]{2,1,0:T(8,128)S(1)}, f32[24,16,128]{2,1,0:T(8,128)}, u32[]{:S(2)}) %copy-start) | copy-done | bytes 196632
  1.6 0.0 copy-start.2
  1.6 0.9 %copy-done.2 = f32[24,16,128]{2,1,0:T(8,128)S(1)} copy-done((f32[24,16,128]{2,1,0:T(8,128)S(1)}, f32[24,16,128]{2,1,0:T(8,128)}, u32[]{:S(2)}) %copy-start.2) | copy-done | bytes 196632
  2.5 0.0 copy-start.3
  2.5 0.9 %copy-done.3 = f32[24,16,128]{2,1,0:T(8,128)S(1)} copy-done((f32[24,16,128]{2,1,0:T(8,128)S(1)}, f32[24,16,128]{2,1,0:T(8,128)}, u32[]{:S(2)}) %copy-start.3) | copy-done | bytes 196632
  3.4 0.0 copy-start.5
  3.4 0.9 %copy-done.5 = f32[24,16,128]{2,1,0:T(8,128)S(1)} copy-done((f32[24,16,128]{2,1,0:T(8,128)S(1)}, f32[24,16,128]{2,1,0:T(8,128)}, u32[]{:S(2)}) %copy-start.5) | copy-done | bytes 196632
  4.3 0.0 copy-start.7
  4.3 0.9 %copy-done.7 = f32[24,16,128]{2,1,0:T(8,128)S(1)} copy-done((f32[24,16,128]{2,1,0:T(8,128)S(1)}, f32[24,16,128]{2,1,0:T(8,128)}, u32[]{:S(2)}) %copy-start.7) | copy-done | bytes 196632
  5.3 0.0 copy-start.1
  5.3 0.0 copy-start.9
  5.3 0.0 copy-start.10
  5.3 0.0 copy-start.11
  5.3 0.0 copy-start.12
  5.3 0.2 shard_map.145
  5.5 3.3 %collective-permute-start = (f32[26,8,128]{2,1,0:T(8,128)S(1)}, f32[26,8,128]{2,1,0:T(8,128)S(1)}, u32[]{:S(2)}, u32[]{:S(2)}) collective-permute-start(f32[26,8,128]{2,1,0:T(8,128)S(1)} %get-tuple-element.20), channel_id=1, source_target_pairs={{0,7},{1,0},{2,1},{3,2},{4,3},{5,4},{6,5},{7,6},{8,15},{9,8},{10,9... | collective-permute-start | bytes 319496 | tf_op jit(solution)/shard_map/ppermute | solution.py:541
  8.7 0.0 collective-permute-start.1
  8.7 1.8 %collective-permute-done.from_north = f32[26,8,128]{2,1,0:T(8,128)S(1)} collective-permute-done((f32[26,8,128]{2,1,0:T(8,128)S(1)}, f32[26,8,128]{2,1,0:T(8,128)S(1)}, u32[]{:S(2)}, u32[]{:S(2)}) %collective-permute-start) | collective-permute-done | bytes 106528 | tf_op jit(solution)/shard_map/ppermute | solution.py:541
  10.6 0.0 collective-permute-done.1.from_south
  10.6 0.0 copy-start.4
  10.6 0.0 copy-start.6
  10.6 0.0 copy-start.8
  10.6 0.0 copy-start.13
  10.6 7.8 %collective-permute-start.2 = (f32[7,24,128]{2,1,0:T(8,128)S(1)}, f32[7,24,128]{2,1,0:T(8,128)S(1)}, u32[]{:S(2)}, u32[]{:S(2)}) collective-permute-start(f32[7,24,128]{2,1,0:T(8,128)S(1)} %get-tuple-element.22.to_west), channel_id=1, source_target_pairs={{0,248},{8,0},{16,8},{24,16},{32,24},{40,32},{48,40},{56,48},{64,5... | collective-permute-start | bytes 258056 | tf_op jit(solution)/shard_map/ppermute | solution.py:549
  18.5 0.0 collective-permute-start.3
  18.5 1.5 %collective-permute-done.2.from_east = f32[7,24,128]{2,1,0:T(8,128)S(1)} collective-permute-done((f32[7,24,128]{2,1,0:T(8,128)S(1)}, f32[7,24,128]{2,1,0:T(8,128)S(1)}, u32[]{:S(2)}, u32[]{:S(2)}) %collective-permute-start.2) | collective-permute-done | bytes 86048 | tf_op jit(solution)/shard_map/ppermute | solution.py:549
  20.0 5.1 %collective-permute-done.3.from_west = f32[7,24,128]{2,1,0:T(8,128)S(1)} collective-permute-done((f32[7,24,128]{2,1,0:T(8,128)S(1)}, f32[7,24,128]{2,1,0:T(8,128)S(1)}, u32[]{:S(2)}, u32[]{:S(2)}) %collective-permute-start.3) | collective-permute-done | bytes 86048 | tf_op jit(solution)/shard_map/ppermute | solution.py:550
  25.1 0.0 copy-done.1
  25.1 0.0 copy-done.9
  25.2 0.0 copy-done.10
  25.2 0.0 copy-done.11
  25.2 0.0 copy-done.12
  25.2 1.7 %shard_map.147 = (f32[4,32,24,128]{3,2,1,0:T(8,128)S(1)}, f32[512,128]{1,0:T(8,128)S(1)}) custom-call(s32[16]{0:T(128)S(1)} %bitcast.14, f32[24,16,128]{2,1,0:T(8,128)S(1)} %get-tuple-element.19.partial, f32[26,8,128]{2,1,0:T(8,128)S(1)} %collective-permute-done.from_north, f32[26,8,128]{2,1,0:T(8,128)S(1)} %collective-permute-done.1.from_south, ...), custom_call_target="tpu_custom_call" | custom-call | flops 1000000 | bytes 1000000 | tf_op jit(solution)/shard_map/pallas_call | solution.py:505
  26.9 14.1 %all_to_all.15.arrived = f32[16,32,128]{2,1,0:T(8,128)S(1)} all-to-all(f32[16,32,128]{2,1,0:T(8,128)S(1)} %bitcast.11), channel_id=1, replica_groups=mesh['grp'=2,'gx'=16,'gy'=8] {'gx'}, dimensions={0} | all-to-all | bytes 524288 | tf_op jit(solution)/shard_map/all_to_all | solution.py:570
  41.0 16.3 %all_to_all.16.totals = f32[16,8,128]{2,1,0:T(8,128)S(1)} all-to-all(f32[16,8,128]{2,1,0:T(8,128)S(1)} %broadcast_in_dim.4), channel_id=1, replica_groups=mesh['grp'=2,'gx'=16,'gy'=8] {'grp','gy'}, dimensions={0} | all-to-all | bytes 131072 | tf_op jit(solution)/shard_map/all_to_all | solution.py:572
  57.3 0.0 copy-done.4
  57.3 0.0 copy-done.6
  57.3 0.0 copy-done.8
  57.3 0.0 copy-done.13
  57.3 4.5 %shard_map.148 = (f32[24,16,128]{2,1,0:T(8,128)}, f32[24,16,128]{2,1,0:T(8,128)}, f32[24,16,128]{2,1,0:T(8,128)}, f32[24,16,128]{2,1,0:T(8,128)}, f32[24,16,128]{2,1,0:T(8,128)}, /*index=5*/f32[16,8,128]{2,1,0:T(8,128)S(1)}) custom-call(s32[8]{0:T(128)S(1)} %bitcast.16, f32[16,8,128]{2,1,0:T(8,128)S(1)} %all_to_all.16.totals, ...), custom_call_target="tpu_custom_call" | custom-call | flops 1000000 | bytes 1000000 | tf_op jit(solution)/shard_map/pallas_call | solution.py:505
  61.8 12.2 %all_to_all.17 = f32[16,8,128]{2,1,0:T(8,128)S(1)} all-to-all(f32[16,8,128]{2,1,0:T(8,128)S(1)} %get-tuple-element.31), channel_id=1, replica_groups=mesh['grp'=2,'gx'=16,'gy'=8] {'gx'}, dimensions={0} | all-to-all | bytes 131072 | tf_op jit(solution)/shard_map/all_to_all | solution.py:598
  74.0 1.2 %shard_map.149 = f32[16,1024]{1,0:T(8,128)} custom-call(s32[16]{0:T(128)S(1)} %bitcast.15, f32[128,128]{1,0:T(8,128)S(1)} %bitcast.10, f32[16,1024]{1,0:T(8,128)S(1)} %bitcast.9), custom_call_target="tpu_custom_call" | custom-call | flops 1000000 | bytes 1000000 | tf_op jit(solution)/shard_map/pallas_call | solution.py:505
  (3 shorter events, 0.1 us)
Async XLA Ops:
  0.6 0.9 %copy-start = (f32[24,16,128]{2,1,0:T(8,128)S(1)}, f32[24,16,128]{2,1,0:T(8,128)}, u32[]{:S(2)}) copy-start(f32[24,16,128]{2,1,0:T(8,128)} %meridional.7) | copy-start | bytes 589828
  1.6 0.9 %copy-start.2 = (f32[24,16,128]{2,1,0:T(8,128)S(1)}, f32[24,16,128]{2,1,0:T(8,128)}, u32[]{:S(2)}) copy-start(f32[24,16,128]{2,1,0:T(8,128)} %theta.5) | copy-start | bytes 589828
  2.5 0.9 %copy-start.3 = (f32[24,16,128]{2,1,0:T(8,128)S(1)}, f32[24,16,128]{2,1,0:T(8,128)}, u32[]{:S(2)}) copy-start(f32[24,16,128]{2,1,0:T(8,128)} %humidity.5) | copy-start | bytes 589828
  3.4 0.9 %copy-start.5 = (f32[24,16,128]{2,1,0:T(8,128)S(1)}, f32[24,16,128]{2,1,0:T(8,128)}, u32[]{:S(2)}) copy-start(f32[24,16,128]{2,1,0:T(8,128)} %zonal.5) | copy-start | bytes 589828
  4.3 0.9 %copy-start.7 = (f32[24,16,128]{2,1,0:T(8,128)S(1)}, f32[24,16,128]{2,1,0:T(8,128)}, u32[]{:S(2)}) copy-start(f32[24,16,128]{2,1,0:T(8,128)} %vertical.3) | copy-start | bytes 589828
  5.3 19.9 %copy-start.1 = (f32[24,16,128]{2,1,0:T(8,128)S(1)}, f32[24,16,128]{2,1,0:T(8,128)}, u32[]{:S(2)}) copy-start(f32[24,16,128]{2,1,0:T(8,128)} %meridional.7) | copy-start | bytes 589828
  5.3 19.9 %copy-start.9 = (f32[1,1,16,1024]{3,2,1,0:T(8,128)S(1)}, f32[1,1,16,1024]{3,2,1,0:T(8,128)}, u32[]{:S(2)}) copy-start(f32[1,1,16,1024]{3,2,1,0:T(8,128)} %param.17) | copy-start | bytes 196612
  5.3 19.9 %copy-start.10 = (f32[1,1,16,1024]{3,2,1,0:T(8,128)S(1)}, f32[1,1,16,1024]{3,2,1,0:T(8,128)}, u32[]{:S(2)}) copy-start(f32[1,1,16,1024]{3,2,1,0:T(8,128)} %param.18) | copy-start | bytes 196612
  5.3 19.9 %copy-start.11 = (s32[1,1,16,1024]{3,2,1,0:T(8,128)S(1)}, s32[1,1,16,1024]{3,2,1,0:T(8,128)}, u32[]{:S(2)}) copy-start(s32[1,1,16,1024]{3,2,1,0:T(8,128)} %param.19) | copy-start | bytes 196612
  5.3 19.9 %copy-start.12 = (s32[1,1,16]{2,1,0:T(1,128)S(1)}, s32[1,1,16]{2,1,0:T(1,128)}, u32[]{:S(2)}) copy-start(s32[1,1,16]{2,1,0:T(1,128)} %param.16) | copy-start | bytes 196
  5.5 5.1 %collective-permute-start = (f32[26,8,128]{2,1,0:T(8,128)S(1)}, f32[26,8,128]{2,1,0:T(8,128)S(1)}, u32[]{:S(2)}, u32[]{:S(2)}) collective-permute-start(f32[26,8,128]{2,1,0:T(8,128)S(1)} %get-tuple-element.20), channel_id=1, source_target_pairs={{0,7},{1,0},{2,1},{3,2},{4,3},{5,4},{6,5},{7,6},{8,15},{9,8},{10,9... | collective-permute-start | bytes 319496 | tf_op jit(solution)/shard_map/ppermute | solution.py:541
  8.7 1.8 %collective-permute-start.1 = (f32[26,8,128]{2,1,0:T(8,128)S(1)}, f32[26,8,128]{2,1,0:T(8,128)S(1)}, u32[]{:S(2)}, u32[]{:S(2)}) collective-permute-start(f32[26,8,128]{2,1,0:T(8,128)S(1)} %get-tuple-element.21), channel_id=1, source_target_pairs={{0,1},{1,2},{2,3},{3,4},{4,5},{5,6},{6,7},{7,0},{8,9},{9,10},{10,1... | collective-permute-start | bytes 319496 | tf_op jit(solution)/shard_map/ppermute | solution.py:542
  10.6 46.7 %copy-start.4 = (f32[24,16,128]{2,1,0:T(8,128)S(1)}, f32[24,16,128]{2,1,0:T(8,128)}, u32[]{:S(2)}) copy-start(f32[24,16,128]{2,1,0:T(8,128)} %humidity.5) | copy-start | bytes 589828
  10.6 46.7 %copy-start.6 = (f32[24,16,128]{2,1,0:T(8,128)S(1)}, f32[24,16,128]{2,1,0:T(8,128)}, u32[]{:S(2)}) copy-start(f32[24,16,128]{2,1,0:T(8,128)} %zonal.5) | copy-start | bytes 589828
  10.6 46.7 %copy-start.8 = (f32[24,16,128]{2,1,0:T(8,128)S(1)}, f32[24,16,128]{2,1,0:T(8,128)}, u32[]{:S(2)}) copy-start(f32[24,16,128]{2,1,0:T(8,128)} %vertical.3) | copy-start | bytes 589828
  10.6 46.7 %copy-start.13 = (s32[1,1,8]{2,1,0:T(1,128)S(1)}, s32[1,1,8]{2,1,0:T(1,128)}, u32[]{:S(2)}) copy-start(s32[1,1,8]{2,1,0:T(1,128)} %param.15) | copy-start | bytes 100
  10.6 9.4 %collective-permute-start.2 = (f32[7,24,128]{2,1,0:T(8,128)S(1)}, f32[7,24,128]{2,1,0:T(8,128)S(1)}, u32[]{:S(2)}, u32[]{:S(2)}) collective-permute-start(f32[7,24,128]{2,1,0:T(8,128)S(1)} %get-tuple-element.22.to_west), channel_id=1, source_target_pairs={{0,248},{8,0},{16,8},{24,16},{32,24},{40,32},{48,40},{56,48},{64,5... | collective-permute-start | bytes 258056 | tf_op jit(solution)/shard_map/ppermute | solution.py:549
  18.5 6.7 %collective-permute-start.3 = (f32[7,24,128]{2,1,0:T(8,128)S(1)}, f32[7,24,128]{2,1,0:T(8,128)S(1)}, u32[]{:S(2)}, u32[]{:S(2)}) collective-permute-start(f32[7,24,128]{2,1,0:T(8,128)S(1)} %get-tuple-element.23.to_east), channel_id=1, source_target_pairs={{0,8},{8,16},{16,24},{24,32},{32,40},{40,48},{48,56},{56,64},{64,7... | collective-permute-start | bytes 258056 | tf_op jit(solution)/shard_map/ppermute | solution.py:550

commit v2 on v1

--- a/solution.py
+++ b/solution.py
@@ -33,9 +33,12 @@
 SLOT_ROWS = 16
 DPB = 1024
 CHUNKS = DPB // LEVELS
+DROPS = 24
 PARCEL = 32
 SCALE = 1.0 / 6.0
+PACK_LIMIT = 24 * 1024 * 1024
 VMEM_LIMIT = 24 * 1024 * 1024
+FIRST_LIMIT = 54600 * 1024
 
 f32 = jnp.float32
 bf16 = jnp.bfloat16
@@ -62,7 +65,39 @@
     return vertical[i] + TIME_INCREMENT * (THERMAL_LIFT * theta[i] + HUMID_LIFT * humidity[i])
 
 
-def right_side_kernel(theta, humidity, zonal, meridional, vertical, partial, to_south, to_north):
+def right_side_kernel(
+    theta_far,
+    humidity_far,
+    zonal_far,
+    meridional_far,
+    vertical_far,
+    partial,
+    to_south,
+    to_north,
+    edges,
+    theta,
+    humidity,
+    zonal,
+    meridional,
+    vertical,
+    arrivals,
+):
+    copies = [
+        pltpu.make_async_copy(far, near, arrivals.at[n])
+        for n, (far, near) in enumerate(
+            (
+                (theta_far, theta),
+                (humidity_far, humidity),
+                (zonal_far, zonal),
+                (meridional_far, meridional),
+                (vertical_far, vertical),
+            )
+        )
+    ]
+    for copy in copies:
+        copy.start()
+    for copy in copies:
+        copy.wait()
     level, centre, _, _ = vertical_profiles()
     sub = iota((CY, LEVELS), 0)
     sub8 = iota((8, LEVELS), 0)
@@ -95,20 +130,25 @@
             right[8:16],
             jnp.where(sub8 == 0, wind[15:16], jnp.where(sub8 == 1, warm[15:16], damp[15:16])),
         )
-    for place, i in ((CX, 0), (CX + 1, CX - 1)):
-        to_south[place] = zonal[i, 0:8]
-        to_north[place] = zonal[i, 8:16]
+    for n, i in enumerate((0, CX - 1)):
+        to_south[CX + n] = zonal[i, 0:8]
+        to_north[CX + n] = zonal[i, 8:16]
+        edges[7 * n + 4] = zonal[i]
+        edges[7 * n + 5] = theta[i]
+        edges[7 * n + 6] = humidity[i]
+    for t in range(4):
+        edges[t] = meridional[t]
+        edges[7 + t] = meridional[CX - 4 + t]
 
 
 def joined(north, south):
     return jnp.where(iota((8, LEVELS), 0) < 4, north, south)
 
 
-def completed_row(i, partial, meridional, from_north, from_south, third):
+def completed_row(i, partial, wind, from_north, from_south, third):
     sub8 = iota((8, LEVELS), 0)
     north = from_north[i]
     south = from_south[i]
-    wind = meridional[i]
     low = partial[i, 0:8] + jnp.where(sub8 == 0, third * south[0:1], 0.0)
     high = partial[i, 8:16] - jnp.where(sub8 == 7, third * north[4:5], 0.0)
     halo = (
@@ -119,29 +159,52 @@
     return low, high, halo
 
 
-def side_kernel(
-    partial, from_north, from_south, theta, humidity, zonal, meridional, to_west, to_east
-):
+def side_kernel(partial, from_north, from_south, edges, to_west, to_east):
     _, centre, _, _ = vertical_profiles()
     third = centre * (0.5 / TIME_INCREMENT)
-    for target, first, edge, place in ((to_west, 0, 0, CX), (to_east, CX - 4, CX - 1, CX + 1)):
+    for n, (target, first) in enumerate(((to_west, 0), (to_east, CX - 4))):
         for t in range(4):
             low, high, halo = completed_row(
-                first + t, partial, meridional, from_north, from_south, third
+                first + t, partial, edges[7 * n + t], from_north, from_south, third
             )
             target[t, 0:8] = low
             target[t, 8:16] = high
             target[t, 16:24] = halo
-        target[4, 0:16] = zonal[edge]
-        target[4, 16:24] = joined(from_north[place], from_south[place])
-        target[5, 0:16] = theta[edge]
-        target[5, 16:24] = jnp.zeros((8, LEVELS), f32)
-        target[6, 0:16] = humidity[edge]
-        target[6, 16:24] = jnp.zeros((8, LEVELS), f32)
+        target[4, 0:16] = edges[7 * n + 4]
+        target[4, 16:24] = joined(from_north[CX + n], from_south[CX + n])
+        for t in (5, 6):
+            target[t, 0:16] = edges[7 * n + t]
+            target[t, 16:24] = jnp.zeros((8, LEVELS), f32)
+
+
+def pack_kernel(
+    counts, squares_far, numbers_far, cells_far, drops, squares, numbers, cells, arrivals
+):
+    copies = [
+        pltpu.make_async_copy(far, near, arrivals.at[n])
+        for n, (far, near) in enumerate(
+            ((squares_far, squares), (numbers_far, numbers), (cells_far, cells))
+        )
+    ]
+    for copy in copies:
+        copy.start()
+    for copy in copies:
+        copy.wait()
+    row = iota((SLOT_ROWS, LEVELS), 0)
+    lane = iota((SLOT_ROWS, LEVELS), 1)
+    live = jnp.zeros((SLOT_ROWS, LEVELS), jnp.int32)
+    for r in range(SLOT_ROWS):
+        live = jnp.where(row == r, counts[r], live)
+    for s in range(CHUNKS):
+        part = slice(LEVELS * s, LEVELS * (s + 1))
+        drops[pl.ds(s, SLOT_ROWS, stride=DROPS), :] = squares[:, part]
+        drops[pl.ds(8 + s, SLOT_ROWS, stride=DROPS), :] = jnp.where(
+            lane + LEVELS * s < live, numbers[:, part], 0.0
+        )
+        drops[pl.ds(16 + s, SLOT_ROWS, stride=DROPS), :] = cells[:, part].astype(f32)
 
 
 def power_kernel(
-    counts,
     partial,
     from_north,
     from_south,
@@ -150,16 +213,14 @@
     to_east,
     from_east,
     from_west,
-    squares,
-    numbers,
-    cells,
+    drops,
     powers,
     parcels,
 ):
     _, centre, face, face_below = vertical_profiles()
     third = centre * (0.5 / TIME_INCREMENT)
     for i in range(4, CX - 4):
-        low, high, halo = completed_row(i, partial, meridional, from_north, from_south, third)
+        low, high, halo = completed_row(i, partial, meridional[i], from_north, from_south, third)
         powers[0, i, 0:8] = low
         powers[0, i, 8:16] = high
         powers[0, i, 16:24] = halo
@@ -214,19 +275,8 @@
     for k in range(2 * ITERS):
         packed = jnp.where(sub8 == k, jnp.sum(sums[k], axis=0, keepdims=True), packed)
     for r in range(SLOT_ROWS):
-        parcels[PARCEL * r + 24 : PARCEL * r + 32] = packed
-    row = iota((SLOT_ROWS, LEVELS), 0)
-    lane = iota((SLOT_ROWS, LEVELS), 1)
-    live = jnp.zeros((SLOT_ROWS, LEVELS), jnp.int32)
-    for r in range(SLOT_ROWS):
-        live = jnp.where(row == r, counts[r], live)
-    for s in range(CHUNKS):
-        part = slice(LEVELS * s, LEVELS * (s + 1))
-        parcels[pl.ds(s, SLOT_ROWS, stride=PARCEL), :] = squares[:, part]
-        parcels[pl.ds(8 + s, SLOT_ROWS, stride=PARCEL), :] = jnp.where(
-            lane + LEVELS * s < live, numbers[:, part], 0.0
-        )
-        parcels[pl.ds(16 + s, SLOT_ROWS, stride=PARCEL), :] = cells[:, part].astype(f32)
+        parcels[r, 0:DROPS] = drops[DROPS * r : DROPS * (r + 1)]
+        parcels[r, DROPS:PARCEL] = packed
 
 
 def two_sum(a, b):
@@ -318,7 +368,36 @@
     return high, values - high
 
 
-def step_kernel(
+HALF = TIME_INCREMENT * 0.5
+
+
+def new_winds(i, potential, theta, humidity, zonal, meridional, vertical):
+    level = iota((1, LEVELS), 1)
+    here = potential[i + 1]
+    mid = here[0:16]
+    east = zonal[i] - HALF * (potential[i + 2, 0:16] - potential[i, 0:16])
+    north = meridional[i] - HALF * (turn(here, -1, 0)[0:16] - turn(here, 1, 0)[0:16])
+    up = lifted_row(i, theta, humidity, vertical) - HALF * (
+        jnp.where(level < LEVELS - 1, turn(mid, -1, 1), 0.0)
+        - jnp.where(level > 0, turn(mid, 1, 1), 0.0)
+    )
+    return east, north, up
+
+
+def chunk(values, t):
+    return jnp.concatenate([values[2 * t : 2 * t + 1], values[2 * t + 1 : 2 * t + 2]], axis=1)
+
+
+def where_at(arrived, owner):
+    cell = arrived[owner, 16:24].astype(jnp.int32)
+    column = lax.shift_right_logical(cell, 7)
+    return (
+        jnp.bitwise_and(cell, LEVELS - 1) - KLO,
+        jnp.bitwise_and(column, 1) * CX + lax.shift_right_logical(column, 1),
+    )
+
+
+def growth_kernel(
     owners,
     totals,
     powers,
@@ -332,20 +411,14 @@
     from_south,
     from_east,
     from_west,
-    new_theta,
-    new_humidity,
-    new_zonal,
-    new_meridional,
-    new_vertical,
     returned,
     potential,
-    excess,
     warmth,
     vapour,
+    mass,
+    excess,
     picked_excess,
     picked_warmth,
-    mass,
-    condensed,
 ):
     level, _, _, _ = vertical_profiles()
     sub = iota((CY, LEVELS), 0)
@@ -356,19 +429,8 @@
         for j in range(1, ITERS):
             total = total + weights[j] * powers[j, i]
         potential[t] = total
-    half = TIME_INCREMENT * 0.5
     for i in range(CX):
-        here = potential[i + 1]
-        east = zonal[i] - half * (potential[i + 2, 0:16] - potential[i, 0:16])
-        north = meridional[i] - half * (turn(here, -1, 0)[0:16] - turn(here, 1, 0)[0:16])
-        mid = here[0:16]
-        up = lifted_row(i, theta, humidity, vertical) - half * (
-            jnp.where(level < LEVELS - 1, turn(mid, -1, 1), 0.0)
-            - jnp.where(level > 0, turn(mid, 1, 1), 0.0)
-        )
-        new_zonal[i] = east
-        new_meridional[i] = north
-        new_vertical[i] = up
+        east, north, up = new_winds(i, potential, theta, humidity, zonal, meridional, vertical)
         moved = []
         for f, (field, side, in_north, in_south) in enumerate(
             ((theta, 5, 5, 1), (humidity, 6, 6, 2))
@@ -412,20 +474,9 @@
         both = jnp.where(lane < BAND, turn(high, -KLO, 1), turn(low, BAND - KLO, 1))
         return both[:, : 2 * BAND].astype(bf16)
 
-    def chunk(values, t):
-        return jnp.concatenate([values[2 * t : 2 * t + 1], values[2 * t + 1 : 2 * t + 2]], axis=1)
-
-    def where_at(b):
-        cell = arrived[owners[b], 16:24].astype(jnp.int32)
-        column = lax.shift_right_logical(cell, 7)
-        return (
-            jnp.bitwise_and(cell, LEVELS - 1) - KLO,
-            jnp.bitwise_and(column, 1) * CX + lax.shift_right_logical(column, 1),
-        )
-
     for b in range(NBD):
         table = jnp.concatenate([band(excess, b), band(warmth, b)], axis=0)
-        heights, places = where_at(b)
+        heights, places = where_at(arrived, owners[b])
         for t in range(CHUNKS // 2):
             hot = jnp.where(height == chunk(heights, t), 1.0, 0.0).astype(bf16)
             found = jnp.dot(
@@ -455,8 +506,35 @@
             number > 0.0, number * (now * jnp.sqrt(now) - old * jnp.sqrt(old)), 0.0
         )
         returned[owner] = now
+
+
+def condense_kernel(
+    owners,
+    potential,
+    warmth,
+    vapour,
+    mass,
+    arrived,
+    theta,
+    humidity,
+    zonal,
+    meridional,
+    vertical,
+    new_theta,
+    new_humidity,
+    new_zonal,
+    new_meridional,
+    new_vertical,
+    condensed,
+):
+    for i in range(CX):
+        new_zonal[i], new_meridional[i], new_vertical[i] = new_winds(
+            i, potential, theta, humidity, zonal, meridional, vertical
+        )
+    height = iota((BAND, 2 * LEVELS), 0)
+    place = iota((2 * CX, 2 * LEVELS), 0)
     for b in range(NBD):
-        heights, places = where_at(b)
+        heights, places = where_at(arrived, owners[b])
         gained = mass[CHUNKS * b : CHUNKS * (b + 1)]
         total = jnp.zeros((4 * CX, BAND), f32)
         for t in range(CHUNKS // 2):
@@ -499,17 +577,19 @@
         )
 
 
-def local(kernel, outs, scalars, operands, scratch=(), cost=(1_000_000, 1_000_000)):
+def local(kernel, outs, scalars, operands, scratch=(), far=0, limit=VMEM_LIMIT, cost=1_000_000):
     whole = pl.BlockSpec(memory_space=pltpu.VMEM)
     single = len(outs) == 1
     return pl.pallas_call(
         kernel,
         out_shape=outs[0] if single else outs,
-        in_specs=[pl.BlockSpec(memory_space=pltpu.SMEM)] * len(scalars) + [whole] * len(operands),
+        in_specs=[pl.BlockSpec(memory_space=pltpu.SMEM)] * len(scalars)
+        + [pl.BlockSpec(memory_space=pltpu.HBM)] * far
+        + [whole] * (len(operands) - far),
         out_specs=whole if single else [whole] * len(outs),
         scratch_shapes=list(scratch),
-        compiler_params=pltpu.CompilerParams(vmem_limit_bytes=VMEM_LIMIT),
-        cost_estimate=pl.CostEstimate(flops=cost[0], bytes_accessed=cost[1], transcendentals=0),
+        compiler_params=pltpu.CompilerParams(vmem_limit_bytes=limit),
+        cost_estimate=pl.CostEstimate(flops=cost, bytes_accessed=cost, transcendentals=0),
     )(*scalars, *operands)
 
 
@@ -532,11 +612,14 @@
     cells = cells.reshape(SLOT_ROWS, DPB)
     tiles = ("grp", "gx")
     tile = shape(CX, CY, LEVELS)
-    partial, to_south, to_north = local(
+    partial, to_south, to_north, edges = local(
         right_side_kernel,
-        [tile, shape(CX + 2, 8, LEVELS), shape(CX + 2, 8, LEVELS)],
+        [tile, shape(CX + 2, 8, LEVELS), shape(CX + 2, 8, LEVELS), shape(14, CY, LEVELS)],
         [],
         [theta, humidity, zonal, meridional, vertical],
+        [pltpu.VMEM((CX, CY, LEVELS), f32)] * 5 + [pltpu.SemaphoreType.DMA((5,))],
+        far=5,
+        limit=FIRST_LIMIT,
     )
     from_north = lax.ppermute(to_south, "gy", ring("gy", -1))
     from_south = lax.ppermute(to_north, "gy", ring("gy", 1))
@@ -544,14 +627,24 @@
         side_kernel,
         [shape(7, EY, LEVELS), shape(7, EY, LEVELS)],
         [],
-        [partial, from_north, from_south, theta, humidity, zonal, meridional],
+        [partial, from_north, from_south, edges],
     )
     from_east = lax.ppermute(to_west, tiles, ring(tiles, -1))
     from_west = lax.ppermute(to_east, tiles, ring(tiles, 1))
+    drops = local(
+        pack_kernel,
+        [shape(SLOT_ROWS * DROPS, LEVELS)],
+        [counts],
+        [squares, numbers, cells],
+        [pltpu.VMEM((SLOT_ROWS, DPB), f32)] * 2
+        + [pltpu.VMEM((SLOT_ROWS, DPB), jnp.int32), pltpu.SemaphoreType.DMA((3,))],
+        far=3,
+        limit=PACK_LIMIT,
+    )
     powers, parcels = local(
         power_kernel,
-        [shape(ITERS, EX, EY, LEVELS), shape(SLOT_ROWS * PARCEL, LEVELS)],
-        [counts],
+        [shape(ITERS, EX, EY, LEVELS), shape(SLOT_ROWS, PARCEL, LEVELS)],
+        [],
         [
             partial,
             from_north,
@@ -561,20 +654,23 @@
             to_east,
             from_east,
             from_west,
-            squares,
-            numbers,
-            cells,
+            drops,
         ],
     )
-    parcels = parcels.reshape(SLOT_ROWS, PARCEL, LEVELS)
     arrived = lax.all_to_all(parcels, "gx", split_axis=0, concat_axis=0, tiled=True)
     shared = jnp.broadcast_to(jnp.sum(arrived[:, 24:], axis=0)[None], (16, 8, LEVELS))
     totals = lax.all_to_all(shared, ("grp", "gy"), split_axis=0, concat_axis=0, tiled=True)
     flat = (CX * CY, LEVELS)
     picked = (NBD * CHUNKS, LEVELS)
-    new_theta, new_humidity, new_zonal, new_meridional, new_vertical, returned = local(
-        step_kernel,
-        [tile] * 5 + [shape(SLOT_ROWS, CHUNKS, LEVELS)],
+    returned, potential, warmth, vapour, mass = local(
+        growth_kernel,
+        [
+            shape(SLOT_ROWS, CHUNKS, LEVELS),
+            shape(CX + 2, EY, LEVELS),
+            shape(*flat),
+            shape(*flat),
+            shape(*picked),
+        ],
         [owners],
         [
             totals,
@@ -590,12 +686,27 @@
             from_east,
             from_west,
         ],
-        [pltpu.VMEM((CX + 2, EY, LEVELS), f32)]
-        + [pltpu.VMEM(flat, f32)] * 3
-        + [pltpu.VMEM(picked, f32)] * 3
-        + [pltpu.VMEM(flat, f32)],
+        [pltpu.VMEM(flat, f32)] + [pltpu.VMEM(picked, f32)] * 2,
     )
     returned = lax.all_to_all(returned, "gx", split_axis=0, concat_axis=0, tiled=True)
+    new_theta, new_humidity, new_zonal, new_meridional, new_vertical = local(
+        condense_kernel,
+        [tile] * 5,
+        [owners],
+        [
+            potential,
+            warmth,
+            vapour,
+            mass,
+            arrived,
+            theta,
+            humidity,
+            zonal,
+            meridional,
+            vertical,
+        ],
+        [pltpu.VMEM(flat, f32)],
+    )
     new_squares = local(
         size_kernel,
         [shape(SLOT_ROWS, DPB)],

time: 75.5 us -> 71.9 us (0.952)
  blocking collectives: 42.5 us -> 30.4 us
  starting transfers between devices: 11.1 us -> 14.7 us
  waiting for transfers between devices: 8.49 us -> 11.7 us
  Pallas kernels: 7.59 us -> 10.6 us
  local copies, waits for them, and re-layouts: 4.67 us -> 3.22 us
    all_to_all x1 -> x0, blocking collectives: 12.2 us -> none  [on_device(): lax.all_to_all(returned, 'gx', split_axis=0, concat_axis=0, tiled=True)]
    all_to_all x0 -> x1, waiting for transfers between devices: none -> 7.27 us  [on_device(): lax.all_to_all(returned, 'gx', split_axis=0, concat_axis=0, tiled=True)]
    all_to_all x0 -> x1, starting transfers between devices: none -> 3.63 us  [on_device(): lax.all_to_all(returned, 'gx', split_axis=0, concat_axis=0, tiled=True)]
    pallas_call x5 -> x7, Pallas kernels: 7.59 us -> 10.6 us  [local(): pl.pallas_call(kernel, out_shape=outs[0] if single else outs, in_specs=[p...]
    ppermute x1, waiting for transfers between devices: 5.13 us -> 2.6 us  [on_device(): from_west = lax.ppermute(to_east, tiles, ring(tiles, 1))]
    ppermute x1, waiting for transfers between devices: 1.52 us -> 0.01 us  [on_device(): from_east = lax.ppermute(to_west, tiles, ring(tiles, -1))]
    unnamed x28 -> x24, local copies, waits for them, and re-layouts: 4.66 us -> 3.21 us
    all_to_all x1, blocking collectives: 16.3 us -> 15.2 us  [on_device(): lax.all_to_all(shared, ('grp', 'gy'), split_axis=0, concat_axis=0, tiled=...]
  transfers between devices with their start and end apart: 4 -> 5, of which waited for: 3 -> 3; matrix products, arithmetic and copies ran while one was open for 0% -> 0% of each run, Pallas kernels for 0% -> 4%
where the time goes in v2:
time: 71.9 us; the launch traced here: 71.5 us
  blocking collectives  30.4 us (42%)
  starting transfers between devices  14.7 us (20%)
  waiting for transfers between devices  11.7 us (16%)
  Pallas kernels  10.6 us (15%)
  local copies, waits for them, and re-layouts  3.22 us (4%)
  between operations  0.76 us (1%)
    all_to_all x1, blocking collectives, on_device(): lax.all_to_all(shared, ('grp', 'gy'), split_axis=0, concat_axis=0, tiled=...  15.2 us
    all_to_all x1, blocking collectives, on_device(): lax.all_to_all(parcels, 'gx', split_axis=0, concat_axis=0, tiled=True)  15.2 us
    pallas_call x7, Pallas kernels, local(): pl.pallas_call(kernel, out_shape=outs[0] if single else outs, in_specs=[p...  10.6 us
    ppermute x1, starting transfers between devices, on_device(): from_east = lax.ppermute(to_west, tiles, ring(tiles, -1))  7.85 us
    all_to_all x1, waiting for transfers between devices, on_device(): lax.all_to_all(returned, 'gx', split_axis=0, concat_axis=0, tiled=True)  7.27 us
    all_to_all x1, starting transfers between devices, on_device(): lax.all_to_all(returned, 'gx', split_axis=0, concat_axis=0, tiled=True)  3.63 us
    ppermute x1, starting transfers between devices, on_device(): from_north = lax.ppermute(to_south, 'gy', ring('gy', -1))  3.25 us
    unnamed x24, local copies, waits for them, and re-layouts  3.21 us
  transfers between devices with their start and end apart: 5, of which 3 were waited for; matrix products, arithmetic and copies ran while one was open for 0% of the time, Pallas kernels for 4%

profile of v2, /device:TPU:1, one launch (start us, length us, event | category | flops | bytes accessed | tf_op | source)
XLA Modules:
  0.0 71.5 jit_solution(14052778984190178828)
XLA Ops:
  0.6 0.0 copy-start
  0.6 0.0 copy-start.11
  0.7 1.5 %shard_map.145 = (f32[24,16,128]{2,1,0:T(8,128)S(1)}, f32[26,8,128]{2,1,0:T(8,128)S(1)}, f32[26,8,128]{2,1,0:T(8,128)S(1)}, f32[14,16,128]{2,1,0:T(8,128)S(1)}) custom-call(f32[24,16,128]{2,1,0:T(8,128)} %theta.3, f32[24,16,128]{2,1,0:T(8,128)} %humidity.3, f32[24,16,128]{2,1,0:T(8,128)} %zonal.3, f32[24,16,128]{2,1,0:T(8,128)} %meridional.5, ...), custom_call_target="tpu_custom_call" | custom-call | flops 1000000 | bytes 1000000 | tf_op jit(solution)/shard_map/pallas_call | solution.py:583
  2.2 0.0 copy-start.1
  2.2 0.0 copy-start.2
  2.2 0.0 copy-start.3
  2.2 0.0 copy-start.4
  2.2 3.3 %collective-permute-start = (f32[26,8,128]{2,1,0:T(8,128)S(1)}, f32[26,8,128]{2,1,0:T(8,128)S(1)}, u32[]{:S(2)}, u32[]{:S(2)}) collective-permute-start(f32[26,8,128]{2,1,0:T(8,128)S(1)} %get-tuple-element.25), channel_id=1, source_target_pairs={{0,7},{1,0},{2,1},{3,2},{4,3},{5,4},{6,5},{7,6},{8,15},{9,8},{10,9... | collective-permute-start | bytes 319496 | tf_op jit(solution)/shard_map/ppermute | solution.py:624
  5.5 0.0 collective-permute-start.1
  5.5 1.8 %collective-permute-done.from_north = f32[26,8,128]{2,1,0:T(8,128)S(1)} collective-permute-done((f32[26,8,128]{2,1,0:T(8,128)S(1)}, f32[26,8,128]{2,1,0:T(8,128)S(1)}, u32[]{:S(2)}, u32[]{:S(2)}) %collective-permute-start) | collective-permute-done | bytes 106528 | tf_op jit(solution)/shard_map/ppermute | solution.py:624
  7.3 0.0 collective-permute-done.1.from_south
  7.4 7.8 %collective-permute-start.2 = (f32[7,24,128]{2,1,0:T(8,128)S(1)}, f32[7,24,128]{2,1,0:T(8,128)S(1)}, u32[]{:S(2)}, u32[]{:S(2)}) collective-permute-start(f32[7,24,128]{2,1,0:T(8,128)S(1)} %get-tuple-element.28.to_west), channel_id=1, source_target_pairs={{0,248},{8,0},{16,8},{24,16},{32,24},{40,32},{48,40},{56,48},{64,5... | collective-permute-start | bytes 258056 | tf_op jit(solution)/shard_map/ppermute | solution.py:632
  15.2 0.0 collective-permute-start.3
  15.2 0.0 copy-start.5
  15.2 0.8 %copy-done.5 = f32[1,1,16,1024]{3,2,1,0:T(8,128)S(1)} copy-done((f32[1,1,16,1024]{3,2,1,0:T(8,128)S(1)}, f32[1,1,16,1024]{3,2,1,0:T(8,128)}, u32[]{:S(2)}) %copy-start.5) | copy-done | bytes 65560
  16.1 0.0 copy-start.7
  16.1 0.8 %copy-done.7 = f32[1,1,16,1024]{3,2,1,0:T(8,128)S(1)} copy-done((f32[1,1,16,1024]{3,2,1,0:T(8,128)S(1)}, f32[1,1,16,1024]{3,2,1,0:T(8,128)}, u32[]{:S(2)}) %copy-start.7) | copy-done | bytes 65560
  16.9 0.0 copy-start.8
  16.9 0.8 %copy-done.8 = s32[1,1,16,1024]{3,2,1,0:T(8,128)S(1)} copy-done((s32[1,1,16,1024]{3,2,1,0:T(8,128)S(1)}, s32[1,1,16,1024]{3,2,1,0:T(8,128)}, u32[]{:S(2)}) %copy-start.8) | copy-done | bytes 65560
  17.8 0.0 copy-start.9
  17.8 0.7 copy-done.9
  18.4 0.9 %shard_map.147.drops = f32[384,128]{1,0:T(8,128)S(1)} custom-call(s32[16]{0:T(128)S(1)} %bitcast.12, f32[16,1024]{1,0:T(8,128)S(1)} %bitcast.8, f32[16,1024]{1,0:T(8,128)S(1)} %bitcast.10, s32[16,1024]{1,0:T(8,128)S(1)} %bitcast.11), custom_call_target="tpu_custom_call" | custom-call | flops 1000000 | bytes 1000000 | tf_op jit(solution)/shard_map/pallas_call | solution.py:583
  19.3 0.0 collective-permute-done.2.from_east
  19.3 2.6 %collective-permute-done.3.from_west = f32[7,24,128]{2,1,0:T(8,128)S(1)} collective-permute-done((f32[7,24,128]{2,1,0:T(8,128)S(1)}, f32[7,24,128]{2,1,0:T(8,128)S(1)}, u32[]{:S(2)}, u32[]{:S(2)}) %collective-permute-start.3) | collective-permute-done | bytes 86048 | tf_op jit(solution)/shard_map/ppermute | solution.py:633
  21.9 0.0 copy-done
  21.9 1.0 %shard_map.148 = (f32[4,32,24,128]{3,2,1,0:T(8,128)S(1)}, f32[16,32,128]{2,1,0:T(8,128)S(1)}) custom-call(f32[24,16,128]{2,1,0:T(8,128)S(1)} %get-tuple-element.24.partial, f32[26,8,128]{2,1,0:T(8,128)S(1)} %collective-permute-done.from_north, f32[26,8,128]{2,1,0:T(8,128)S(1)} %collective-permute-done.1.from_south, f32[24,16,128]{2,1,0:T(8,128)S(1)} %copy-done, ...), custom_call_target="tpu_custom_call" | custom-call | flops 1000000 | bytes 1000000 | tf_op jit(solution)/shard_map/pallas_call | solution.py:583
  22.9 15.2 %all_to_all.15.arrived = f32[16,32,128]{2,1,0:T(8,128)S(1)} all-to-all(f32[16,32,128]{2,1,0:T(8,128)S(1)} %get-tuple-element.30), channel_id=1, replica_groups=mesh['grp'=2,'gx'=16,'gy'=8] {'gx'}, dimensions={0} | all-to-all | bytes 524288 | tf_op jit(solution)/shard_map/all_to_all | solution.py:660
  38.1 15.2 %all_to_all.16.totals = f32[16,8,128]{2,1,0:T(8,128)S(1)} all-to-all(f32[16,8,128]{2,1,0:T(8,128)S(1)} %broadcast_in_dim.4), channel_id=1, replica_groups=mesh['grp'=2,'gx'=16,'gy'=8] {'grp','gy'}, dimensions={0} | all-to-all | bytes 131072 | tf_op jit(solution)/shard_map/all_to_all | solution.py:662
  53.3 0.0 copy-done.11
  53.3 0.0 copy-done.1
  53.3 0.0 copy-done.2
  53.3 0.0 copy-done.3
  53.3 0.0 copy-done.4
  53.3 3.9 %shard_map.149 = (f32[16,8,128]{2,1,0:T(8,128)}, f32[26,24,128]{2,1,0:T(8,128)S(1)}, f32[384,128]{1,0:T(8,128)S(1)}, f32[384,128]{1,0:T(8,128)S(1)}, f32[64,128]{1,0:T(8,128)S(1)}) custom-call(s32[8]{0:T(128)S(1)} %bitcast.14, f32[16,8,128]{2,1,0:T(8,128)S(1)} %all_to_all.16.totals, f32[4,32,24,128]{3,2,1,0:T(8,128)S(1)} %get-tuple-element.31.powers, ...), custom_call_target="tpu_custom_call" | custom-call | flops 1000000 | bytes 1000000 | tf_op jit(solution)/shard_map/pallas_call | solution.py:583
  57.2 0.0 copy-start.6
  57.2 0.0 copy-start.10
  57.2 3.6 %all-to-all-start.2 = ((f32[16,8,128]{2,1,0:T(8,128)}), f32[16,8,128]{2,1,0:T(8,128)S(1)}, u32[]{:S(2)}, u32[]{:S(2)}) async-start(f32[16,8,128]{2,1,0:T(8,128)} %get-tuple-element.41), calls=%async_computation.2 | async-start | bytes 131072 | tf_op jit(solution)/shard_map/all_to_all | solution.py:691
  60.9 2.2 %shard_map.150 = (f32[24,16,128]{2,1,0:T(8,128)}, f32[24,16,128]{2,1,0:T(8,128)}, f32[24,16,128]{2,1,0:T(8,128)}, f32[24,16,128]{2,1,0:T(8,128)}, f32[24,16,128]{2,1,0:T(8,128)}) custom-call(s32[8]{0:T(128)S(1)} %bitcast.15, f32[26,24,128]{2,1,0:T(8,128)S(1)} %get-tuple-element.32.potential, f32[384,128]{1,0:T(8,128)S(1)} %get-tuple-element.33.warmth, ...), custom_call_target="tpu_custom_call" | custom-call | flops 1000000 | bytes 1000000 | tf_op jit(solution)/shard_map/pallas_call | solution.py:583
  63.0 7.3 %all-to-all-done.2 = f32[16,8,128]{2,1,0:T(8,128)S(1)} async-done(((f32[16,8,128]{2,1,0:T(8,128)}), f32[16,8,128]{2,1,0:T(8,128)S(1)}, u32[]{:S(2)}, u32[]{:S(2)}) %all-to-all-start.2) | async-done | bytes 65568 | tf_op jit(solution)/shard_map/all_to_all | solution.py:691
  70.3 0.0 copy-done.6
  70.3 0.0 copy-done.10
  70.3 1.2 %shard_map.151 = f32[16,1024]{1,0:T(8,128)} custom-call(s32[16]{0:T(128)S(1)} %bitcast.13, f32[128,128]{1,0:T(8,128)S(1)} %bitcast.7, f32[16,1024]{1,0:T(8,128)S(1)} %bitcast.9), custom_call_target="tpu_custom_call" | custom-call | flops 1000000 | bytes 1000000 | tf_op jit(solution)/shard_map/pallas_call | solution.py:583
  (3 shorter events, 0.1 us)
Async XLA Ops:
  0.6 21.3 %copy-start = (f32[24,16,128]{2,1,0:T(8,128)S(1)}, f32[24,16,128]{2,1,0:T(8,128)}, u32[]{:S(2)}) copy-start(f32[24,16,128]{2,1,0:T(8,128)} %meridional.5) | copy-start | bytes 589828
  0.6 52.7 %copy-start.11 = (s32[1,1,8]{2,1,0:T(1,128)S(1)}, s32[1,1,8]{2,1,0:T(1,128)}, u32[]{:S(2)}) copy-start(s32[1,1,8]{2,1,0:T(1,128)} %param.15) | copy-start | bytes 100
  2.2 51.1 %copy-start.1 = (f32[24,16,128]{2,1,0:T(8,128)S(1)}, f32[24,16,128]{2,1,0:T(8,128)}, u32[]{:S(2)}) copy-start(f32[24,16,128]{2,1,0:T(8,128)} %theta.3) | copy-start | bytes 589828
  2.2 51.1 %copy-start.2 = (f32[24,16,128]{2,1,0:T(8,128)S(1)}, f32[24,16,128]{2,1,0:T(8,128)}, u32[]{:S(2)}) copy-start(f32[24,16,128]{2,1,0:T(8,128)} %humidity.3) | copy-start | bytes 589828
  2.2 51.1 %copy-start.3 = (f32[24,16,128]{2,1,0:T(8,128)S(1)}, f32[24,16,128]{2,1,0:T(8,128)}, u32[]{:S(2)}) copy-start(f32[24,16,128]{2,1,0:T(8,128)} %zonal.3) | copy-start | bytes 589828
  2.2 51.1 %copy-start.4 = (f32[24,16,128]{2,1,0:T(8,128)S(1)}, f32[24,16,128]{2,1,0:T(8,128)}, u32[]{:S(2)}) copy-start(f32[24,16,128]{2,1,0:T(8,128)} %vertical.3) | copy-start | bytes 589828
  2.2 5.1 %collective-permute-start = (f32[26,8,128]{2,1,0:T(8,128)S(1)}, f32[26,8,128]{2,1,0:T(8,128)S(1)}, u32[]{:S(2)}, u32[]{:S(2)}) collective-permute-start(f32[26,8,128]{2,1,0:T(8,128)S(1)} %get-tuple-element.25), channel_id=1, source_target_pairs={{0,7},{1,0},{2,1},{3,2},{4,3},{5,4},{6,5},{7,6},{8,15},{9,8},{10,9... | collective-permute-start | bytes 319496 | tf_op jit(solution)/shard_map/ppermute | solution.py:624
  5.5 1.8 %collective-permute-start.1 = (f32[26,8,128]{2,1,0:T(8,128)S(1)}, f32[26,8,128]{2,1,0:T(8,128)S(1)}, u32[]{:S(2)}, u32[]{:S(2)}) collective-permute-start(f32[26,8,128]{2,1,0:T(8,128)S(1)} %get-tuple-element.26), channel_id=1, source_target_pairs={{0,1},{1,2},{2,3},{3,4},{4,5},{5,6},{6,7},{7,0},{8,9},{9,10},{10,1... | collective-permute-start | bytes 319496 | tf_op jit(solution)/shard_map/ppermute | solution.py:625
  7.4 11.9 %collective-permute-start.2 = (f32[7,24,128]{2,1,0:T(8,128)S(1)}, f32[7,24,128]{2,1,0:T(8,128)S(1)}, u32[]{:S(2)}, u32[]{:S(2)}) collective-permute-start(f32[7,24,128]{2,1,0:T(8,128)S(1)} %get-tuple-element.28.to_west), channel_id=1, source_target_pairs={{0,248},{8,0},{16,8},{24,16},{32,24},{40,32},{48,40},{56,48},{64,5... | collective-permute-start | bytes 258056 | tf_op jit(solution)/shard_map/ppermute | solution.py:632
  15.2 6.7 %collective-permute-start.3 = (f32[7,24,128]{2,1,0:T(8,128)S(1)}, f32[7,24,128]{2,1,0:T(8,128)S(1)}, u32[]{:S(2)}, u32[]{:S(2)}) collective-permute-start(f32[7,24,128]{2,1,0:T(8,128)S(1)} %get-tuple-element.29.to_east), channel_id=1, source_target_pairs={{0,8},{8,16},{16,24},{24,32},{32,40},{40,48},{48,56},{56,64},{64,7... | collective-permute-start | bytes 258056 | tf_op jit(solution)/shard_map/ppermute | solution.py:633
  15.2 0.8 %copy-start.5 = (f32[1,1,16,1024]{3,2,1,0:T(8,128)S(1)}, f32[1,1,16,1024]{3,2,1,0:T(8,128)}, u32[]{:S(2)}) copy-start(f32[1,1,16,1024]{3,2,1,0:T(8,128)} %param.17) | copy-start | bytes 196612
  16.1 0.8 %copy-start.7 = (f32[1,1,16,1024]{3,2,1,0:T(8,128)S(1)}, f32[1,1,16,1024]{3,2,1,0:T(8,128)}, u32[]{:S(2)}) copy-start(f32[1,1,16,1024]{3,2,1,0:T(8,128)} %param.18) | copy-start | bytes 196612
  16.9 0.8 %copy-start.8 = (s32[1,1,16,1024]{3,2,1,0:T(8,128)S(1)}, s32[1,1,16,1024]{3,2,1,0:T(8,128)}, u32[]{:S(2)}) copy-start(s32[1,1,16,1024]{3,2,1,0:T(8,128)} %param.19) | copy-start | bytes 196612
  17.8 0.7 copy-start.9
  57.2 13.1 %copy-start.6 = (f32[1,1,16,1024]{3,2,1,0:T(8,128)S(1)}, f32[1,1,16,1024]{3,2,1,0:T(8,128)}, u32[]{:S(2)}) copy-start(f32[1,1,16,1024]{3,2,1,0:T(8,128)} %param.17) | copy-start | bytes 196612
  57.2 13.1 %copy-start.10 = (s32[1,1,16]{2,1,0:T(1,128)S(1)}, s32[1,1,16]{2,1,0:T(1,128)}, u32[]{:S(2)}) copy-start(s32[1,1,16]{2,1,0:T(1,128)} %param.16) | copy-start | bytes 196
  57.2 13.1 %all-to-all-start.2 = ((f32[16,8,128]{2,1,0:T(8,128)}), f32[16,8,128]{2,1,0:T(8,128)S(1)}, u32[]{:S(2)}, u32[]{:S(2)}) async-start(f32[16,8,128]{2,1,0:T(8,128)} %get-tuple-element.41), calls=%async_computation.2 | async-start | bytes 131072 | tf_op jit(solution)/shard_map/all_to_all | solution.py:691

commit v3 on v2

--- a/solution.py
+++ b/solution.py
@@ -33,11 +33,10 @@
 SLOT_ROWS = 16
 DPB = 1024
 CHUNKS = DPB // LEVELS
-DROPS = 24
 PARCEL = 32
 SCALE = 1.0 / 6.0
-PACK_LIMIT = 24 * 1024 * 1024
 VMEM_LIMIT = 24 * 1024 * 1024
+COSTP = 1_000_000
 FIRST_LIMIT = 54600 * 1024
 
 f32 = jnp.float32
@@ -177,19 +176,14 @@
             target[t, 16:24] = jnp.zeros((8, LEVELS), f32)
 
 
-def pack_kernel(
-    counts, squares_far, numbers_far, cells_far, drops, squares, numbers, cells, arrivals
-):
-    copies = [
-        pltpu.make_async_copy(far, near, arrivals.at[n])
-        for n, (far, near) in enumerate(
-            ((squares_far, squares), (numbers_far, numbers), (cells_far, cells))
-        )
-    ]
-    for copy in copies:
-        copy.start()
-    for copy in copies:
-        copy.wait()
+def pack_kernel(squares, cells, packed):
+    for s in range(CHUNKS):
+        part = slice(LEVELS * s, LEVELS * (s + 1))
+        packed[pl.ds(s, SLOT_ROWS, stride=16), :] = squares[:, part]
+        packed[pl.ds(8 + s, SLOT_ROWS, stride=16), :] = cells[:, part].astype(f32)
+
+
+def pack_live_kernel(counts, numbers, packed):
     row = iota((SLOT_ROWS, LEVELS), 0)
     lane = iota((SLOT_ROWS, LEVELS), 1)
     live = jnp.zeros((SLOT_ROWS, LEVELS), jnp.int32)
@@ -197,11 +191,9 @@
         live = jnp.where(row == r, counts[r], live)
     for s in range(CHUNKS):
         part = slice(LEVELS * s, LEVELS * (s + 1))
-        drops[pl.ds(s, SLOT_ROWS, stride=DROPS), :] = squares[:, part]
-        drops[pl.ds(8 + s, SLOT_ROWS, stride=DROPS), :] = jnp.where(
+        packed[pl.ds(s, SLOT_ROWS, stride=8), :] = jnp.where(
             lane + LEVELS * s < live, numbers[:, part], 0.0
         )
-        drops[pl.ds(16 + s, SLOT_ROWS, stride=DROPS), :] = cells[:, part].astype(f32)
 
 
 def power_kernel(
@@ -214,6 +206,7 @@
     from_east,
     from_west,
     drops,
+    live,
     powers,
     parcels,
 ):
@@ -275,8 +268,10 @@
     for k in range(2 * ITERS):
         packed = jnp.where(sub8 == k, jnp.sum(sums[k], axis=0, keepdims=True), packed)
     for r in range(SLOT_ROWS):
-        parcels[r, 0:DROPS] = drops[DROPS * r : DROPS * (r + 1)]
-        parcels[r, DROPS:PARCEL] = packed
+        parcels[r, 0:8] = drops[16 * r : 16 * r + 8]
+        parcels[r, 8:16] = live[8 * r : 8 * r + 8]
+        parcels[r, 16:24] = drops[16 * r + 8 : 16 * r + 16]
+        parcels[r, 24:PARCEL] = packed
 
 
 def two_sum(a, b):
@@ -623,24 +618,21 @@
     )
     from_north = lax.ppermute(to_south, "gy", ring("gy", -1))
     from_south = lax.ppermute(to_north, "gy", ring("gy", 1))
+    edges, early_squares, early_cells = lax.optimization_barrier((edges, squares, cells))
+    drops = local(
+        pack_kernel, [shape(SLOT_ROWS * 16, LEVELS)], [], [early_squares, early_cells], cost=COSTP
+    )
+    edges, drops = lax.optimization_barrier((edges, drops))
     to_west, to_east = local(
         side_kernel,
         [shape(7, EY, LEVELS), shape(7, EY, LEVELS)],
         [],
         [partial, from_north, from_south, edges],
     )
+    to_west, to_east, late_numbers = lax.optimization_barrier((to_west, to_east, numbers))
+    live = local(pack_live_kernel, [shape(SLOT_ROWS * 8, LEVELS)], [counts], [late_numbers], cost=COSTP)
     from_east = lax.ppermute(to_west, tiles, ring(tiles, -1))
     from_west = lax.ppermute(to_east, tiles, ring(tiles, 1))
-    drops = local(
-        pack_kernel,
-        [shape(SLOT_ROWS * DROPS, LEVELS)],
-        [counts],
-        [squares, numbers, cells],
-        [pltpu.VMEM((SLOT_ROWS, DPB), f32)] * 2
-        + [pltpu.VMEM((SLOT_ROWS, DPB), jnp.int32), pltpu.SemaphoreType.DMA((3,))],
-        far=3,
-        limit=PACK_LIMIT,
-    )
     powers, parcels = local(
         power_kernel,
         [shape(ITERS, EX, EY, LEVELS), shape(SLOT_ROWS, PARCEL, LEVELS)],
@@ -655,6 +647,7 @@
             from_east,
             from_west,
             drops,
+            live,
         ],
     )
     arrived = lax.all_to_all(parcels, "gx", split_axis=0, concat_axis=0, tiled=True)

time: 71.9 us -> 71.9 us (level)
  waiting for transfers between devices: 11.7 us -> 13.5 us
  local copies, waits for them, and re-layouts: 3.22 us -> 1.73 us
    ppermute x1, waiting for transfers between devices: 2.6 us -> 5.13 us  [on_device(): from_west = lax.ppermute(to_east, tiles, ring(tiles, 1))]
    ppermute x1, waiting for transfers between devices: 1.83 us -> 0.11 us  [on_device(): from_north = lax.ppermute(to_south, 'gy', ring('gy', -1))]
    unnamed x24 -> x22, local copies, waits for them, and re-layouts: 3.21 us -> 1.72 us
    all_to_all x1, blocking collectives: 15.2 us -> 16.3 us  [on_device(): lax.all_to_all(shared, ('grp', 'gy'), split_axis=0, concat_axis=0, tiled=...]
    all_to_all x1, blocking collectives: 15.2 us -> 14.1 us  [on_device(): lax.all_to_all(parcels, 'gx', split_axis=0, concat_axis=0, tiled=True)]
    ppermute x1, waiting for transfers between devices: 0.01 us -> 0.94 us  [on_device(): from_east = lax.ppermute(to_west, tiles, ring(tiles, -1))]
    pallas_call x7 -> x8, Pallas kernels: 10.6 us -> 10.4 us  [local(): pl.pallas_call(kernel, out_shape=outs[0] if single else outs, in_specs=[p...]
  transfers between devices with their start and end apart: 5 -> 5, of which waited for: 3 -> 4; matrix products, arithmetic and copies ran while one was open for 0% -> 0% of each run, Pallas kernels for 4% -> 4%
where the time goes in v3:
time: 71.9 us; the launch traced here: 71.5 us
  blocking collectives  30.4 us (42%)
  starting transfers between devices  14.7 us (20%)
  waiting for transfers between devices  13.5 us (19%)
  Pallas kernels  10.4 us (14%)
  local copies, waits for them, and re-layouts  1.73 us (2%)
  between operations  0.78 us (1%)
    all_to_all x1, blocking collectives, on_device(): lax.all_to_all(shared, ('grp', 'gy'), split_axis=0, concat_axis=0, tiled=...  16.3 us
    all_to_all x1, blocking collectives, on_device(): lax.all_to_all(parcels, 'gx', split_axis=0, concat_axis=0, tiled=True)  14.1 us
    pallas_call x8, Pallas kernels, local(): pl.pallas_call(kernel, out_shape=outs[0] if single else outs, in_specs=[p...  10.4 us
    ppermute x1, starting transfers between devices, on_device(): from_east = lax.ppermute(to_west, tiles, ring(tiles, -1))  7.85 us
    all_to_all x1, waiting for transfers between devices, on_device(): lax.all_to_all(returned, 'gx', split_axis=0, concat_axis=0, tiled=True)  7.27 us
    ppermute x1, waiting for transfers between devices, on_device(): from_west = lax.ppermute(to_east, tiles, ring(tiles, 1))  5.13 us
    all_to_all x1, starting transfers between devices, on_device(): lax.all_to_all(returned, 'gx', split_axis=0, concat_axis=0, tiled=True)  3.63 us
    ppermute x1, starting transfers between devices, on_device(): from_north = lax.ppermute(to_south, 'gy', ring('gy', -1))  3.25 us
  transfers between devices with their start and end apart: 5, of which 4 were waited for; matrix products, arithmetic and copies ran while one was open for 0% of the time, Pallas kernels for 4%

profile of v3, /device:TPU:1, one launch (start us, length us, event | category | flops | bytes accessed | tf_op | source)
XLA Modules:
  0.0 71.5 jit_solution(3989587428904398481)
XLA Ops:
  0.6 0.0 copy-start
  0.6 0.0 copy-start.7
  0.7 0.0 copy-start.9
  0.7 0.0 copy-start.10
  0.7 1.6 %shard_map.145 = (f32[24,16,128]{2,1,0:T(8,128)S(1)}, f32[26,8,128]{2,1,0:T(8,128)S(1)}, f32[26,8,128]{2,1,0:T(8,128)S(1)}, f32[14,16,128]{2,1,0:T(8,128)S(1)}) custom-call(f32[24,16,128]{2,1,0:T(8,128)} %theta.3, f32[24,16,128]{2,1,0:T(8,128)} %humidity.3, f32[24,16,128]{2,1,0:T(8,128)} %zonal.3, f32[24,16,128]{2,1,0:T(8,128)} %meridional.5, ...), custom_call_target="tpu_custom_call" | custom-call | flops 1000000 | bytes 1000000 | tf_op jit(solution)/shard_map/pallas_call | solution.py:578
  2.3 0.0 copy-start.1
  2.3 0.0 copy-start.2
  2.3 0.0 copy-start.3
  2.3 0.0 copy-start.4
  2.3 3.3 %collective-permute-start = (f32[26,8,128]{2,1,0:T(8,128)S(1)}, f32[26,8,128]{2,1,0:T(8,128)S(1)}, u32[]{:S(2)}, u32[]{:S(2)}) collective-permute-start(f32[26,8,128]{2,1,0:T(8,128)S(1)} %get-tuple-element.33), channel_id=1, source_target_pairs={{0,7},{1,0},{2,1},{3,2},{4,3},{5,4},{6,5},{7,6},{8,15},{9,8},{10,9... | collective-permute-start | bytes 319496 | tf_op jit(solution)/shard_map/ppermute | solution.py:619
  5.6 0.0 collective-permute-start.1
  5.6 0.0 copy-start.5
  5.6 0.8 %copy-done.5 = f32[1,1,16,1024]{3,2,1,0:T(8,128)S(1)} copy-done((f32[1,1,16,1024]{3,2,1,0:T(8,128)S(1)}, f32[1,1,16,1024]{3,2,1,0:T(8,128)}, u32[]{:S(2)}) %copy-start.5) | copy-done | bytes 65560
  6.4 0.0 copy-start.8
  6.4 0.8 %copy-done.8 = s32[1,1,16,1024]{3,2,1,0:T(8,128)S(1)} copy-done((s32[1,1,16,1024]{3,2,1,0:T(8,128)S(1)}, s32[1,1,16,1024]{3,2,1,0:T(8,128)}, u32[]{:S(2)}) %copy-start.8) | copy-done | bytes 65560
  7.3 0.1 collective-permute-done.from_north
  7.4 0.0 collective-permute-done.1.from_south
  7.4 7.8 %collective-permute-start.2 = (f32[7,24,128]{2,1,0:T(8,128)S(1)}, f32[7,24,128]{2,1,0:T(8,128)S(1)}, u32[]{:S(2)}, u32[]{:S(2)}) collective-permute-start(f32[7,24,128]{2,1,0:T(8,128)S(1)} %get-tuple-element.42.to_west), channel_id=1, source_target_pairs={{0,248},{8,0},{16,8},{24,16},{32,24},{40,32},{48,40},{56,48},{64,5... | collective-permute-start | bytes 258056 | tf_op jit(solution)/shard_map/ppermute | solution.py:634
  15.3 0.0 collective-permute-start.3
  15.3 0.0 copy-done.7
  15.3 0.0 copy-done.9
  15.3 0.6 shard_map.148.live
  15.9 0.9 %collective-permute-done.2.from_east = f32[7,24,128]{2,1,0:T(8,128)S(1)} collective-permute-done((f32[7,24,128]{2,1,0:T(8,128)S(1)}, f32[7,24,128]{2,1,0:T(8,128)S(1)}, u32[]{:S(2)}, u32[]{:S(2)}) %collective-permute-start.2) | collective-permute-done | bytes 86048 | tf_op jit(solution)/shard_map/ppermute | solution.py:634
  16.8 5.1 %collective-permute-done.3.from_west = f32[7,24,128]{2,1,0:T(8,128)S(1)} collective-permute-done((f32[7,24,128]{2,1,0:T(8,128)S(1)}, f32[7,24,128]{2,1,0:T(8,128)S(1)}, u32[]{:S(2)}, u32[]{:S(2)}) %collective-permute-start.3) | collective-permute-done | bytes 86048 | tf_op jit(solution)/shard_map/ppermute | solution.py:635
  21.9 0.0 copy-done
  21.9 1.0 %shard_map.149 = (f32[4,32,24,128]{3,2,1,0:T(8,128)S(1)}, f32[16,32,128]{2,1,0:T(8,128)S(1)}) custom-call(f32[24,16,128]{2,1,0:T(8,128)S(1)} %get-tuple-element.32.partial, f32[26,8,128]{2,1,0:T(8,128)S(1)} %collective-permute-done.from_north, f32[26,8,128]{2,1,0:T(8,128)S(1)} %collective-permute-done.1.from_south, f32[24,16,128]{2,1,0:T(8,128)S(1)} %copy-done, ...), custom_call_target="tpu_custom_call" | custom-call | flops 1000000 | bytes 1000000 | tf_op jit(solution)/shard_map/pallas_call | solution.py:578
  22.9 14.1 %all_to_all.15.arrived = f32[16,32,128]{2,1,0:T(8,128)S(1)} all-to-all(f32[16,32,128]{2,1,0:T(8,128)S(1)} %get-tuple-element.46), channel_id=1, replica_groups=mesh['grp'=2,'gx'=16,'gy'=8] {'gx'}, dimensions={0} | all-to-all | bytes 524288 | tf_op jit(solution)/shard_map/all_to_all | solution.py:653
  37.1 16.3 %all_to_all.16.totals = f32[16,8,128]{2,1,0:T(8,128)S(1)} all-to-all(f32[16,8,128]{2,1,0:T(8,128)S(1)} %broadcast_in_dim.4), channel_id=1, replica_groups=mesh['grp'=2,'gx'=16,'gy'=8] {'grp','gy'}, dimensions={0} | all-to-all | bytes 131072 | tf_op jit(solution)/shard_map/all_to_all | solution.py:655
  53.4 0.0 copy-done.10
  53.4 0.0 copy-done.1
  53.4 0.0 copy-done.2
  53.4 0.0 copy-done.3
  53.4 0.0 copy-done.4
  53.4 3.9 %shard_map.150 = (f32[16,8,128]{2,1,0:T(8,128)}, f32[26,24,128]{2,1,0:T(8,128)S(1)}, f32[384,128]{1,0:T(8,128)S(1)}, f32[384,128]{1,0:T(8,128)S(1)}, f32[64,128]{1,0:T(8,128)S(1)}) custom-call(s32[8]{0:T(128)S(1)} %bitcast.14, f32[16,8,128]{2,1,0:T(8,128)S(1)} %all_to_all.16.totals, f32[4,32,24,128]{3,2,1,0:T(8,128)S(1)} %get-tuple-element.47.powers, ...), custom_call_target="tpu_custom_call" | custom-call | flops 1000000 | bytes 1000000 | tf_op jit(solution)/shard_map/pallas_call | solution.py:578
  57.3 0.0 copy-start.6
  57.3 3.6 %all-to-all-start.2 = ((f32[16,8,128]{2,1,0:T(8,128)}), f32[16,8,128]{2,1,0:T(8,128)S(1)}, u32[]{:S(2)}, u32[]{:S(2)}) async-start(f32[16,8,128]{2,1,0:T(8,128)} %get-tuple-element.57), calls=%async_computation.2 | async-start | bytes 131072 | tf_op jit(solution)/shard_map/all_to_all | solution.py:684
  60.9 2.1 %shard_map.151 = (f32[24,16,128]{2,1,0:T(8,128)}, f32[24,16,128]{2,1,0:T(8,128)}, f32[24,16,128]{2,1,0:T(8,128)}, f32[24,16,128]{2,1,0:T(8,128)}, f32[24,16,128]{2,1,0:T(8,128)}) custom-call(s32[8]{0:T(128)S(1)} %bitcast.15, f32[26,24,128]{2,1,0:T(8,128)S(1)} %get-tuple-element.48.potential, f32[384,128]{1,0:T(8,128)S(1)} %get-tuple-element.49.warmth, ...), custom_call_target="tpu_custom_call" | custom-call | flops 1000000 | bytes 1000000 | tf_op jit(solution)/shard_map/pallas_call | solution.py:578
  63.1 7.3 %all-to-all-done.2 = f32[16,8,128]{2,1,0:T(8,128)S(1)} async-done(((f32[16,8,128]{2,1,0:T(8,128)}), f32[16,8,128]{2,1,0:T(8,128)S(1)}, u32[]{:S(2)}, u32[]{:S(2)}) %all-to-all-start.2) | async-done | bytes 65568 | tf_op jit(solution)/shard_map/all_to_all | solution.py:684
  70.3 0.0 copy-done.6
  70.3 1.2 %shard_map.152 = f32[16,1024]{1,0:T(8,128)} custom-call(s32[16]{0:T(128)S(1)} %bitcast.13, f32[128,128]{1,0:T(8,128)S(1)} %bitcast.7, f32[16,1024]{1,0:T(8,128)S(1)} %bitcast.9), custom_call_target="tpu_custom_call" | custom-call | flops 1000000 | bytes 1000000 | tf_op jit(solution)/shard_map/pallas_call | solution.py:578
  (4 shorter events, 0.1 us)
Async XLA Ops:
  0.6 21.3 %copy-start = (f32[24,16,128]{2,1,0:T(8,128)S(1)}, f32[24,16,128]{2,1,0:T(8,128)}, u32[]{:S(2)}) copy-start(f32[24,16,128]{2,1,0:T(8,128)} %meridional.5) | copy-start | bytes 589828
  0.6 14.6 %copy-start.7 = (f32[1,1,16,1024]{3,2,1,0:T(8,128)S(1)}, f32[1,1,16,1024]{3,2,1,0:T(8,128)}, u32[]{:S(2)}) copy-start(f32[1,1,16,1024]{3,2,1,0:T(8,128)} %param.18) | copy-start | bytes 196612
  0.7 14.6 %copy-start.9 = (s32[1,1,16]{2,1,0:T(1,128)S(1)}, s32[1,1,16]{2,1,0:T(1,128)}, u32[]{:S(2)}) copy-start(s32[1,1,16]{2,1,0:T(1,128)} %param.16) | copy-start | bytes 196
  0.7 52.7 %copy-start.10 = (s32[1,1,8]{2,1,0:T(1,128)S(1)}, s32[1,1,8]{2,1,0:T(1,128)}, u32[]{:S(2)}) copy-start(s32[1,1,8]{2,1,0:T(1,128)} %param.15) | copy-start | bytes 100
  2.3 51.1 %copy-start.1 = (f32[24,16,128]{2,1,0:T(8,128)S(1)}, f32[24,16,128]{2,1,0:T(8,128)}, u32[]{:S(2)}) copy-start(f32[24,16,128]{2,1,0:T(8,128)} %theta.3) | copy-start | bytes 589828
  2.3 51.1 %copy-start.2 = (f32[24,16,128]{2,1,0:T(8,128)S(1)}, f32[24,16,128]{2,1,0:T(8,128)}, u32[]{:S(2)}) copy-start(f32[24,16,128]{2,1,0:T(8,128)} %humidity.3) | copy-start | bytes 589828
  2.3 51.1 %copy-start.3 = (f32[24,16,128]{2,1,0:T(8,128)S(1)}, f32[24,16,128]{2,1,0:T(8,128)}, u32[]{:S(2)}) copy-start(f32[24,16,128]{2,1,0:T(8,128)} %zonal.3) | copy-start | bytes 589828
  2.3 51.1 %copy-start.4 = (f32[24,16,128]{2,1,0:T(8,128)S(1)}, f32[24,16,128]{2,1,0:T(8,128)}, u32[]{:S(2)}) copy-start(f32[24,16,128]{2,1,0:T(8,128)} %vertical.3) | copy-start | bytes 589828
  2.3 5.1 %collective-permute-start = (f32[26,8,128]{2,1,0:T(8,128)S(1)}, f32[26,8,128]{2,1,0:T(8,128)S(1)}, u32[]{:S(2)}, u32[]{:S(2)}) collective-permute-start(f32[26,8,128]{2,1,0:T(8,128)S(1)} %get-tuple-element.33), channel_id=1, source_target_pairs={{0,7},{1,0},{2,1},{3,2},{4,3},{5,4},{6,5},{7,6},{8,15},{9,8},{10,9... | collective-permute-start | bytes 319496 | tf_op jit(solution)/shard_map/ppermute | solution.py:619
  5.6 1.8 %collective-permute-start.1 = (f32[26,8,128]{2,1,0:T(8,128)S(1)}, f32[26,8,128]{2,1,0:T(8,128)S(1)}, u32[]{:S(2)}, u32[]{:S(2)}) collective-permute-start(f32[26,8,128]{2,1,0:T(8,128)S(1)} %get-tuple-element.34), channel_id=1, source_target_pairs={{0,1},{1,2},{2,3},{3,4},{4,5},{5,6},{6,7},{7,0},{8,9},{9,10},{10,1... | collective-permute-start | bytes 319496 | tf_op jit(solution)/shard_map/ppermute | solution.py:620
  5.6 0.8 %copy-start.5 = (f32[1,1,16,1024]{3,2,1,0:T(8,128)S(1)}, f32[1,1,16,1024]{3,2,1,0:T(8,128)}, u32[]{:S(2)}) copy-start(f32[1,1,16,1024]{3,2,1,0:T(8,128)} %param.17) | copy-start | bytes 196612
  6.4 0.8 %copy-start.8 = (s32[1,1,16,1024]{3,2,1,0:T(8,128)S(1)}, s32[1,1,16,1024]{3,2,1,0:T(8,128)}, u32[]{:S(2)}) copy-start(s32[1,1,16,1024]{3,2,1,0:T(8,128)} %param.19) | copy-start | bytes 196612
  7.4 9.4 %collective-permute-start.2 = (f32[7,24,128]{2,1,0:T(8,128)S(1)}, f32[7,24,128]{2,1,0:T(8,128)S(1)}, u32[]{:S(2)}, u32[]{:S(2)}) collective-permute-start(f32[7,24,128]{2,1,0:T(8,128)S(1)} %get-tuple-element.42.to_west), channel_id=1, source_target_pairs={{0,248},{8,0},{16,8},{24,16},{32,24},{40,32},{48,40},{56,48},{64,5... | collective-permute-start | bytes 258056 | tf_op jit(solution)/shard_map/ppermute | solution.py:634
  15.3 6.7 %collective-permute-start.3 = (f32[7,24,128]{2,1,0:T(8,128)S(1)}, f32[7,24,128]{2,1,0:T(8,128)S(1)}, u32[]{:S(2)}, u32[]{:S(2)}) collective-permute-start(f32[7,24,128]{2,1,0:T(8,128)S(1)} %get-tuple-element.43.to_east), channel_id=1, source_target_pairs={{0,8},{8,16},{16,24},{24,32},{32,40},{40,48},{48,56},{56,64},{64,7... | collective-permute-start | bytes 258056 | tf_op jit(solution)/shard_map/ppermute | solution.py:635
  57.3 13.1 %copy-start.6 = (f32[1,1,16,1024]{3,2,1,0:T(8,128)S(1)}, f32[1,1,16,1024]{3,2,1,0:T(8,128)}, u32[]{:S(2)}) copy-start(f32[1,1,16,1024]{3,2,1,0:T(8,128)} %param.17) | copy-start | bytes 196612
  57.3 13.1 %all-to-all-start.2 = ((f32[16,8,128]{2,1,0:T(8,128)}), f32[16,8,128]{2,1,0:T(8,128)S(1)}, u32[]{:S(2)}, u32[]{:S(2)}) async-start(f32[16,8,128]{2,1,0:T(8,128)} %get-tuple-element.57), calls=%async_computation.2 | async-start | bytes 131072 | tf_op jit(solution)/shard_map/all_to_all | solution.py:684

commit v4 on v3

--- a/solution.py
+++ b/solution.py
@@ -326,11 +326,12 @@
     for t in range(1, totals.shape[0]):
         high, e = two_sum(high, totals[t])
         low = low + e
-    by = LEVELS // 2
-    high, low = quick_sum(high, low)
-    while by:
-        high, low = pair_add((high, low), (turn(high, by, 1), turn(low, by, 1)))
-        by //= 2
+    bound = 256.0 * jnp.max(jnp.abs(high), axis=1, keepdims=True)
+    coarse = (bound + high) - bound
+    fine = (high - coarse) + low
+    high, low = quick_sum(
+        jnp.sum(coarse, axis=1, keepdims=True), jnp.sum(fine, axis=1, keepdims=True)
+    )
     moment = []
     for k in range(2 * ITERS):
         moment.append(
@@ -392,7 +393,7 @@
     )
 
 
-def growth_kernel(
+def step_kernel(
     owners,
     totals,
     powers,
@@ -406,17 +407,41 @@
     from_south,
     from_east,
     from_west,
+    new_theta,
+    new_humidity,
+    new_zonal,
+    new_meridional,
+    new_vertical,
     returned,
     potential,
     warmth,
     vapour,
     mass,
     excess,
+    condensed,
     picked_excess,
     picked_warmth,
+    spans,
 ):
     level, _, _, _ = vertical_profiles()
     sub = iota((CY, LEVELS), 0)
+    for i in range(CX):
+        for f, (field, side, in_north, in_south) in enumerate(
+            ((theta, 5, 5, 1), (humidity, 6, 6, 2))
+        ):
+            values = field[i]
+            f_e = field[i + 1] if i < CX - 1 else from_east[side, 0:16]
+            f_w = field[i - 1] if i > 0 else from_west[side, 0:16]
+            f_n = jnp.where(
+                sub < CY - 1, turn(values, -1, 0), from_north[i, in_north : in_north + 1]
+            )
+            f_s = jnp.where(sub > 0, turn(values, 1, 0), from_south[i, in_south : in_south + 1])
+            f_t = jnp.where(level < LEVELS - 1, turn(values, -1, 1), values)
+            f_b = jnp.where(level > 0, turn(values, 1, 1), values)
+            for n, span in enumerate(
+                (values - f_w, f_e - values, values - f_s, f_n - values, values - f_b, f_t - values)
+            ):
+                spans[6 * f + n, i] = span
     weights = coefficients(totals)
     for t in range(CX + 2):
         i = (t - 1) % EX
@@ -426,28 +451,17 @@
         potential[t] = total
     for i in range(CX):
         east, north, up = new_winds(i, potential, theta, humidity, zonal, meridional, vertical)
+        new_zonal[i] = east
+        new_meridional[i] = north
+        new_vertical[i] = up
         moved = []
-        for f, (field, side, in_north, in_south) in enumerate(
-            ((theta, 5, 5, 1), (humidity, 6, 6, 2))
-        ):
-            values = field[i]
-            f_e = field[i + 1] if i < CX - 1 else from_east[side, 0:16]
-            f_w = field[i - 1] if i > 0 else from_west[side, 0:16]
-            f_n = jnp.where(
-                sub < CY - 1, turn(values, -1, 0), from_north[i, in_north : in_north + 1]
-            )
-            f_s = jnp.where(sub > 0, turn(values, 1, 0), from_south[i, in_south : in_south + 1])
-            f_t = jnp.where(level < LEVELS - 1, turn(values, -1, 1), values)
-            f_b = jnp.where(level > 0, turn(values, 1, 1), values)
+        for f, field in enumerate((theta, humidity)):
             tendency = (
-                jnp.maximum(east, 0.0) * (values - f_w)
-                + jnp.minimum(east, 0.0) * (f_e - values)
-                + jnp.maximum(north, 0.0) * (values - f_s)
-                + jnp.minimum(north, 0.0) * (f_n - values)
-                + jnp.maximum(up, 0.0) * (values - f_b)
-                + jnp.minimum(up, 0.0) * (f_t - values)
-            )
-            moved.append(values - TIME_INCREMENT * tendency)
+                east * jnp.where(east > 0.0, spans[6 * f, i], spans[6 * f + 1, i])
+                + north * jnp.where(north > 0.0, spans[6 * f + 2, i], spans[6 * f + 3, i])
+                + up * jnp.where(up > 0.0, spans[6 * f + 4, i], spans[6 * f + 5, i])
+            )
+            moved.append(field[i] - TIME_INCREMENT * tendency)
         rows = slice(CY * i, CY * (i + 1))
         warmth[rows] = moved[0]
         vapour[rows] = moved[1]
@@ -501,33 +515,6 @@
             number > 0.0, number * (now * jnp.sqrt(now) - old * jnp.sqrt(old)), 0.0
         )
         returned[owner] = now
-
-
-def condense_kernel(
-    owners,
-    potential,
-    warmth,
-    vapour,
-    mass,
-    arrived,
-    theta,
-    humidity,
-    zonal,
-    meridional,
-    vertical,
-    new_theta,
-    new_humidity,
-    new_zonal,
-    new_meridional,
-    new_vertical,
-    condensed,
-):
-    for i in range(CX):
-        new_zonal[i], new_meridional[i], new_vertical[i] = new_winds(
-            i, potential, theta, humidity, zonal, meridional, vertical
-        )
-    height = iota((BAND, 2 * LEVELS), 0)
-    place = iota((2 * CX, 2 * LEVELS), 0)
     for b in range(NBD):
         heights, places = where_at(arrived, owners[b])
         gained = mass[CHUNKS * b : CHUNKS * (b + 1)]
@@ -655,15 +642,9 @@
     totals = lax.all_to_all(shared, ("grp", "gy"), split_axis=0, concat_axis=0, tiled=True)
     flat = (CX * CY, LEVELS)
     picked = (NBD * CHUNKS, LEVELS)
-    returned, potential, warmth, vapour, mass = local(
-        growth_kernel,
-        [
-            shape(SLOT_ROWS, CHUNKS, LEVELS),
-            shape(CX + 2, EY, LEVELS),
-            shape(*flat),
-            shape(*flat),
-            shape(*picked),
-        ],
+    new_theta, new_humidity, new_zonal, new_meridional, new_vertical, returned = local(
+        step_kernel,
+        [tile] * 5 + [shape(SLOT_ROWS, CHUNKS, LEVELS)],
         [owners],
         [
             totals,
@@ -679,27 +660,14 @@
             from_east,
             from_west,
         ],
-        [pltpu.VMEM(flat, f32)] + [pltpu.VMEM(picked, f32)] * 2,
+        [pltpu.VMEM((CX + 2, EY, LEVELS), f32)]
+        + [pltpu.VMEM(flat, f32)] * 2
+        + [pltpu.VMEM(picked, f32)]
+        + [pltpu.VMEM(flat, f32)] * 2
+        + [pltpu.VMEM(picked, f32)] * 2
+        + [pltpu.VMEM((12, CX, CY, LEVELS), f32)],
     )
     returned = lax.all_to_all(returned, "gx", split_axis=0, concat_axis=0, tiled=True)
-    new_theta, new_humidity, new_zonal, new_meridional, new_vertical = local(
-        condense_kernel,
-        [tile] * 5,
-        [owners],
-        [
-            potential,
-            warmth,
-            vapour,
-            mass,
-            arrived,
-            theta,
-            humidity,
-            zonal,
-            meridional,
-            vertical,
-        ],
-        [pltpu.VMEM(flat, f32)],
-    )
     new_squares = local(
         size_kernel,
         [shape(SLOT_ROWS, DPB)],

time: 71.9 us -> 71.2 us (level)
  blocking collectives: 30.4 us -> 42.5 us
  waiting for transfers between devices: 13.5 us -> 6.19 us
  starting transfers between devices: 14.7 us -> 11.1 us
  Pallas kernels: 10.4 us -> 8.49 us
    all_to_all x0 -> x1, blocking collectives: none -> 12.2 us  [on_device(): lax.all_to_all(returned, 'gx', split_axis=0, concat_axis=0, tiled=True)]
    all_to_all x1 -> x0, waiting for transfers between devices: 7.27 us -> none  [on_device(): lax.all_to_all(returned, 'gx', split_axis=0, concat_axis=0, tiled=True)]
    all_to_all x1 -> x0, starting transfers between devices: 3.63 us -> none  [on_device(): lax.all_to_all(returned, 'gx', split_axis=0, concat_axis=0, tiled=True)]
    pallas_call x8 -> x7, Pallas kernels: 10.4 us -> 8.49 us  [local(): pl.pallas_call(kernel, out_shape=outs[0] if single else outs, in_specs=[p...]
  transfers between devices with their start and end apart: 5 -> 4, of which waited for: 4 -> 3; matrix products, arithmetic and copies ran while one was open for 0% -> 0% of each run, Pallas kernels for 4% -> 1%
where the time goes in v4:
time: 71.2 us; the launch traced here: 70.9 us
  blocking collectives  42.5 us (60%)
  starting transfers between devices  11.1 us (16%)
  Pallas kernels  8.49 us (12%)
  waiting for transfers between devices  6.19 us (9%)
  local copies, waits for them, and re-layouts  1.74 us (2%)
  between operations  0.78 us (1%)
    all_to_all x1, blocking collectives, on_device(): lax.all_to_all(shared, ('grp', 'gy'), split_axis=0, concat_axis=0, tiled=...  16.3 us
    all_to_all x1, blocking collectives, on_device(): lax.all_to_all(parcels, 'gx', split_axis=0, concat_axis=0, tiled=True)  14.1 us
    all_to_all x1, blocking collectives, on_device(): lax.all_to_all(returned, 'gx', split_axis=0, concat_axis=0, tiled=True)  12.2 us
    pallas_call x7, Pallas kernels, local(): pl.pallas_call(kernel, out_shape=outs[0] if single else outs, in_specs=[p...  8.49 us
    ppermute x1, starting transfers between devices, on_device(): from_east = lax.ppermute(to_west, tiles, ring(tiles, -1))  7.85 us
    ppermute x1, waiting for transfers between devices, on_device(): from_west = lax.ppermute(to_east, tiles, ring(tiles, 1))  5.13 us
    ppermute x1, starting transfers between devices, on_device(): from_north = lax.ppermute(to_south, 'gy', ring('gy', -1))  3.25 us
    unnamed x22, local copies, waits for them, and re-layouts  1.73 us
  transfers between devices with their start and end apart: 4, of which 3 were waited for; matrix products, arithmetic and copies ran while one was open for 0% of the time, Pallas kernels for 1%

profile of v4, /device:TPU:1, one launch (start us, length us, event | category | flops | bytes accessed | tf_op | source)
XLA Modules:
  0.0 70.9 jit_solution(17195442283075869705)
XLA Ops:
  0.6 0.0 copy-start
  0.6 0.0 copy-start.7
  0.7 0.0 copy-start.9
  0.7 0.0 copy-start.10
  0.7 1.6 %shard_map.145 = (f32[24,16,128]{2,1,0:T(8,128)S(1)}, f32[26,8,128]{2,1,0:T(8,128)S(1)}, f32[26,8,128]{2,1,0:T(8,128)S(1)}, f32[14,16,128]{2,1,0:T(8,128)S(1)}) custom-call(f32[24,16,128]{2,1,0:T(8,128)} %theta.1, f32[24,16,128]{2,1,0:T(8,128)} %humidity.1, f32[24,16,128]{2,1,0:T(8,128)} %zonal.1, f32[24,16,128]{2,1,0:T(8,128)} %meridional.3, ...), custom_call_target="tpu_custom_call" | custom-call | flops 1000000 | bytes 1000000 | tf_op jit(solution)/shard_map/pallas_call | solution.py:565
  2.3 0.0 copy-start.1
  2.3 0.0 copy-start.2
  2.3 0.0 copy-start.3
  2.3 0.0 copy-start.4
  2.3 3.3 %collective-permute-start = (f32[26,8,128]{2,1,0:T(8,128)S(1)}, f32[26,8,128]{2,1,0:T(8,128)S(1)}, u32[]{:S(2)}, u32[]{:S(2)}) collective-permute-start(f32[26,8,128]{2,1,0:T(8,128)S(1)} %get-tuple-element.29), channel_id=1, source_target_pairs={{0,7},{1,0},{2,1},{3,2},{4,3},{5,4},{6,5},{7,6},{8,15},{9,8},{10,9... | collective-permute-start | bytes 319496 | tf_op jit(solution)/shard_map/ppermute | solution.py:606
  5.6 0.0 collective-permute-start.1
  5.6 0.0 copy-start.5
  5.6 0.8 %copy-done.5 = f32[1,1,16,1024]{3,2,1,0:T(8,128)S(1)} copy-done((f32[1,1,16,1024]{3,2,1,0:T(8,128)S(1)}, f32[1,1,16,1024]{3,2,1,0:T(8,128)}, u32[]{:S(2)}) %copy-start.5) | copy-done | bytes 65560
  6.4 0.0 copy-start.8
  6.4 0.8 %copy-done.8 = s32[1,1,16,1024]{3,2,1,0:T(8,128)S(1)} copy-done((s32[1,1,16,1024]{3,2,1,0:T(8,128)S(1)}, s32[1,1,16,1024]{3,2,1,0:T(8,128)}, u32[]{:S(2)}) %copy-start.8) | copy-done | bytes 65560
  7.3 0.1 collective-permute-done.from_north
  7.4 0.0 collective-permute-done.1.from_south
  7.4 7.8 %collective-permute-start.2 = (f32[7,24,128]{2,1,0:T(8,128)S(1)}, f32[7,24,128]{2,1,0:T(8,128)S(1)}, u32[]{:S(2)}, u32[]{:S(2)}) collective-permute-start(f32[7,24,128]{2,1,0:T(8,128)S(1)} %get-tuple-element.38.to_west), channel_id=1, source_target_pairs={{0,248},{8,0},{16,8},{24,16},{32,24},{40,32},{48,40},{56,48},{64,5... | collective-permute-start | bytes 258056 | tf_op jit(solution)/shard_map/ppermute | solution.py:621
  15.3 0.0 collective-permute-start.3
  15.3 0.0 copy-done.7
  15.3 0.0 copy-done.9
  15.3 0.6 shard_map.148.live
  15.9 0.9 %collective-permute-done.2.from_east = f32[7,24,128]{2,1,0:T(8,128)S(1)} collective-permute-done((f32[7,24,128]{2,1,0:T(8,128)S(1)}, f32[7,24,128]{2,1,0:T(8,128)S(1)}, u32[]{:S(2)}, u32[]{:S(2)}) %collective-permute-start.2) | collective-permute-done | bytes 86048 | tf_op jit(solution)/shard_map/ppermute | solution.py:621
  16.8 5.1 %collective-permute-done.3.from_west = f32[7,24,128]{2,1,0:T(8,128)S(1)} collective-permute-done((f32[7,24,128]{2,1,0:T(8,128)S(1)}, f32[7,24,128]{2,1,0:T(8,128)S(1)}, u32[]{:S(2)}, u32[]{:S(2)}) %collective-permute-start.3) | collective-permute-done | bytes 86048 | tf_op jit(solution)/shard_map/ppermute | solution.py:622
  21.9 0.0 copy-done
  21.9 1.0 %shard_map.149 = (f32[4,32,24,128]{3,2,1,0:T(8,128)S(1)}, f32[16,32,128]{2,1,0:T(8,128)S(1)}) custom-call(f32[24,16,128]{2,1,0:T(8,128)S(1)} %get-tuple-element.28.partial, f32[26,8,128]{2,1,0:T(8,128)S(1)} %collective-permute-done.from_north, f32[26,8,128]{2,1,0:T(8,128)S(1)} %collective-permute-done.1.from_south, f32[24,16,128]{2,1,0:T(8,128)S(1)} %copy-done, ...), custom_call_target="tpu_custom_call" | custom-call | flops 1000000 | bytes 1000000 | tf_op jit(solution)/shard_map/pallas_call | solution.py:565
  22.9 14.1 %all_to_all.15.arrived = f32[16,32,128]{2,1,0:T(8,128)S(1)} all-to-all(f32[16,32,128]{2,1,0:T(8,128)S(1)} %get-tuple-element.42), channel_id=1, replica_groups=mesh['grp'=2,'gx'=16,'gy'=8] {'gx'}, dimensions={0} | all-to-all | bytes 524288 | tf_op jit(solution)/shard_map/all_to_all | solution.py:640
  37.1 16.3 %all_to_all.16.totals = f32[16,8,128]{2,1,0:T(8,128)S(1)} all-to-all(f32[16,8,128]{2,1,0:T(8,128)S(1)} %broadcast_in_dim.4), channel_id=1, replica_groups=mesh['grp'=2,'gx'=16,'gy'=8] {'grp','gy'}, dimensions={0} | all-to-all | bytes 131072 | tf_op jit(solution)/shard_map/all_to_all | solution.py:642
  53.4 0.0 copy-done.10
  53.4 0.0 copy-done.1
  53.4 0.0 copy-done.2
  53.4 0.0 copy-done.3
  53.4 0.0 copy-done.4
  53.4 0.0 copy-start.6
  53.4 4.1 %shard_map.150 = (f32[24,16,128]{2,1,0:T(8,128)}, f32[24,16,128]{2,1,0:T(8,128)}, f32[24,16,128]{2,1,0:T(8,128)}, f32[24,16,128]{2,1,0:T(8,128)}, f32[24,16,128]{2,1,0:T(8,128)}, /*index=5*/f32[16,8,128]{2,1,0:T(8,128)S(1)}) custom-call(s32[8]{0:T(128)S(1)} %bitcast.14, f32[16,8,128]{2,1,0:T(8,128)S(1)} %all_to_all.16.totals, ...), custom_call_target="tpu_custom_call" | custom-call | flops 1000000 | bytes 1000000 | tf_op jit(solution)/shard_map/pallas_call | solution.py:565
  57.5 12.2 %all_to_all.17 = f32[16,8,128]{2,1,0:T(8,128)S(1)} all-to-all(f32[16,8,128]{2,1,0:T(8,128)S(1)} %get-tuple-element.49), channel_id=1, replica_groups=mesh['grp'=2,'gx'=16,'gy'=8] {'gx'}, dimensions={0} | all-to-all | bytes 131072 | tf_op jit(solution)/shard_map/all_to_all | solution.py:670
  69.7 0.0 copy-done.6
  69.7 1.2 %shard_map.151 = f32[16,1024]{1,0:T(8,128)} custom-call(s32[16]{0:T(128)S(1)} %bitcast.13, f32[128,128]{1,0:T(8,128)S(1)} %bitcast.7, f32[16,1024]{1,0:T(8,128)S(1)} %bitcast.9), custom_call_target="tpu_custom_call" | custom-call | flops 1000000 | bytes 1000000 | tf_op jit(solution)/shard_map/pallas_call | solution.py:565
  (4 shorter events, 0.1 us)
Async XLA Ops:
  0.6 21.3 %copy-start = (f32[24,16,128]{2,1,0:T(8,128)S(1)}, f32[24,16,128]{2,1,0:T(8,128)}, u32[]{:S(2)}) copy-start(f32[24,16,128]{2,1,0:T(8,128)} %meridional.3) | copy-start | bytes 589828
  0.6 14.7 %copy-start.7 = (f32[1,1,16,1024]{3,2,1,0:T(8,128)S(1)}, f32[1,1,16,1024]{3,2,1,0:T(8,128)}, u32[]{:S(2)}) copy-start(f32[1,1,16,1024]{3,2,1,0:T(8,128)} %param.18) | copy-start | bytes 196612
  0.7 14.6 %copy-start.9 = (s32[1,1,16]{2,1,0:T(1,128)S(1)}, s32[1,1,16]{2,1,0:T(1,128)}, u32[]{:S(2)}) copy-start(s32[1,1,16]{2,1,0:T(1,128)} %param.16) | copy-start | bytes 196
  0.7 52.7 %copy-start.10 = (s32[1,1,8]{2,1,0:T(1,128)S(1)}, s32[1,1,8]{2,1,0:T(1,128)}, u32[]{:S(2)}) copy-start(s32[1,1,8]{2,1,0:T(1,128)} %param.15) | copy-start | bytes 100
  2.3 51.1 %copy-start.1 = (f32[24,16,128]{2,1,0:T(8,128)S(1)}, f32[24,16,128]{2,1,0:T(8,128)}, u32[]{:S(2)}) copy-start(f32[24,16,128]{2,1,0:T(8,128)} %theta.1) | copy-start | bytes 589828
  2.3 51.1 %copy-start.2 = (f32[24,16,128]{2,1,0:T(8,128)S(1)}, f32[24,16,128]{2,1,0:T(8,128)}, u32[]{:S(2)}) copy-start(f32[24,16,128]{2,1,0:T(8,128)} %humidity.1) | copy-start | bytes 589828
  2.3 51.1 %copy-start.3 = (f32[24,16,128]{2,1,0:T(8,128)S(1)}, f32[24,16,128]{2,1,0:T(8,128)}, u32[]{:S(2)}) copy-start(f32[24,16,128]{2,1,0:T(8,128)} %zonal.1) | copy-start | bytes 589828
  2.3 51.1 %copy-start.4 = (f32[24,16,128]{2,1,0:T(8,128)S(1)}, f32[24,16,128]{2,1,0:T(8,128)}, u32[]{:S(2)}) copy-start(f32[24,16,128]{2,1,0:T(8,128)} %vertical.1) | copy-start | bytes 589828
  2.3 5.1 %collective-permute-start = (f32[26,8,128]{2,1,0:T(8,128)S(1)}, f32[26,8,128]{2,1,0:T(8,128)S(1)}, u32[]{:S(2)}, u32[]{:S(2)}) collective-permute-start(f32[26,8,128]{2,1,0:T(8,128)S(1)} %get-tuple-element.29), channel_id=1, source_target_pairs={{0,7},{1,0},{2,1},{3,2},{4,3},{5,4},{6,5},{7,6},{8,15},{9,8},{10,9... | collective-permute-start | bytes 319496 | tf_op jit(solution)/shard_map/ppermute | solution.py:606
  5.6 1.8 %collective-permute-start.1 = (f32[26,8,128]{2,1,0:T(8,128)S(1)}, f32[26,8,128]{2,1,0:T(8,128)S(1)}, u32[]{:S(2)}, u32[]{:S(2)}) collective-permute-start(f32[26,8,128]{2,1,0:T(8,128)S(1)} %get-tuple-element.30), channel_id=1, source_target_pairs={{0,1},{1,2},{2,3},{3,4},{4,5},{5,6},{6,7},{7,0},{8,9},{9,10},{10,1... | collective-permute-start | bytes 319496 | tf_op jit(solution)/shard_map/ppermute | solution.py:607
  5.6 0.8 %copy-start.5 = (f32[1,1,16,1024]{3,2,1,0:T(8,128)S(1)}, f32[1,1,16,1024]{3,2,1,0:T(8,128)}, u32[]{:S(2)}) copy-start(f32[1,1,16,1024]{3,2,1,0:T(8,128)} %param.17) | copy-start | bytes 196612
  6.4 0.8 %copy-start.8 = (s32[1,1,16,1024]{3,2,1,0:T(8,128)S(1)}, s32[1,1,16,1024]{3,2,1,0:T(8,128)}, u32[]{:S(2)}) copy-start(s32[1,1,16,1024]{3,2,1,0:T(8,128)} %param.19) | copy-start | bytes 196612
  7.4 9.4 %collective-permute-start.2 = (f32[7,24,128]{2,1,0:T(8,128)S(1)}, f32[7,24,128]{2,1,0:T(8,128)S(1)}, u32[]{:S(2)}, u32[]{:S(2)}) collective-permute-start(f32[7,24,128]{2,1,0:T(8,128)S(1)} %get-tuple-element.38.to_west), channel_id=1, source_target_pairs={{0,248},{8,0},{16,8},{24,16},{32,24},{40,32},{48,40},{56,48},{64,5... | collective-permute-start | bytes 258056 | tf_op jit(solution)/shard_map/ppermute | solution.py:621
  15.3 6.7 %collective-permute-start.3 = (f32[7,24,128]{2,1,0:T(8,128)S(1)}, f32[7,24,128]{2,1,0:T(8,128)S(1)}, u32[]{:S(2)}, u32[]{:S(2)}) collective-permute-start(f32[7,24,128]{2,1,0:T(8,128)S(1)} %get-tuple-element.39.to_east), channel_id=1, source_target_pairs={{0,8},{8,16},{16,24},{24,32},{32,40},{40,48},{48,56},{56,64},{64,7... | collective-permute-start | bytes 258056 | tf_op jit(solution)/shard_map/ppermute | solution.py:622
  53.4 16.3 %copy-start.6 = (f32[1,1,16,1024]{3,2,1,0:T(8,128)S(1)}, f32[1,1,16,1024]{3,2,1,0:T(8,128)}, u32[]{:S(2)}) copy-start(f32[1,1,16,1024]{3,2,1,0:T(8,128)} %param.17) | copy-start | bytes 196612

commit v5 on v4

--- a/solution.py
+++ b/solution.py
@@ -196,73 +196,100 @@
         )
 
 
-def power_kernel(
-    partial,
-    from_north,
-    from_south,
-    meridional,
+def power_row(inner, outer, j, i):
+    return inner[j, i] if j < i < CX - 1 - j else outer[j, i]
+
+
+def applied(inner, outer, j, i):
+    _, centre, face, face_below = vertical_profiles()
+    here = ((4.0 + HELMHOLTZ) * centre + face + face_below) * SCALE
+    values = power_row(inner, outer, j, i)
+    lateral = (
+        power_row(inner, outer, j, (i + 1) % EX)
+        + power_row(inner, outer, j, (i - 1) % EX)
+        + turn(values, -1, 0)
+        + turn(values, 1, 0)
+    )
+    return (
+        here * values
+        - (centre * SCALE) * lateral
+        - (face * SCALE) * turn(values, -1, 1)
+        - (face_below * SCALE) * turn(values, 1, 1)
+    )
+
+
+def add_products(sums, inner, outer, rows):
+    sums = list(sums)
+    for i in rows:
+        terms = [power_row(inner, outer, j, i)[0:16] for j in range(ITERS)]
+        terms.append(applied(inner, outer, ITERS - 1, i)[0:16])
+        for k in range(2 * ITERS):
+            product = terms[k // 2] * terms[(k + 1) // 2]
+            sums[k] = sums[k] + (product[0:8] + product[8:16])
+    return sums
+
+
+INNER_ROWS = range(ITERS + 1, CX - ITERS - 1)
+
+
+def inner_kernel(
+    partial, from_north, from_south, meridional, to_west, to_east, inner, products
+):
+    _, centre, _, _ = vertical_profiles()
+    third = centre * (0.5 / TIME_INCREMENT)
+    for i in range(1, CX - 1):
+        if i < 4:
+            inner[0, i] = to_west[i]
+        elif i >= CX - 4:
+            inner[0, i] = to_east[i - (CX - 4)]
+        else:
+            low, high, halo = completed_row(
+                i, partial, meridional[i], from_north, from_south, third
+            )
+            inner[0, i, 0:8] = low
+            inner[0, i, 8:16] = high
+            inner[0, i, 16:24] = halo
+    for j in range(ITERS - 1):
+        for i in range(j + 2, CX - 2 - j):
+            inner[j + 1, i] = applied(inner, None, j, i)
+    sums = [jnp.zeros((8, LEVELS), f32) for _ in range(2 * ITERS)]
+    sums = add_products(sums, inner, None, INNER_ROWS)
+    for k in range(2 * ITERS):
+        products[k] = sums[k]
+
+
+def outer_kernel(
+    inner,
+    products,
     to_west,
     to_east,
     from_east,
     from_west,
     drops,
     live,
-    powers,
+    outer,
     parcels,
 ):
-    _, centre, face, face_below = vertical_profiles()
+    _, centre, _, _ = vertical_profiles()
     third = centre * (0.5 / TIME_INCREMENT)
-    for i in range(4, CX - 4):
-        low, high, halo = completed_row(i, partial, meridional[i], from_north, from_south, third)
-        powers[0, i, 0:8] = low
-        powers[0, i, 8:16] = high
-        powers[0, i, 16:24] = halo
+    outer[0, 0] = to_west[0] + third * from_west[4]
+    outer[0, CX - 1] = to_east[3] - third * from_east[4]
     for t in range(4):
-        west = to_west[t]
-        east = to_east[t]
-        far_east = from_east[t]
-        far_west = from_west[t]
+        east = from_east[t]
+        west = from_west[t]
         if t == 0:
-            west = west + third * from_west[4]
-            far_east = far_east + third * to_east[4]
+            east = east + third * to_east[4]
         if t == 3:
-            east = east - third * from_east[4]
-            far_west = far_west - third * to_west[4]
-        powers[0, t] = west
-        powers[0, CX - 4 + t] = east
-        powers[0, CX + t] = far_east
-        powers[0, CX + 4 + t] = far_west
-    here = ((4.0 + HELMHOLTZ) * centre + face + face_below) * SCALE
-    beside = centre * SCALE
-    above = face * SCALE
-    below = face_below * SCALE
-
-    def applied(j, i):
-        values = powers[j, i]
-        lateral = (
-            powers[j, (i + 1) % EX]
-            + powers[j, (i - 1) % EX]
-            + turn(values, -1, 0)
-            + turn(values, 1, 0)
-        )
-        return (
-            here * values
-            - beside * lateral
-            - above * turn(values, -1, 1)
-            - below * turn(values, 1, 1)
-        )
-
+            west = west - third * to_west[4]
+        outer[0, CX + t] = east
+        outer[0, CX + 4 + t] = west
     for j in range(ITERS - 1):
         reach = ITERS - 1 - j
         for i in range(-reach, CX + reach):
-            powers[j + 1, i % EX] = applied(j, i % EX)
-    sums = [jnp.zeros((8, LEVELS), f32) for _ in range(2 * ITERS)]
-    for i in range(CX):
-        rows = [powers[j, i, 0:16] for j in range(ITERS)]
-        rows.append(applied(ITERS - 1, i)[0:16])
-        for k in range(2 * ITERS):
-            product = rows[k // 2] * rows[(k + 1) // 2]
-            sums[k] = sums[k] + (product[0:8] + product[8:16])
+            if not j + 1 < i < CX - 2 - j:
+                outer[j + 1, i % EX] = applied(inner, outer, j, i % EX)
+    sums = [products[k] for k in range(2 * ITERS)]
+    sums = add_products(sums, inner, outer, [i for i in range(CX) if i not in INNER_ROWS])
     sub8 = iota((8, LEVELS), 0)
     packed = jnp.zeros((8, LEVELS), f32)
     for k in range(2 * ITERS):
@@ -396,7 +423,8 @@
 def step_kernel(
     owners,
     totals,
-    powers,
+    inner,
+    outer,
     arrived,
     theta,
     humidity,
@@ -407,11 +435,11 @@
     from_south,
     from_east,
     from_west,
-    new_theta,
-    new_humidity,
-    new_zonal,
-    new_meridional,
-    new_vertical,
+    far_theta,
+    far_humidity,
+    far_zonal,
+    far_meridional,
+    far_vertical,
     returned,
     potential,
     warmth,
@@ -422,7 +450,25 @@
     picked_excess,
     picked_warmth,
     spans,
+    new_theta,
+    new_humidity,
+    new_zonal,
+    new_meridional,
+    new_vertical,
+    departures,
 ):
+    copies = [
+        pltpu.make_async_copy(near, far, departures.at[n])
+        for n, (near, far) in enumerate(
+            (
+                (new_theta, far_theta),
+                (new_humidity, far_humidity),
+                (new_zonal, far_zonal),
+                (new_meridional, far_meridional),
+                (new_vertical, far_vertical),
+            )
+        )
+    ]
     level, _, _, _ = vertical_profiles()
     sub = iota((CY, LEVELS), 0)
     for i in range(CX):
@@ -445,9 +491,9 @@
     weights = coefficients(totals)
     for t in range(CX + 2):
         i = (t - 1) % EX
-        total = weights[0] * powers[0, i]
+        total = weights[0] * power_row(inner, outer, 0, i)
         for j in range(1, ITERS):
-            total = total + weights[j] * powers[j, i]
+            total = total + weights[j] * power_row(inner, outer, j, i)
         potential[t] = total
     for i in range(CX):
         east, north, up = new_winds(i, potential, theta, humidity, zonal, meridional, vertical)
@@ -467,6 +513,8 @@
         vapour[rows] = moved[1]
         excess[rows] = moved[1] * jnp.exp(-CLAUSIUS_FACTOR * moved[0]) - 1.0
 
+    for copy in copies[2:]:
+        copy.start()
     lane = iota((2 * CX, LEVELS), 1)
     height = iota((BAND, 2 * LEVELS), 0)
     place = iota((2 * CX, 2 * LEVELS), 0)
@@ -542,6 +590,10 @@
         rows = slice(CY * i, CY * (i + 1))
         new_theta[i] = warmth[rows] + PHASE_WARMING * condensed[rows]
         new_humidity[i] = vapour[rows] - condensed[rows]
+    for copy in copies[:2]:
+        copy.start()
+    for copy in copies:
+        copy.wait()
 
 
 def size_kernel(counts, returned, squares, new_squares):
@@ -559,7 +611,7 @@
         )
 
 
-def local(kernel, outs, scalars, operands, scratch=(), far=0, limit=VMEM_LIMIT, cost=1_000_000):
+def local(kernel, outs, scalars, operands, scratch=(), far=0, far_outs=0, limit=VMEM_LIMIT, cost=1_000_000):
     whole = pl.BlockSpec(memory_space=pltpu.VMEM)
     single = len(outs) == 1
     return pl.pallas_call(
@@ -568,7 +620,9 @@
         in_specs=[pl.BlockSpec(memory_space=pltpu.SMEM)] * len(scalars)
         + [pl.BlockSpec(memory_space=pltpu.HBM)] * far
         + [whole] * (len(operands) - far),
-        out_specs=whole if single else [whole] * len(outs),
+        out_specs=whole
+        if single
+        else [pl.BlockSpec(memory_space=pltpu.HBM)] * far_outs + [whole] * (len(outs) - far_outs),
         scratch_shapes=list(scratch),
         compiler_params=pltpu.CompilerParams(vmem_limit_bytes=limit),
         cost_estimate=pl.CostEstimate(flops=cost, bytes_accessed=cost, transcendentals=0),
@@ -620,22 +674,17 @@
     live = local(pack_live_kernel, [shape(SLOT_ROWS * 8, LEVELS)], [counts], [late_numbers], cost=COSTP)
     from_east = lax.ppermute(to_west, tiles, ring(tiles, -1))
     from_west = lax.ppermute(to_east, tiles, ring(tiles, 1))
-    powers, parcels = local(
-        power_kernel,
+    inner, products = local(
+        inner_kernel,
+        [shape(ITERS, CX, EY, LEVELS), shape(2 * ITERS, 8, LEVELS)],
+        [],
+        [partial, from_north, from_south, meridional, to_west, to_east],
+    )
+    outer, parcels = local(
+        outer_kernel,
         [shape(ITERS, EX, EY, LEVELS), shape(SLOT_ROWS, PARCEL, LEVELS)],
         [],
-        [
-            partial,
-            from_north,
-            from_south,
-            meridional,
-            to_west,
-            to_east,
-            from_east,
-            from_west,
-            drops,
-            live,
-        ],
+        [inner, products, to_west, to_east, from_east, from_west, drops, live],
     )
     arrived = lax.all_to_all(parcels, "gx", split_axis=0, concat_axis=0, tiled=True)
     shared = jnp.broadcast_to(jnp.sum(arrived[:, 24:], axis=0)[None], (16, 8, LEVELS))
@@ -648,7 +697,8 @@
         [owners],
         [
             totals,
-            powers,
+            inner,
+            outer,
             arrived,
             theta,
             humidity,
@@ -665,7 +715,10 @@
         + [pltpu.VMEM(picked, f32)]
         + [pltpu.VMEM(flat, f32)] * 2
         + [pltpu.VMEM(picked, f32)] * 2
-        + [pltpu.VMEM((12, CX, CY, LEVELS), f32)],
+        + [pltpu.VMEM((12, CX, CY, LEVELS), f32)]
+        + [pltpu.VMEM((CX, CY, LEVELS), f32)] * 5
+        + [pltpu.SemaphoreType.DMA((5,))],
+        far_outs=5,
     )
     returned = lax.all_to_all(returned, "gx", split_axis=0, concat_axis=0, tiled=True)
     new_squares = local(

time: 71.2 us -> 70.5 us (level)
  waiting for transfers between devices: 6.19 us -> 5.47 us
    ppermute x1, waiting for transfers between devices: 0.94 us -> 0.23 us  [on_device(): from_east = lax.ppermute(to_west, tiles, ring(tiles, -1))]
    pallas_call x7 -> x8, Pallas kernels: 8.49 us -> 8.52 us  [local(): pl.pallas_call(kernel, out_shape=outs[0] if single else outs, in_specs=[p...]
  transfers between devices with their start and end apart: 4 -> 4, of which waited for: 3 -> 3; matrix products, arithmetic and copies ran while one was open for 0% -> 0% of each run, Pallas kernels for 1% -> 2%
where the time goes in v5:
time: 70.5 us; the launch traced here: 70.2 us
  blocking collectives  42.6 us (60%)
  starting transfers between devices  11.1 us (16%)
  Pallas kernels  8.52 us (12%)
  waiting for transfers between devices  5.47 us (8%)
  local copies, waits for them, and re-layouts  1.74 us (2%)
  between operations  0.79 us (1%)
    all_to_all x1, blocking collectives, on_device(): lax.all_to_all(shared, ('grp', 'gy'), split_axis=0, concat_axis=0, tiled=...  16.3 us
    all_to_all x1, blocking collectives, on_device(): lax.all_to_all(parcels, 'gx', split_axis=0, concat_axis=0, tiled=True)  14.1 us
    all_to_all x1, blocking collectives, on_device(): lax.all_to_all(returned, 'gx', split_axis=0, concat_axis=0, tiled=True)  12.2 us
    pallas_call x8, Pallas kernels, local(): pl.pallas_call(kernel, out_shape=outs[0] if single else outs, in_specs=[p...  8.52 us
    ppermute x1, starting transfers between devices, on_device(): from_east = lax.ppermute(to_west, tiles, ring(tiles, -1))  7.85 us
    ppermute x1, waiting for transfers between devices, on_device(): from_west = lax.ppermute(to_east, tiles, ring(tiles, 1))  5.13 us
    ppermute x1, starting transfers between devices, on_device(): from_north = lax.ppermute(to_south, 'gy', ring('gy', -1))  3.25 us
    unnamed x22, local copies, waits for them, and re-layouts  1.73 us
  transfers between devices with their start and end apart: 4, of which 3 were waited for; matrix products, arithmetic and copies ran while one was open for 0% of the time, Pallas kernels for 2%

profile of v5, /device:TPU:1, one launch (start us, length us, event | category | flops | bytes accessed | tf_op | source)
XLA Modules:
  0.0 70.2 jit_solution(16772072815462898298)
XLA Ops:
  0.6 0.0 copy-start
  0.6 0.0 copy-start.7
  0.7 0.0 copy-start.9
  0.7 1.5 %shard_map.145 = (f32[24,16,128]{2,1,0:T(8,128)S(1)}, f32[26,8,128]{2,1,0:T(8,128)S(1)}, f32[26,8,128]{2,1,0:T(8,128)S(1)}, f32[14,16,128]{2,1,0:T(8,128)S(1)}) custom-call(f32[24,16,128]{2,1,0:T(8,128)} %theta.1, f32[24,16,128]{2,1,0:T(8,128)} %humidity.1, f32[24,16,128]{2,1,0:T(8,128)} %zonal.1, f32[24,16,128]{2,1,0:T(8,128)} %meridional.3, ...), custom_call_target="tpu_custom_call" | custom-call | flops 1000000 | bytes 1000000 | tf_op jit(solution)/shard_map/pallas_call | solution.py:617
  2.2 3.3 %collective-permute-start = (f32[26,8,128]{2,1,0:T(8,128)S(1)}, f32[26,8,128]{2,1,0:T(8,128)S(1)}, u32[]{:S(2)}, u32[]{:S(2)}) collective-permute-start(f32[26,8,128]{2,1,0:T(8,128)S(1)} %get-tuple-element.31), channel_id=1, source_target_pairs={{0,7},{1,0},{2,1},{3,2},{4,3},{5,4},{6,5},{7,6},{8,15},{9,8},{10,9... | collective-permute-start | bytes 319496 | tf_op jit(solution)/shard_map/ppermute | solution.py:660
  5.5 0.0 collective-permute-start.1
  5.5 0.0 copy-start.5
  5.5 0.8 %copy-done.5 = f32[1,1,16,1024]{3,2,1,0:T(8,128)S(1)} copy-done((f32[1,1,16,1024]{3,2,1,0:T(8,128)S(1)}, f32[1,1,16,1024]{3,2,1,0:T(8,128)}, u32[]{:S(2)}) %copy-start.5) | copy-done | bytes 65560
  6.3 0.0 copy-start.8
  6.3 0.8 %copy-done.8 = s32[1,1,16,1024]{3,2,1,0:T(8,128)S(1)} copy-done((s32[1,1,16,1024]{3,2,1,0:T(8,128)S(1)}, s32[1,1,16,1024]{3,2,1,0:T(8,128)}, u32[]{:S(2)}) %copy-start.8) | copy-done | bytes 65560
  7.2 0.1 collective-permute-done.from_north
  7.3 0.0 collective-permute-done.1.from_south
  7.3 7.8 %collective-permute-start.2 = (f32[7,24,128]{2,1,0:T(8,128)S(1)}, f32[7,24,128]{2,1,0:T(8,128)S(1)}, u32[]{:S(2)}, u32[]{:S(2)}) collective-permute-start(f32[7,24,128]{2,1,0:T(8,128)S(1)} %get-tuple-element.40.to_west), channel_id=1, source_target_pairs={{0,248},{8,0},{16,8},{24,16},{32,24},{40,32},{48,40},{56,48},{64,5... | collective-permute-start | bytes 258056 | tf_op jit(solution)/shard_map/ppermute | solution.py:675
  15.2 0.0 collective-permute-start.3
  15.2 0.0 copy-done.7
  15.2 0.0 copy-done.9
  15.2 0.6 shard_map.149.live
  15.8 0.0 copy-done
  15.8 0.0 copy-start.1
  15.8 0.0 copy-start.2
  15.8 0.0 copy-start.3
  15.8 0.0 copy-start.4
  15.8 0.0 copy-start.10
  15.8 0.6 shard_map.148
  16.5 0.2 collective-permute-done.2.from_east
  16.7 5.1 %collective-permute-done.3.from_west = f32[7,24,128]{2,1,0:T(8,128)S(1)} collective-permute-done((f32[7,24,128]{2,1,0:T(8,128)S(1)}, f32[7,24,128]{2,1,0:T(8,128)S(1)}, u32[]{:S(2)}, u32[]{:S(2)}) %collective-permute-start.3) | collective-permute-done | bytes 86048 | tf_op jit(solution)/shard_map/ppermute | solution.py:676
  21.8 0.4 shard_map.150
  22.3 14.1 %all_to_all.15.arrived = f32[16,32,128]{2,1,0:T(8,128)S(1)} all-to-all(f32[16,32,128]{2,1,0:T(8,128)S(1)} %get-tuple-element.46), channel_id=1, replica_groups=mesh['grp'=2,'gx'=16,'gy'=8] {'gx'}, dimensions={0} | all-to-all | bytes 524288 | tf_op jit(solution)/shard_map/all_to_all | solution.py:689
  36.4 16.3 %all_to_all.16.totals = f32[16,8,128]{2,1,0:T(8,128)S(1)} all-to-all(f32[16,8,128]{2,1,0:T(8,128)S(1)} %broadcast_in_dim.4), channel_id=1, replica_groups=mesh['grp'=2,'gx'=16,'gy'=8] {'grp','gy'}, dimensions={0} | all-to-all | bytes 131072 | tf_op jit(solution)/shard_map/all_to_all | solution.py:691
  52.7 0.0 copy-done.1
  52.7 0.0 copy-done.2
  52.7 0.0 copy-done.3
  52.7 0.0 copy-done.4
  52.7 0.0 copy-done.10
  52.7 0.0 copy-start.6
  52.7 4.1 %shard_map.151 = (f32[24,16,128]{2,1,0:T(8,128)}, f32[24,16,128]{2,1,0:T(8,128)}, f32[24,16,128]{2,1,0:T(8,128)}, f32[24,16,128]{2,1,0:T(8,128)}, f32[24,16,128]{2,1,0:T(8,128)}, /*index=5*/f32[16,8,128]{2,1,0:T(8,128)S(1)}) custom-call(s32[8]{0:T(128)S(1)} %bitcast.14, f32[16,8,128]{2,1,0:T(8,128)S(1)} %all_to_all.16.totals, ...), custom_call_target="tpu_custom_call" | custom-call | flops 1000000 | bytes 1000000 | tf_op jit(solution)/shard_map/pallas_call | solution.py:617
  56.8 12.2 %all_to_all.17 = f32[16,8,128]{2,1,0:T(8,128)S(1)} all-to-all(f32[16,8,128]{2,1,0:T(8,128)S(1)} %get-tuple-element.53), channel_id=1, replica_groups=mesh['grp'=2,'gx'=16,'gy'=8] {'gx'}, dimensions={0} | all-to-all | bytes 131072 | tf_op jit(solution)/shard_map/all_to_all | solution.py:723
  69.0 0.0 copy-done.6
  69.0 1.2 %shard_map.152 = f32[16,1024]{1,0:T(8,128)} custom-call(s32[16]{0:T(128)S(1)} %bitcast.13, f32[128,128]{1,0:T(8,128)S(1)} %bitcast.7, f32[16,1024]{1,0:T(8,128)S(1)} %bitcast.9), custom_call_target="tpu_custom_call" | custom-call | flops 1000000 | bytes 1000000 | tf_op jit(solution)/shard_map/pallas_call | solution.py:617
  (4 shorter events, 0.1 us)
Async XLA Ops:
  0.6 15.1 %copy-start = (f32[24,16,128]{2,1,0:T(8,128)S(1)}, f32[24,16,128]{2,1,0:T(8,128)}, u32[]{:S(2)}) copy-start(f32[24,16,128]{2,1,0:T(8,128)} %meridional.3) | copy-start | bytes 589828
  0.6 14.6 %copy-start.7 = (f32[1,1,16,1024]{3,2,1,0:T(8,128)S(1)}, f32[1,1,16,1024]{3,2,1,0:T(8,128)}, u32[]{:S(2)}) copy-start(f32[1,1,16,1024]{3,2,1,0:T(8,128)} %param.18) | copy-start | bytes 196612
  0.7 14.5 %copy-start.9 = (s32[1,1,16]{2,1,0:T(1,128)S(1)}, s32[1,1,16]{2,1,0:T(1,128)}, u32[]{:S(2)}) copy-start(s32[1,1,16]{2,1,0:T(1,128)} %param.16) | copy-start | bytes 196
  2.2 5.1 %collective-permute-start = (f32[26,8,128]{2,1,0:T(8,128)S(1)}, f32[26,8,128]{2,1,0:T(8,128)S(1)}, u32[]{:S(2)}, u32[]{:S(2)}) collective-permute-start(f32[26,8,128]{2,1,0:T(8,128)S(1)} %get-tuple-element.31), channel_id=1, source_target_pairs={{0,7},{1,0},{2,1},{3,2},{4,3},{5,4},{6,5},{7,6},{8,15},{9,8},{10,9... | collective-permute-start | bytes 319496 | tf_op jit(solution)/shard_map/ppermute | solution.py:660
  5.5 1.8 %collective-permute-start.1 = (f32[26,8,128]{2,1,0:T(8,128)S(1)}, f32[26,8,128]{2,1,0:T(8,128)S(1)}, u32[]{:S(2)}, u32[]{:S(2)}) collective-permute-start(f32[26,8,128]{2,1,0:T(8,128)S(1)} %get-tuple-element.32), channel_id=1, source_target_pairs={{0,1},{1,2},{2,3},{3,4},{4,5},{5,6},{6,7},{7,0},{8,9},{9,10},{10,1... | collective-permute-start | bytes 319496 | tf_op jit(solution)/shard_map/ppermute | solution.py:661
  5.5 0.8 %copy-start.5 = (f32[1,1,16,1024]{3,2,1,0:T(8,128)S(1)}, f32[1,1,16,1024]{3,2,1,0:T(8,128)}, u32[]{:S(2)}) copy-start(f32[1,1,16,1024]{3,2,1,0:T(8,128)} %param.17) | copy-start | bytes 196612
  6.3 0.8 %copy-start.8 = (s32[1,1,16,1024]{3,2,1,0:T(8,128)S(1)}, s32[1,1,16,1024]{3,2,1,0:T(8,128)}, u32[]{:S(2)}) copy-start(s32[1,1,16,1024]{3,2,1,0:T(8,128)} %param.19) | copy-start | bytes 196612
  7.3 9.4 %collective-permute-start.2 = (f32[7,24,128]{2,1,0:T(8,128)S(1)}, f32[7,24,128]{2,1,0:T(8,128)S(1)}, u32[]{:S(2)}, u32[]{:S(2)}) collective-permute-start(f32[7,24,128]{2,1,0:T(8,128)S(1)} %get-tuple-element.40.to_west), channel_id=1, source_target_pairs={{0,248},{8,0},{16,8},{24,16},{32,24},{40,32},{48,40},{56,48},{64,5... | collective-permute-start | bytes 258056 | tf_op jit(solution)/shard_map/ppermute | solution.py:675
  15.2 6.7 %collective-permute-start.3 = (f32[7,24,128]{2,1,0:T(8,128)S(1)}, f32[7,24,128]{2,1,0:T(8,128)S(1)}, u32[]{:S(2)}, u32[]{:S(2)}) collective-permute-start(f32[7,24,128]{2,1,0:T(8,128)S(1)} %get-tuple-element.41.to_east), channel_id=1, source_target_pairs={{0,8},{8,16},{16,24},{24,32},{32,40},{40,48},{48,56},{56,64},{64,7... | collective-permute-start | bytes 258056 | tf_op jit(solution)/shard_map/ppermute | solution.py:676
  15.8 36.9 %copy-start.1 = (f32[24,16,128]{2,1,0:T(8,128)S(1)}, f32[24,16,128]{2,1,0:T(8,128)}, u32[]{:S(2)}) copy-start(f32[24,16,128]{2,1,0:T(8,128)} %theta.1) | copy-start | bytes 589828
  15.8 36.9 %copy-start.2 = (f32[24,16,128]{2,1,0:T(8,128)S(1)}, f32[24,16,128]{2,1,0:T(8,128)}, u32[]{:S(2)}) copy-start(f32[24,16,128]{2,1,0:T(8,128)} %humidity.1) | copy-start | bytes 589828
  15.8 36.9 %copy-start.3 = (f32[24,16,128]{2,1,0:T(8,128)S(1)}, f32[24,16,128]{2,1,0:T(8,128)}, u32[]{:S(2)}) copy-start(f32[24,16,128]{2,1,0:T(8,128)} %zonal.1) | copy-start | bytes 589828
  15.8 36.9 %copy-start.4 = (f32[24,16,128]{2,1,0:T(8,128)S(1)}, f32[24,16,128]{2,1,0:T(8,128)}, u32[]{:S(2)}) copy-start(f32[24,16,128]{2,1,0:T(8,128)} %vertical.1) | copy-start | bytes 589828
  15.8 36.9 %copy-start.10 = (s32[1,1,8]{2,1,0:T(1,128)S(1)}, s32[1,1,8]{2,1,0:T(1,128)}, u32[]{:S(2)}) copy-start(s32[1,1,8]{2,1,0:T(1,128)} %param.15) | copy-start | bytes 100
  52.7 16.3 %copy-start.6 = (f32[1,1,16,1024]{3,2,1,0:T(8,128)S(1)}, f32[1,1,16,1024]{3,2,1,0:T(8,128)}, u32[]{:S(2)}) copy-start(f32[1,1,16,1024]{3,2,1,0:T(8,128)} %param.17) | copy-start | bytes 196612

commit v6 on v5

--- a/solution.py
+++ b/solution.py
@@ -435,11 +435,11 @@
     from_south,
     from_east,
     from_west,
-    far_theta,
-    far_humidity,
-    far_zonal,
-    far_meridional,
-    far_vertical,
+    new_theta,
+    new_humidity,
+    new_zonal,
+    new_meridional,
+    new_vertical,
     returned,
     potential,
     warmth,
@@ -450,25 +450,7 @@
     picked_excess,
     picked_warmth,
     spans,
-    new_theta,
-    new_humidity,
-    new_zonal,
-    new_meridional,
-    new_vertical,
-    departures,
 ):
-    copies = [
-        pltpu.make_async_copy(near, far, departures.at[n])
-        for n, (near, far) in enumerate(
-            (
-                (new_theta, far_theta),
-                (new_humidity, far_humidity),
-                (new_zonal, far_zonal),
-                (new_meridional, far_meridional),
-                (new_vertical, far_vertical),
-            )
-        )
-    ]
     level, _, _, _ = vertical_profiles()
     sub = iota((CY, LEVELS), 0)
     for i in range(CX):
@@ -513,8 +495,6 @@
         vapour[rows] = moved[1]
         excess[rows] = moved[1] * jnp.exp(-CLAUSIUS_FACTOR * moved[0]) - 1.0
 
-    for copy in copies[2:]:
-        copy.start()
     lane = iota((2 * CX, LEVELS), 1)
     height = iota((BAND, 2 * LEVELS), 0)
     place = iota((2 * CX, 2 * LEVELS), 0)
@@ -590,13 +570,41 @@
         rows = slice(CY * i, CY * (i + 1))
         new_theta[i] = warmth[rows] + PHASE_WARMING * condensed[rows]
         new_humidity[i] = vapour[rows] - condensed[rows]
-    for copy in copies[:2]:
+
+
+def last_kernel(
+    counts,
+    returned,
+    squares,
+    theta,
+    humidity,
+    zonal,
+    meridional,
+    vertical,
+    far_theta,
+    far_humidity,
+    far_zonal,
+    far_meridional,
+    far_vertical,
+    far_squares,
+    new_squares,
+    departures,
+):
+    copies = [
+        pltpu.make_async_copy(near, far, departures.at[n])
+        for n, (near, far) in enumerate(
+            (
+                (theta, far_theta),
+                (humidity, far_humidity),
+                (zonal, far_zonal),
+                (meridional, far_meridional),
+                (vertical, far_vertical),
+                (new_squares, far_squares),
+            )
+        )
+    ]
+    for copy in copies[:5]:
         copy.start()
-    for copy in copies:
-        copy.wait()
-
-
-def size_kernel(counts, returned, squares, new_squares):
     row = iota((SLOT_ROWS, LEVELS), 0)
     lane = iota((SLOT_ROWS, LEVELS), 1)
     live = jnp.zeros((SLOT_ROWS, LEVELS), jnp.int32)
@@ -609,6 +617,9 @@
             returned[pl.ds(s, SLOT_ROWS, stride=CHUNKS), :],
             squares[:, part],
         )
+    copies[5].start()
+    for copy in copies:
+        copy.wait()
 
 
 def local(kernel, outs, scalars, operands, scratch=(), far=0, far_outs=0, limit=VMEM_LIMIT, cost=1_000_000):
@@ -715,26 +726,26 @@
         + [pltpu.VMEM(picked, f32)]
         + [pltpu.VMEM(flat, f32)] * 2
         + [pltpu.VMEM(picked, f32)] * 2
-        + [pltpu.VMEM((12, CX, CY, LEVELS), f32)]
-        + [pltpu.VMEM((CX, CY, LEVELS), f32)] * 5
-        + [pltpu.SemaphoreType.DMA((5,))],
-        far_outs=5,
+        + [pltpu.VMEM((12, CX, CY, LEVELS), f32)],
     )
     returned = lax.all_to_all(returned, "gx", split_axis=0, concat_axis=0, tiled=True)
-    new_squares = local(
-        size_kernel,
-        [shape(SLOT_ROWS, DPB)],
+    *outputs, new_squares = local(
+        last_kernel,
+        [tile] * 5 + [shape(SLOT_ROWS, DPB)],
         [counts],
-        [returned.reshape(SLOT_ROWS * CHUNKS, LEVELS), squares],
-    )
-    return (
-        new_theta,
-        new_humidity,
-        new_zonal,
-        new_meridional,
-        new_vertical,
-        new_squares[None, None],
-    )
+        [
+            returned.reshape(SLOT_ROWS * CHUNKS, LEVELS),
+            squares,
+            new_theta,
+            new_humidity,
+            new_zonal,
+            new_meridional,
+            new_vertical,
+        ],
+        [pltpu.VMEM((SLOT_ROWS, DPB), f32), pltpu.SemaphoreType.DMA((6,))],
+        far_outs=6,
+    )
+    return (*outputs, new_squares[None, None])
 
 
 def solution(mesh):

time: 70.5 us -> 70.1 us (level)
  no operation moved by 1% of the time
where the time goes in v6:
time: 70.1 us; the launch traced here: 69.8 us
  blocking collectives  42.6 us (61%)
  starting transfers between devices  11.1 us (16%)
  Pallas kernels  8.07 us (12%)
  waiting for transfers between devices  5.47 us (8%)
  local copies, waits for them, and re-layouts  1.74 us (2%)
  between operations  0.79 us (1%)
    all_to_all x1, blocking collectives, on_device(): lax.all_to_all(shared, ('grp', 'gy'), split_axis=0, concat_axis=0, tiled=...  16.3 us
    all_to_all x1, blocking collectives, on_device(): lax.all_to_all(parcels, 'gx', split_axis=0, concat_axis=0, tiled=True)  14.1 us
    all_to_all x1, blocking collectives, on_device(): lax.all_to_all(returned, 'gx', split_axis=0, concat_axis=0, tiled=True)  12.2 us
    pallas_call x8, Pallas kernels, local(): pl.pallas_call(kernel, out_shape=outs[0] if single else outs, in_specs=[p...  8.07 us
    ppermute x1, starting transfers between devices, on_device(): from_east = lax.ppermute(to_west, tiles, ring(tiles, -1))  7.85 us
    ppermute x1, waiting for transfers between devices, on_device(): from_west = lax.ppermute(to_east, tiles, ring(tiles, 1))  5.13 us
    ppermute x1, starting transfers between devices, on_device(): from_north = lax.ppermute(to_south, 'gy', ring('gy', -1))  3.25 us
    unnamed x22, local copies, waits for them, and re-layouts  1.73 us
  transfers between devices with their start and end apart: 4, of which 3 were waited for; matrix products, arithmetic and copies ran while one was open for 0% of the time, Pallas kernels for 2%

profile of v6, /device:TPU:1, one launch (start us, length us, event | category | flops | bytes accessed | tf_op | source)
XLA Modules:
  0.0 69.8 jit_solution(16341698141976073880)
XLA Ops:
  0.6 0.0 copy-start
  0.6 0.0 copy-start.7
  0.7 0.0 copy-start.9
  0.7 1.5 %shard_map.145 = (f32[24,16,128]{2,1,0:T(8,128)S(1)}, f32[26,8,128]{2,1,0:T(8,128)S(1)}, f32[26,8,128]{2,1,0:T(8,128)S(1)}, f32[14,16,128]{2,1,0:T(8,128)S(1)}) custom-call(f32[24,16,128]{2,1,0:T(8,128)} %theta.1, f32[24,16,128]{2,1,0:T(8,128)} %humidity.1, f32[24,16,128]{2,1,0:T(8,128)} %zonal.1, f32[24,16,128]{2,1,0:T(8,128)} %meridional.3, ...), custom_call_target="tpu_custom_call" | custom-call | flops 1000000 | bytes 1000000 | tf_op jit(solution)/shard_map/pallas_call | solution.py:628
  2.2 3.3 %collective-permute-start = (f32[26,8,128]{2,1,0:T(8,128)S(1)}, f32[26,8,128]{2,1,0:T(8,128)S(1)}, u32[]{:S(2)}, u32[]{:S(2)}) collective-permute-start(f32[26,8,128]{2,1,0:T(8,128)S(1)} %get-tuple-element.37), channel_id=1, source_target_pairs={{0,7},{1,0},{2,1},{3,2},{4,3},{5,4},{6,5},{7,6},{8,15},{9,8},{10,9... | collective-permute-start | bytes 319496 | tf_op jit(solution)/shard_map/ppermute | solution.py:671
  5.5 0.0 collective-permute-start.1
  5.5 0.0 copy-start.5
  5.5 0.8 %copy-done.5 = f32[1,1,16,1024]{3,2,1,0:T(8,128)S(1)} copy-done((f32[1,1,16,1024]{3,2,1,0:T(8,128)S(1)}, f32[1,1,16,1024]{3,2,1,0:T(8,128)}, u32[]{:S(2)}) %copy-start.5) | copy-done | bytes 65560
  6.3 0.0 copy-start.8
  6.3 0.8 %copy-done.8 = s32[1,1,16,1024]{3,2,1,0:T(8,128)S(1)} copy-done((s32[1,1,16,1024]{3,2,1,0:T(8,128)S(1)}, s32[1,1,16,1024]{3,2,1,0:T(8,128)}, u32[]{:S(2)}) %copy-start.8) | copy-done | bytes 65560
  7.2 0.1 collective-permute-done.from_north
  7.3 0.0 collective-permute-done.1.from_south
  7.3 7.8 %collective-permute-start.2 = (f32[7,24,128]{2,1,0:T(8,128)S(1)}, f32[7,24,128]{2,1,0:T(8,128)S(1)}, u32[]{:S(2)}, u32[]{:S(2)}) collective-permute-start(f32[7,24,128]{2,1,0:T(8,128)S(1)} %get-tuple-element.46.to_west), channel_id=1, source_target_pairs={{0,248},{8,0},{16,8},{24,16},{32,24},{40,32},{48,40},{56,48},{64,5... | collective-permute-start | bytes 258056 | tf_op jit(solution)/shard_map/ppermute | solution.py:686
  15.2 0.0 collective-permute-start.3
  15.2 0.0 copy-done.7
  15.2 0.0 copy-done.9
  15.2 0.6 shard_map.149.live
  15.8 0.0 copy-done
  15.8 0.0 copy-start.1
  15.8 0.0 copy-start.2
  15.8 0.0 copy-start.3
  15.8 0.0 copy-start.4
  15.8 0.0 copy-start.10
  15.8 0.6 shard_map.148
  16.5 0.2 collective-permute-done.2.from_east
  16.7 5.1 %collective-permute-done.3.from_west = f32[7,24,128]{2,1,0:T(8,128)S(1)} collective-permute-done((f32[7,24,128]{2,1,0:T(8,128)S(1)}, f32[7,24,128]{2,1,0:T(8,128)S(1)}, u32[]{:S(2)}, u32[]{:S(2)}) %collective-permute-start.3) | collective-permute-done | bytes 86048 | tf_op jit(solution)/shard_map/ppermute | solution.py:687
  21.8 0.4 shard_map.150
  22.3 14.1 %all_to_all.15.arrived = f32[16,32,128]{2,1,0:T(8,128)S(1)} all-to-all(f32[16,32,128]{2,1,0:T(8,128)S(1)} %get-tuple-element.52), channel_id=1, replica_groups=mesh['grp'=2,'gx'=16,'gy'=8] {'gx'}, dimensions={0} | all-to-all | bytes 524288 | tf_op jit(solution)/shard_map/all_to_all | solution.py:700
  36.4 16.3 %all_to_all.16.totals = f32[16,8,128]{2,1,0:T(8,128)S(1)} all-to-all(f32[16,8,128]{2,1,0:T(8,128)S(1)} %broadcast_in_dim.4), channel_id=1, replica_groups=mesh['grp'=2,'gx'=16,'gy'=8] {'grp','gy'}, dimensions={0} | all-to-all | bytes 131072 | tf_op jit(solution)/shard_map/all_to_all | solution.py:702
  52.7 0.0 copy-done.1
  52.7 0.0 copy-done.2
  52.7 0.0 copy-done.3
  52.7 0.0 copy-done.4
  52.7 0.0 copy-done.10
  52.7 0.0 copy-start.6
  52.7 3.3 %shard_map.151 = (f32[24,16,128]{2,1,0:T(8,128)S(1)}, f32[24,16,128]{2,1,0:T(8,128)S(1)}, f32[24,16,128]{2,1,0:T(8,128)S(1)}, f32[24,16,128]{2,1,0:T(8,128)S(1)}...) custom-call(s32[8]{0:T(128)S(1)} %bitcast.14, f32[16,8,128]{2,1,0:T(8,128)S(1)} %all_to_all.16.totals, ...), custom_call_target="tpu_custom_call" | custom-call | flops 1000000 | bytes 1000000 | tf_op jit(solution)/shard_map/pallas_call | solution.py:628
  56.0 12.2 %all_to_all.17 = f32[16,8,128]{2,1,0:T(8,128)S(1)} all-to-all(f32[16,8,128]{2,1,0:T(8,128)S(1)} %get-tuple-element.54), channel_id=1, replica_groups=mesh['grp'=2,'gx'=16,'gy'=8] {'gx'}, dimensions={0} | all-to-all | bytes 131072 | tf_op jit(solution)/shard_map/all_to_all | solution.py:731
  68.2 0.0 copy-done.6
  68.2 1.5 %shard_map.152 = (f32[24,16,128]{2,1,0:T(8,128)}, f32[24,16,128]{2,1,0:T(8,128)}, f32[24,16,128]{2,1,0:T(8,128)}, f32[24,16,128]{2,1,0:T(8,128)}, f32[24,16,128]{2,1,0:T(8,128)}, /*index=5*/f32[16,1024]{1,0:T(8,128)}) custom-call(s32[16]{0:T(128)S(1)} %bitcast.13, f32[128,128]{1,0:T(8,128)S(1)} %bitcast.7, f32[16,1024]{1,0:T(8,128)S(1)} %bitcast.9, ...), custom_call_target="tpu_custom_call" | custom-call | flops 1000000 | bytes 1000000 | tf_op jit(solution)/shard_map/pallas_call | solution.py:628
  (4 shorter events, 0.1 us)
Async XLA Ops:
  0.6 15.1 %copy-start = (f32[24,16,128]{2,1,0:T(8,128)S(1)}, f32[24,16,128]{2,1,0:T(8,128)}, u32[]{:S(2)}) copy-start(f32[24,16,128]{2,1,0:T(8,128)} %meridional.3) | copy-start | bytes 589828
  0.6 14.6 %copy-start.7 = (f32[1,1,16,1024]{3,2,1,0:T(8,128)S(1)}, f32[1,1,16,1024]{3,2,1,0:T(8,128)}, u32[]{:S(2)}) copy-start(f32[1,1,16,1024]{3,2,1,0:T(8,128)} %param.18) | copy-start | bytes 196612
  0.7 14.5 %copy-start.9 = (s32[1,1,16]{2,1,0:T(1,128)S(1)}, s32[1,1,16]{2,1,0:T(1,128)}, u32[]{:S(2)}) copy-start(s32[1,1,16]{2,1,0:T(1,128)} %param.16) | copy-start | bytes 196
  2.2 5.1 %collective-permute-start = (f32[26,8,128]{2,1,0:T(8,128)S(1)}, f32[26,8,128]{2,1,0:T(8,128)S(1)}, u32[]{:S(2)}, u32[]{:S(2)}) collective-permute-start(f32[26,8,128]{2,1,0:T(8,128)S(1)} %get-tuple-element.37), channel_id=1, source_target_pairs={{0,7},{1,0},{2,1},{3,2},{4,3},{5,4},{6,5},{7,6},{8,15},{9,8},{10,9... | collective-permute-start | bytes 319496 | tf_op jit(solution)/shard_map/ppermute | solution.py:671
  5.5 1.8 %collective-permute-start.1 = (f32[26,8,128]{2,1,0:T(8,128)S(1)}, f32[26,8,128]{2,1,0:T(8,128)S(1)}, u32[]{:S(2)}, u32[]{:S(2)}) collective-permute-start(f32[26,8,128]{2,1,0:T(8,128)S(1)} %get-tuple-element.38), channel_id=1, source_target_pairs={{0,1},{1,2},{2,3},{3,4},{4,5},{5,6},{6,7},{7,0},{8,9},{9,10},{10,1... | collective-permute-start | bytes 319496 | tf_op jit(solution)/shard_map/ppermute | solution.py:672
  5.5 0.8 %copy-start.5 = (f32[1,1,16,1024]{3,2,1,0:T(8,128)S(1)}, f32[1,1,16,1024]{3,2,1,0:T(8,128)}, u32[]{:S(2)}) copy-start(f32[1,1,16,1024]{3,2,1,0:T(8,128)} %param.17) | copy-start | bytes 196612
  6.3 0.8 %copy-start.8 = (s32[1,1,16,1024]{3,2,1,0:T(8,128)S(1)}, s32[1,1,16,1024]{3,2,1,0:T(8,128)}, u32[]{:S(2)}) copy-start(s32[1,1,16,1024]{3,2,1,0:T(8,128)} %param.19) | copy-start | bytes 196612
  7.3 9.4 %collective-permute-start.2 = (f32[7,24,128]{2,1,0:T(8,128)S(1)}, f32[7,24,128]{2,1,0:T(8,128)S(1)}, u32[]{:S(2)}, u32[]{:S(2)}) collective-permute-start(f32[7,24,128]{2,1,0:T(8,128)S(1)} %get-tuple-element.46.to_west), channel_id=1, source_target_pairs={{0,248},{8,0},{16,8},{24,16},{32,24},{40,32},{48,40},{56,48},{64,5... | collective-permute-start | bytes 258056 | tf_op jit(solution)/shard_map/ppermute | solution.py:686
  15.2 6.7 %collective-permute-start.3 = (f32[7,24,128]{2,1,0:T(8,128)S(1)}, f32[7,24,128]{2,1,0:T(8,128)S(1)}, u32[]{:S(2)}, u32[]{:S(2)}) collective-permute-start(f32[7,24,128]{2,1,0:T(8,128)S(1)} %get-tuple-element.47.to_east), channel_id=1, source_target_pairs={{0,8},{8,16},{16,24},{24,32},{32,40},{40,48},{48,56},{56,64},{64,7... | collective-permute-start | bytes 258056 | tf_op jit(solution)/shard_map/ppermute | solution.py:687
  15.8 36.9 %copy-start.1 = (f32[24,16,128]{2,1,0:T(8,128)S(1)}, f32[24,16,128]{2,1,0:T(8,128)}, u32[]{:S(2)}) copy-start(f32[24,16,128]{2,1,0:T(8,128)} %theta.1) | copy-start | bytes 589828
  15.8 36.9 %copy-start.2 = (f32[24,16,128]{2,1,0:T(8,128)S(1)}, f32[24,16,128]{2,1,0:T(8,128)}, u32[]{:S(2)}) copy-start(f32[24,16,128]{2,1,0:T(8,128)} %humidity.1) | copy-start | bytes 589828
  15.8 36.9 %copy-start.3 = (f32[24,16,128]{2,1,0:T(8,128)S(1)}, f32[24,16,128]{2,1,0:T(8,128)}, u32[]{:S(2)}) copy-start(f32[24,16,128]{2,1,0:T(8,128)} %zonal.1) | copy-start | bytes 589828
  15.8 36.9 %copy-start.4 = (f32[24,16,128]{2,1,0:T(8,128)S(1)}, f32[24,16,128]{2,1,0:T(8,128)}, u32[]{:S(2)}) copy-start(f32[24,16,128]{2,1,0:T(8,128)} %vertical.1) | copy-start | bytes 589828
  15.8 36.9 %copy-start.10 = (s32[1,1,8]{2,1,0:T(1,128)S(1)}, s32[1,1,8]{2,1,0:T(1,128)}, u32[]{:S(2)}) copy-start(s32[1,1,8]{2,1,0:T(1,128)} %param.15) | copy-start | bytes 100
  52.7 15.5 %copy-start.6 = (f32[1,1,16,1024]{3,2,1,0:T(8,128)S(1)}, f32[1,1,16,1024]{3,2,1,0:T(8,128)}, u32[]{:S(2)}) copy-start(f32[1,1,16,1024]{3,2,1,0:T(8,128)} %param.17) | copy-start | bytes 196612

commit v7 on v6

--- a/solution.py
+++ b/solution.py
@@ -28,6 +28,7 @@
 LEVELS = 128
 KLO = 48
 BAND = 32
+STRIP = 12
 EX = 32
 EY = 24
 SLOT_ROWS = 16
@@ -81,26 +82,35 @@
     vertical,
     arrivals,
 ):
+    fields = (
+        (zonal_far, zonal),
+        (theta_far, theta),
+        (humidity_far, humidity),
+        (vertical_far, vertical),
+        (meridional_far, meridional),
+    )
     copies = [
-        pltpu.make_async_copy(far, near, arrivals.at[n])
-        for n, (far, near) in enumerate(
-            (
-                (theta_far, theta),
-                (humidity_far, humidity),
-                (zonal_far, zonal),
-                (meridional_far, meridional),
-                (vertical_far, vertical),
-            )
-        )
+        [
+            pltpu.make_async_copy(
+                far.at[first : first + STRIP], near.at[first : first + STRIP], arrivals.at[m, n]
+            )
+            for n, (far, near) in enumerate(fields)
+        ]
+        for m, first in enumerate(range(0, CX, STRIP))
     ]
-    for copy in copies:
-        copy.start()
-    for copy in copies:
-        copy.wait()
+    for strip in copies:
+        for copy in strip:
+            copy.start()
+    copies[0][0].wait()
     level, centre, _, _ = vertical_profiles()
     sub = iota((CY, LEVELS), 0)
     sub8 = iota((8, LEVELS), 0)
     for i in range(CX):
+        if i % STRIP == 0:
+            for copy in copies[i // STRIP][1:]:
+                copy.wait()
+            if i + STRIP < CX:
+                copies[i // STRIP + 1][0].wait()
         weighted = centre * lifted_row(i, theta, humidity, vertical)
         rise = jnp.where(level < LEVELS - 1, turn(weighted, -1, 1), 0.0) - jnp.where(
             level > 0, turn(weighted, 1, 1), 0.0
@@ -526,41 +536,50 @@
                 target[row : row + 1] = value[:, :LEVELS]
                 target[row + 1 : row + 2] = value[:, LEVELS:]
     returned[...] = jnp.zeros(returned.shape, f32)
-    for b in range(NBD):
-        rows = slice(CHUNKS * b, CHUNKS * (b + 1))
-        owner = owners[b]
-        old = arrived[owner, 0:8]
-        number = arrived[owner, 8:16]
-        oversaturation = picked_excess[rows]
-        rate = GROWTH * jnp.exp(GROWTH_SLOPE * picked_warmth[rows])
-        now = old
-        for substep in range(NSUB):
-            now = jnp.maximum(
-                now + 2.0 * SUB_STEP * rate * (oversaturation - CURVATURE / jnp.sqrt(now)),
-                FLOOR_SQUARE,
-            )
-        mass[rows] = jnp.where(
-            number > 0.0, number * (now * jnp.sqrt(now) - old * jnp.sqrt(old)), 0.0
-        )
-        returned[owner] = now
+    blocks = range(NBD)
+    olds = [arrived[owners[b], 0:8] for b in blocks]
+    pulls = [picked_excess[CHUNKS * b : CHUNKS * (b + 1)] for b in blocks]
+    rates = [
+        (2.0 * SUB_STEP * GROWTH)
+        * jnp.exp(GROWTH_SLOPE * picked_warmth[CHUNKS * b : CHUNKS * (b + 1)])
+        for b in blocks
+    ]
+    nows = list(olds)
+    for substep in range(NSUB):
+        curves = [CURVATURE * lax.rsqrt(now) for now in nows]
+        nows = [
+            jnp.maximum(now + rate * (pull - curve), FLOOR_SQUARE)
+            for now, rate, pull, curve in zip(nows, rates, pulls, curves)
+        ]
+    for b in blocks:
+        old, now = olds[b], nows[b]
+        number = arrived[owners[b], 8:16]
+        gain = now * (now * lax.rsqrt(now)) - old * (old * lax.rsqrt(old))
+        mass[CHUNKS * b : CHUNKS * (b + 1)] = jnp.where(number > 0.0, number * gain, 0.0)
+        returned[owners[b]] = now
     for b in range(NBD):
         heights, places = where_at(arrived, owners[b])
         gained = mass[CHUNKS * b : CHUNKS * (b + 1)]
-        total = jnp.zeros((4 * CX, BAND), f32)
+        spreads = []
+        hots = []
         for t in range(CHUNKS // 2):
-            hot = jnp.where(height == chunk(heights, t), 1.0, 0.0).astype(bf16)
+            hots.append(jnp.where(height == chunk(heights, t), 1.0, 0.0).astype(bf16))
             mine = place == chunk(places, t)
-            high, low = halves(chunk(gained, t))
-            spread = jnp.concatenate(
-                [
-                    jnp.where(mine, high, 0.0).astype(bf16),
-                    jnp.where(mine, low, 0.0).astype(bf16),
-                ],
-                axis=0,
-            )
-            total = total + lax.dot_general(
-                spread, hot, (((1,), (1,)), ((), ())), preferred_element_type=f32
-            )
+            spreads.append(
+                jnp.concatenate(
+                    [
+                        jnp.where(mine, part, 0.0).astype(bf16)
+                        for part in halves(chunk(gained, t))
+                    ],
+                    axis=0,
+                )
+            )
+        total = lax.dot_general(
+            jnp.concatenate(spreads, axis=1),
+            jnp.concatenate(hots, axis=1),
+            (((1,), (1,)), ((), ())),
+            preferred_element_type=f32,
+        )
         liquid = CONDENSE * (total[: 2 * CX] + total[2 * CX :])
         liquid = jnp.concatenate([liquid, jnp.zeros((2 * CX, LEVELS - BAND), f32)], axis=1)
         liquid = turn(liquid, KLO, 1)
@@ -664,7 +683,7 @@
         [tile, shape(CX + 2, 8, LEVELS), shape(CX + 2, 8, LEVELS), shape(14, CY, LEVELS)],
         [],
         [theta, humidity, zonal, meridional, vertical],
-        [pltpu.VMEM((CX, CY, LEVELS), f32)] * 5 + [pltpu.SemaphoreType.DMA((5,))],
+        [pltpu.VMEM((CX, CY, LEVELS), f32)] * 5 + [pltpu.SemaphoreType.DMA((CX // STRIP, 5))],
         far=5,
         limit=FIRST_LIMIT,
     )

time: 70.1 us -> 70 us (level)
  no operation moved by 1% of the time
where the time goes in v7:
time: 70 us; the launch traced here: 69.7 us
  blocking collectives  42.6 us (61%)
  starting transfers between devices  11.1 us (16%)
  Pallas kernels  8.03 us (11%)
  waiting for transfers between devices  5.47 us (8%)
  local copies, waits for them, and re-layouts  1.74 us (2%)
  between operations  0.79 us (1%)
    all_to_all x1, blocking collectives, on_device(): lax.all_to_all(shared, ('grp', 'gy'), split_axis=0, concat_axis=0, tiled=...  16.3 us
    all_to_all x1, blocking collectives, on_device(): lax.all_to_all(parcels, 'gx', split_axis=0, concat_axis=0, tiled=True)  14.1 us
    all_to_all x1, blocking collectives, on_device(): lax.all_to_all(returned, 'gx', split_axis=0, concat_axis=0, tiled=True)  12.2 us
    pallas_call x8, Pallas kernels, local(): pl.pallas_call(kernel, out_shape=outs[0] if single else outs, in_specs=[p...  8.03 us
    ppermute x1, starting transfers between devices, on_device(): from_east = lax.ppermute(to_west, tiles, ring(tiles, -1))  7.85 us
    ppermute x1, waiting for transfers between devices, on_device(): from_west = lax.ppermute(to_east, tiles, ring(tiles, 1))  5.13 us
    ppermute x1, starting transfers between devices, on_device(): from_north = lax.ppermute(to_south, 'gy', ring('gy', -1))  3.25 us
    unnamed x22, local copies, waits for them, and re-layouts  1.73 us
  transfers between devices with their start and end apart: 4, of which 3 were waited for; matrix products, arithmetic and copies ran while one was open for 0% of the time, Pallas kernels for 2%

profile of v7, /device:TPU:1, one launch (start us, length us, event | category | flops | bytes accessed | tf_op | source)
XLA Modules:
  0.0 69.7 jit_solution(16619766888770921201)
XLA Ops:
  0.6 0.0 copy-start
  0.6 0.0 copy-start.7
  0.7 0.0 copy-start.9
  0.7 1.5 %shard_map.145 = (f32[24,16,128]{2,1,0:T(8,128)S(1)}, f32[26,8,128]{2,1,0:T(8,128)S(1)}, f32[26,8,128]{2,1,0:T(8,128)S(1)}, f32[14,16,128]{2,1,0:T(8,128)S(1)}) custom-call(f32[24,16,128]{2,1,0:T(8,128)} %theta.1, f32[24,16,128]{2,1,0:T(8,128)} %humidity.1, f32[24,16,128]{2,1,0:T(8,128)} %zonal.1, f32[24,16,128]{2,1,0:T(8,128)} %meridional.3, ...), custom_call_target="tpu_custom_call" | custom-call | flops 1000000 | bytes 1000000 | tf_op jit(solution)/shard_map/pallas_call | solution.py:647
  2.2 3.3 %collective-permute-start = (f32[26,8,128]{2,1,0:T(8,128)S(1)}, f32[26,8,128]{2,1,0:T(8,128)S(1)}, u32[]{:S(2)}, u32[]{:S(2)}) collective-permute-start(f32[26,8,128]{2,1,0:T(8,128)S(1)} %get-tuple-element.37), channel_id=1, source_target_pairs={{0,7},{1,0},{2,1},{3,2},{4,3},{5,4},{6,5},{7,6},{8,15},{9,8},{10,9... | collective-permute-start | bytes 319496 | tf_op jit(solution)/shard_map/ppermute | solution.py:690
  5.5 0.0 collective-permute-start.1
  5.5 0.0 copy-start.5
  5.5 0.8 %copy-done.5 = f32[1,1,16,1024]{3,2,1,0:T(8,128)S(1)} copy-done((f32[1,1,16,1024]{3,2,1,0:T(8,128)S(1)}, f32[1,1,16,1024]{3,2,1,0:T(8,128)}, u32[]{:S(2)}) %copy-start.5) | copy-done | bytes 65560
  6.3 0.0 copy-start.8
  6.3 0.8 %copy-done.8 = s32[1,1,16,1024]{3,2,1,0:T(8,128)S(1)} copy-done((s32[1,1,16,1024]{3,2,1,0:T(8,128)S(1)}, s32[1,1,16,1024]{3,2,1,0:T(8,128)}, u32[]{:S(2)}) %copy-start.8) | copy-done | bytes 65560
  7.2 0.1 collective-permute-done.from_north
  7.3 0.0 collective-permute-done.1.from_south
  7.3 7.8 %collective-permute-start.2 = (f32[7,24,128]{2,1,0:T(8,128)S(1)}, f32[7,24,128]{2,1,0:T(8,128)S(1)}, u32[]{:S(2)}, u32[]{:S(2)}) collective-permute-start(f32[7,24,128]{2,1,0:T(8,128)S(1)} %get-tuple-element.46.to_west), channel_id=1, source_target_pairs={{0,248},{8,0},{16,8},{24,16},{32,24},{40,32},{48,40},{56,48},{64,5... | collective-permute-start | bytes 258056 | tf_op jit(solution)/shard_map/ppermute | solution.py:705
  15.2 0.0 collective-permute-start.3
  15.2 0.0 copy-done.7
  15.2 0.0 copy-done.9
  15.2 0.6 shard_map.149.live
  15.8 0.0 copy-done
  15.8 0.0 copy-start.1
  15.8 0.0 copy-start.2
  15.8 0.0 copy-start.3
  15.8 0.0 copy-start.4
  15.8 0.0 copy-start.10
  15.8 0.6 shard_map.148
  16.5 0.2 collective-permute-done.2.from_east
  16.7 5.1 %collective-permute-done.3.from_west = f32[7,24,128]{2,1,0:T(8,128)S(1)} collective-permute-done((f32[7,24,128]{2,1,0:T(8,128)S(1)}, f32[7,24,128]{2,1,0:T(8,128)S(1)}, u32[]{:S(2)}, u32[]{:S(2)}) %collective-permute-start.3) | collective-permute-done | bytes 86048 | tf_op jit(solution)/shard_map/ppermute | solution.py:706
  21.8 0.4 shard_map.150
  22.3 14.1 %all_to_all.15.arrived = f32[16,32,128]{2,1,0:T(8,128)S(1)} all-to-all(f32[16,32,128]{2,1,0:T(8,128)S(1)} %get-tuple-element.52), channel_id=1, replica_groups=mesh['grp'=2,'gx'=16,'gy'=8] {'gx'}, dimensions={0} | all-to-all | bytes 524288 | tf_op jit(solution)/shard_map/all_to_all | solution.py:719
  36.4 16.3 %all_to_all.16.totals = f32[16,8,128]{2,1,0:T(8,128)S(1)} all-to-all(f32[16,8,128]{2,1,0:T(8,128)S(1)} %broadcast_in_dim.4), channel_id=1, replica_groups=mesh['grp'=2,'gx'=16,'gy'=8] {'grp','gy'}, dimensions={0} | all-to-all | bytes 131072 | tf_op jit(solution)/shard_map/all_to_all | solution.py:721
  52.7 0.0 copy-done.1
  52.7 0.0 copy-done.2
  52.7 0.0 copy-done.3
  52.7 0.0 copy-done.4
  52.7 0.0 copy-done.10
  52.7 0.0 copy-start.6
  52.7 3.2 %shard_map.151 = (f32[24,16,128]{2,1,0:T(8,128)S(1)}, f32[24,16,128]{2,1,0:T(8,128)S(1)}, f32[24,16,128]{2,1,0:T(8,128)S(1)}, f32[24,16,128]{2,1,0:T(8,128)S(1)}...) custom-call(s32[8]{0:T(128)S(1)} %bitcast.14, f32[16,8,128]{2,1,0:T(8,128)S(1)} %all_to_all.16.totals, ...), custom_call_target="tpu_custom_call" | custom-call | flops 1000000 | bytes 1000000 | tf_op jit(solution)/shard_map/pallas_call | solution.py:647
  56.0 12.2 %all_to_all.17 = f32[16,8,128]{2,1,0:T(8,128)S(1)} all-to-all(f32[16,8,128]{2,1,0:T(8,128)S(1)} %get-tuple-element.54), channel_id=1, replica_groups=mesh['grp'=2,'gx'=16,'gy'=8] {'gx'}, dimensions={0} | all-to-all | bytes 131072 | tf_op jit(solution)/shard_map/all_to_all | solution.py:750
  68.2 0.0 copy-done.6
  68.2 1.5 %shard_map.152 = (f32[24,16,128]{2,1,0:T(8,128)}, f32[24,16,128]{2,1,0:T(8,128)}, f32[24,16,128]{2,1,0:T(8,128)}, f32[24,16,128]{2,1,0:T(8,128)}, f32[24,16,128]{2,1,0:T(8,128)}, /*index=5*/f32[16,1024]{1,0:T(8,128)}) custom-call(s32[16]{0:T(128)S(1)} %bitcast.13, f32[128,128]{1,0:T(8,128)S(1)} %bitcast.7, f32[16,1024]{1,0:T(8,128)S(1)} %bitcast.9, ...), custom_call_target="tpu_custom_call" | custom-call | flops 1000000 | bytes 1000000 | tf_op jit(solution)/shard_map/pallas_call | solution.py:647
  (4 shorter events, 0.1 us)
Async XLA Ops:
  0.6 15.1 %copy-start = (f32[24,16,128]{2,1,0:T(8,128)S(1)}, f32[24,16,128]{2,1,0:T(8,128)}, u32[]{:S(2)}) copy-start(f32[24,16,128]{2,1,0:T(8,128)} %meridional.3) | copy-start | bytes 589828
  0.6 14.5 %copy-start.7 = (f32[1,1,16,1024]{3,2,1,0:T(8,128)S(1)}, f32[1,1,16,1024]{3,2,1,0:T(8,128)}, u32[]{:S(2)}) copy-start(f32[1,1,16,1024]{3,2,1,0:T(8,128)} %param.18) | copy-start | bytes 196612
  0.7 14.5 %copy-start.9 = (s32[1,1,16]{2,1,0:T(1,128)S(1)}, s32[1,1,16]{2,1,0:T(1,128)}, u32[]{:S(2)}) copy-start(s32[1,1,16]{2,1,0:T(1,128)} %param.16) | copy-start | bytes 196
  2.2 5.1 %collective-permute-start = (f32[26,8,128]{2,1,0:T(8,128)S(1)}, f32[26,8,128]{2,1,0:T(8,128)S(1)}, u32[]{:S(2)}, u32[]{:S(2)}) collective-permute-start(f32[26,8,128]{2,1,0:T(8,128)S(1)} %get-tuple-element.37), channel_id=1, source_target_pairs={{0,7},{1,0},{2,1},{3,2},{4,3},{5,4},{6,5},{7,6},{8,15},{9,8},{10,9... | collective-permute-start | bytes 319496 | tf_op jit(solution)/shard_map/ppermute | solution.py:690
  5.5 1.8 %collective-permute-start.1 = (f32[26,8,128]{2,1,0:T(8,128)S(1)}, f32[26,8,128]{2,1,0:T(8,128)S(1)}, u32[]{:S(2)}, u32[]{:S(2)}) collective-permute-start(f32[26,8,128]{2,1,0:T(8,128)S(1)} %get-tuple-element.38), channel_id=1, source_target_pairs={{0,1},{1,2},{2,3},{3,4},{4,5},{5,6},{6,7},{7,0},{8,9},{9,10},{10,1... | collective-permute-start | bytes 319496 | tf_op jit(solution)/shard_map/ppermute | solution.py:691
  5.5 0.8 %copy-start.5 = (f32[1,1,16,1024]{3,2,1,0:T(8,128)S(1)}, f32[1,1,16,1024]{3,2,1,0:T(8,128)}, u32[]{:S(2)}) copy-start(f32[1,1,16,1024]{3,2,1,0:T(8,128)} %param.17) | copy-start | bytes 196612
  6.3 0.8 %copy-start.8 = (s32[1,1,16,1024]{3,2,1,0:T(8,128)S(1)}, s32[1,1,16,1024]{3,2,1,0:T(8,128)}, u32[]{:S(2)}) copy-start(s32[1,1,16,1024]{3,2,1,0:T(8,128)} %param.19) | copy-start | bytes 196612
  7.3 9.4 %collective-permute-start.2 = (f32[7,24,128]{2,1,0:T(8,128)S(1)}, f32[7,24,128]{2,1,0:T(8,128)S(1)}, u32[]{:S(2)}, u32[]{:S(2)}) collective-permute-start(f32[7,24,128]{2,1,0:T(8,128)S(1)} %get-tuple-element.46.to_west), channel_id=1, source_target_pairs={{0,248},{8,0},{16,8},{24,16},{32,24},{40,32},{48,40},{56,48},{64,5... | collective-permute-start | bytes 258056 | tf_op jit(solution)/shard_map/ppermute | solution.py:705
  15.2 6.7 %collective-permute-start.3 = (f32[7,24,128]{2,1,0:T(8,128)S(1)}, f32[7,24,128]{2,1,0:T(8,128)S(1)}, u32[]{:S(2)}, u32[]{:S(2)}) collective-permute-start(f32[7,24,128]{2,1,0:T(8,128)S(1)} %get-tuple-element.47.to_east), channel_id=1, source_target_pairs={{0,8},{8,16},{16,24},{24,32},{32,40},{40,48},{48,56},{56,64},{64,7... | collective-permute-start | bytes 258056 | tf_op jit(solution)/shard_map/ppermute | solution.py:706
  15.8 36.9 %copy-start.1 = (f32[24,16,128]{2,1,0:T(8,128)S(1)}, f32[24,16,128]{2,1,0:T(8,128)}, u32[]{:S(2)}) copy-start(f32[24,16,128]{2,1,0:T(8,128)} %theta.1) | copy-start | bytes 589828
  15.8 36.9 %copy-start.2 = (f32[24,16,128]{2,1,0:T(8,128)S(1)}, f32[24,16,128]{2,1,0:T(8,128)}, u32[]{:S(2)}) copy-start(f32[24,16,128]{2,1,0:T(8,128)} %humidity.1) | copy-start | bytes 589828
  15.8 36.9 %copy-start.3 = (f32[24,16,128]{2,1,0:T(8,128)S(1)}, f32[24,16,128]{2,1,0:T(8,128)}, u32[]{:S(2)}) copy-start(f32[24,16,128]{2,1,0:T(8,128)} %zonal.1) | copy-start | bytes 589828
  15.8 36.9 %copy-start.4 = (f32[24,16,128]{2,1,0:T(8,128)S(1)}, f32[24,16,128]{2,1,0:T(8,128)}, u32[]{:S(2)}) copy-start(f32[24,16,128]{2,1,0:T(8,128)} %vertical.1) | copy-start | bytes 589828
  15.8 36.9 %copy-start.10 = (s32[1,1,8]{2,1,0:T(1,128)S(1)}, s32[1,1,8]{2,1,0:T(1,128)}, u32[]{:S(2)}) copy-start(s32[1,1,8]{2,1,0:T(1,128)} %param.15) | copy-start | bytes 100
  52.7 15.4 %copy-start.6 = (f32[1,1,16,1024]{3,2,1,0:T(8,128)S(1)}, f32[1,1,16,1024]{3,2,1,0:T(8,128)}, u32[]{:S(2)}) copy-start(f32[1,1,16,1024]{3,2,1,0:T(8,128)} %param.17) | copy-start | bytes 196612

commit v8 on v7

--- a/solution.py
+++ b/solution.py
@@ -28,7 +28,6 @@
 LEVELS = 128
 KLO = 48
 BAND = 32
-STRIP = 12
 EX = 32
 EY = 24
 SLOT_ROWS = 16
@@ -82,35 +81,26 @@
     vertical,
     arrivals,
 ):
-    fields = (
-        (zonal_far, zonal),
-        (theta_far, theta),
-        (humidity_far, humidity),
-        (vertical_far, vertical),
-        (meridional_far, meridional),
-    )
     copies = [
-        [
-            pltpu.make_async_copy(
-                far.at[first : first + STRIP], near.at[first : first + STRIP], arrivals.at[m, n]
-            )
-            for n, (far, near) in enumerate(fields)
-        ]
-        for m, first in enumerate(range(0, CX, STRIP))
+        pltpu.make_async_copy(far, near, arrivals.at[n])
+        for n, (far, near) in enumerate(
+            (
+                (theta_far, theta),
+                (humidity_far, humidity),
+                (zonal_far, zonal),
+                (meridional_far, meridional),
+                (vertical_far, vertical),
+            )
+        )
     ]
-    for strip in copies:
-        for copy in strip:
-            copy.start()
-    copies[0][0].wait()
+    for copy in copies:
+        copy.start()
+    for copy in copies:
+        copy.wait()
     level, centre, _, _ = vertical_profiles()
     sub = iota((CY, LEVELS), 0)
     sub8 = iota((8, LEVELS), 0)
     for i in range(CX):
-        if i % STRIP == 0:
-            for copy in copies[i // STRIP][1:]:
-                copy.wait()
-            if i + STRIP < CX:
-                copies[i // STRIP + 1][0].wait()
         weighted = centre * lifted_row(i, theta, humidity, vertical)
         rise = jnp.where(level < LEVELS - 1, turn(weighted, -1, 1), 0.0) - jnp.where(
             level > 0, turn(weighted, 1, 1), 0.0
@@ -683,7 +673,7 @@
         [tile, shape(CX + 2, 8, LEVELS), shape(CX + 2, 8, LEVELS), shape(14, CY, LEVELS)],
         [],
         [theta, humidity, zonal, meridional, vertical],
-        [pltpu.VMEM((CX, CY, LEVELS), f32)] * 5 + [pltpu.SemaphoreType.DMA((CX // STRIP, 5))],
+        [pltpu.VMEM((CX, CY, LEVELS), f32)] * 5 + [pltpu.SemaphoreType.DMA((5,))],
         far=5,
         limit=FIRST_LIMIT,
     )

time: 70 us -> 70 us (level)
  no operation moved by 1% of the time
where the time goes in v8:
time: 70 us; the launch traced here: 69.7 us
  blocking collectives  42.6 us (61%)
  starting transfers between devices  11.1 us (16%)
  Pallas kernels  8.03 us (11%)
  waiting for transfers between devices  5.47 us (8%)
  local copies, waits for them, and re-layouts  1.74 us (2%)
  between operations  0.79 us (1%)
    all_to_all x1, blocking collectives, on_device(): lax.all_to_all(shared, ('grp', 'gy'), split_axis=0, concat_axis=0, tiled=...  16.3 us
    all_to_all x1, blocking collectives, on_device(): lax.all_to_all(parcels, 'gx', split_axis=0, concat_axis=0, tiled=True)  14.1 us
    all_to_all x1, blocking collectives, on_device(): lax.all_to_all(returned, 'gx', split_axis=0, concat_axis=0, tiled=True)  12.2 us
    pallas_call x8, Pallas kernels, local(): pl.pallas_call(kernel, out_shape=outs[0] if single else outs, in_specs=[p...  8.03 us
    ppermute x1, starting transfers between devices, on_device(): from_east = lax.ppermute(to_west, tiles, ring(tiles, -1))  7.85 us
    ppermute x1, waiting for transfers between devices, on_device(): from_west = lax.ppermute(to_east, tiles, ring(tiles, 1))  5.13 us
    ppermute x1, starting transfers between devices, on_device(): from_north = lax.ppermute(to_south, 'gy', ring('gy', -1))  3.25 us
    unnamed x22, local copies, waits for them, and re-layouts  1.73 us
  transfers between devices with their start and end apart: 4, of which 3 were waited for; matrix products, arithmetic and copies ran while one was open for 0% of the time, Pallas kernels for 2%

profile of v8, /device:TPU:1, one launch (start us, length us, event | category | flops | bytes accessed | tf_op | source)
XLA Modules:
  0.0 69.7 jit_solution(945001405603040045)
XLA Ops:
  0.6 0.0 copy-start
  0.6 0.0 copy-start.7
  0.7 0.0 copy-start.9
  0.7 1.5 %shard_map.145 = (f32[24,16,128]{2,1,0:T(8,128)S(1)}, f32[26,8,128]{2,1,0:T(8,128)S(1)}, f32[26,8,128]{2,1,0:T(8,128)S(1)}, f32[14,16,128]{2,1,0:T(8,128)S(1)}) custom-call(f32[24,16,128]{2,1,0:T(8,128)} %theta.1, f32[24,16,128]{2,1,0:T(8,128)} %humidity.1, f32[24,16,128]{2,1,0:T(8,128)} %zonal.1, f32[24,16,128]{2,1,0:T(8,128)} %meridional.3, ...), custom_call_target="tpu_custom_call" | custom-call | flops 1000000 | bytes 1000000 | tf_op jit(solution)/shard_map/pallas_call | solution.py:637
  2.2 3.3 %collective-permute-start = (f32[26,8,128]{2,1,0:T(8,128)S(1)}, f32[26,8,128]{2,1,0:T(8,128)S(1)}, u32[]{:S(2)}, u32[]{:S(2)}) collective-permute-start(f32[26,8,128]{2,1,0:T(8,128)S(1)} %get-tuple-element.37), channel_id=1, source_target_pairs={{0,7},{1,0},{2,1},{3,2},{4,3},{5,4},{6,5},{7,6},{8,15},{9,8},{10,9... | collective-permute-start | bytes 319496 | tf_op jit(solution)/shard_map/ppermute | solution.py:680
  5.5 0.0 collective-permute-start.1
  5.5 0.0 copy-start.5
  5.5 0.8 %copy-done.5 = f32[1,1,16,1024]{3,2,1,0:T(8,128)S(1)} copy-done((f32[1,1,16,1024]{3,2,1,0:T(8,128)S(1)}, f32[1,1,16,1024]{3,2,1,0:T(8,128)}, u32[]{:S(2)}) %copy-start.5) | copy-done | bytes 65560
  6.3 0.0 copy-start.8
  6.3 0.8 %copy-done.8 = s32[1,1,16,1024]{3,2,1,0:T(8,128)S(1)} copy-done((s32[1,1,16,1024]{3,2,1,0:T(8,128)S(1)}, s32[1,1,16,1024]{3,2,1,0:T(8,128)}, u32[]{:S(2)}) %copy-start.8) | copy-done | bytes 65560
  7.2 0.1 collective-permute-done.from_north
  7.3 0.0 collective-permute-done.1.from_south
  7.3 7.8 %collective-permute-start.2 = (f32[7,24,128]{2,1,0:T(8,128)S(1)}, f32[7,24,128]{2,1,0:T(8,128)S(1)}, u32[]{:S(2)}, u32[]{:S(2)}) collective-permute-start(f32[7,24,128]{2,1,0:T(8,128)S(1)} %get-tuple-element.46.to_west), channel_id=1, source_target_pairs={{0,248},{8,0},{16,8},{24,16},{32,24},{40,32},{48,40},{56,48},{64,5... | collective-permute-start | bytes 258056 | tf_op jit(solution)/shard_map/ppermute | solution.py:695
  15.2 0.0 collective-permute-start.3
  15.2 0.0 copy-done.7
  15.2 0.0 copy-done.9
  15.2 0.6 shard_map.149.live
  15.8 0.0 copy-done
  15.8 0.0 copy-start.1
  15.8 0.0 copy-start.2
  15.8 0.0 copy-start.3
  15.8 0.0 copy-start.4
  15.8 0.0 copy-start.10
  15.8 0.6 shard_map.148
  16.5 0.2 collective-permute-done.2.from_east
  16.7 5.1 %collective-permute-done.3.from_west = f32[7,24,128]{2,1,0:T(8,128)S(1)} collective-permute-done((f32[7,24,128]{2,1,0:T(8,128)S(1)}, f32[7,24,128]{2,1,0:T(8,128)S(1)}, u32[]{:S(2)}, u32[]{:S(2)}) %collective-permute-start.3) | collective-permute-done | bytes 86048 | tf_op jit(solution)/shard_map/ppermute | solution.py:696
  21.8 0.4 shard_map.150
  22.3 14.1 %all_to_all.15.arrived = f32[16,32,128]{2,1,0:T(8,128)S(1)} all-to-all(f32[16,32,128]{2,1,0:T(8,128)S(1)} %get-tuple-element.52), channel_id=1, replica_groups=mesh['grp'=2,'gx'=16,'gy'=8] {'gx'}, dimensions={0} | all-to-all | bytes 524288 | tf_op jit(solution)/shard_map/all_to_all | solution.py:709
  36.4 16.3 %all_to_all.16.totals = f32[16,8,128]{2,1,0:T(8,128)S(1)} all-to-all(f32[16,8,128]{2,1,0:T(8,128)S(1)} %broadcast_in_dim.4), channel_id=1, replica_groups=mesh['grp'=2,'gx'=16,'gy'=8] {'grp','gy'}, dimensions={0} | all-to-all | bytes 131072 | tf_op jit(solution)/shard_map/all_to_all | solution.py:711
  52.7 0.0 copy-done.1
  52.7 0.0 copy-done.2
  52.7 0.0 copy-done.3
  52.7 0.0 copy-done.4
  52.7 0.0 copy-done.10
  52.7 0.0 copy-start.6
  52.7 3.2 %shard_map.151 = (f32[24,16,128]{2,1,0:T(8,128)S(1)}, f32[24,16,128]{2,1,0:T(8,128)S(1)}, f32[24,16,128]{2,1,0:T(8,128)S(1)}, f32[24,16,128]{2,1,0:T(8,128)S(1)}...) custom-call(s32[8]{0:T(128)S(1)} %bitcast.14, f32[16,8,128]{2,1,0:T(8,128)S(1)} %all_to_all.16.totals, ...), custom_call_target="tpu_custom_call" | custom-call | flops 1000000 | bytes 1000000 | tf_op jit(solution)/shard_map/pallas_call | solution.py:637
  56.0 12.2 %all_to_all.17 = f32[16,8,128]{2,1,0:T(8,128)S(1)} all-to-all(f32[16,8,128]{2,1,0:T(8,128)S(1)} %get-tuple-element.54), channel_id=1, replica_groups=mesh['grp'=2,'gx'=16,'gy'=8] {'gx'}, dimensions={0} | all-to-all | bytes 131072 | tf_op jit(solution)/shard_map/all_to_all | solution.py:740
  68.2 0.0 copy-done.6
  68.2 1.5 %shard_map.152 = (f32[24,16,128]{2,1,0:T(8,128)}, f32[24,16,128]{2,1,0:T(8,128)}, f32[24,16,128]{2,1,0:T(8,128)}, f32[24,16,128]{2,1,0:T(8,128)}, f32[24,16,128]{2,1,0:T(8,128)}, /*index=5*/f32[16,1024]{1,0:T(8,128)}) custom-call(s32[16]{0:T(128)S(1)} %bitcast.13, f32[128,128]{1,0:T(8,128)S(1)} %bitcast.7, f32[16,1024]{1,0:T(8,128)S(1)} %bitcast.9, ...), custom_call_target="tpu_custom_call" | custom-call | flops 1000000 | bytes 1000000 | tf_op jit(solution)/shard_map/pallas_call | solution.py:637
  (4 shorter events, 0.1 us)
Async XLA Ops:
  0.6 15.1 %copy-start = (f32[24,16,128]{2,1,0:T(8,128)S(1)}, f32[24,16,128]{2,1,0:T(8,128)}, u32[]{:S(2)}) copy-start(f32[24,16,128]{2,1,0:T(8,128)} %meridional.3) | copy-start | bytes 589828
  0.6 14.6 %copy-start.7 = (f32[1,1,16,1024]{3,2,1,0:T(8,128)S(1)}, f32[1,1,16,1024]{3,2,1,0:T(8,128)}, u32[]{:S(2)}) copy-start(f32[1,1,16,1024]{3,2,1,0:T(8,128)} %param.18) | copy-start | bytes 196612
  0.7 14.5 %copy-start.9 = (s32[1,1,16]{2,1,0:T(1,128)S(1)}, s32[1,1,16]{2,1,0:T(1,128)}, u32[]{:S(2)}) copy-start(s32[1,1,16]{2,1,0:T(1,128)} %param.16) | copy-start | bytes 196
  2.2 5.1 %collective-permute-start = (f32[26,8,128]{2,1,0:T(8,128)S(1)}, f32[26,8,128]{2,1,0:T(8,128)S(1)}, u32[]{:S(2)}, u32[]{:S(2)}) collective-permute-start(f32[26,8,128]{2,1,0:T(8,128)S(1)} %get-tuple-element.37), channel_id=1, source_target_pairs={{0,7},{1,0},{2,1},{3,2},{4,3},{5,4},{6,5},{7,6},{8,15},{9,8},{10,9... | collective-permute-start | bytes 319496 | tf_op jit(solution)/shard_map/ppermute | solution.py:680
  5.5 1.8 %collective-permute-start.1 = (f32[26,8,128]{2,1,0:T(8,128)S(1)}, f32[26,8,128]{2,1,0:T(8,128)S(1)}, u32[]{:S(2)}, u32[]{:S(2)}) collective-permute-start(f32[26,8,128]{2,1,0:T(8,128)S(1)} %get-tuple-element.38), channel_id=1, source_target_pairs={{0,1},{1,2},{2,3},{3,4},{4,5},{5,6},{6,7},{7,0},{8,9},{9,10},{10,1... | collective-permute-start | bytes 319496 | tf_op jit(solution)/shard_map/ppermute | solution.py:681
  5.5 0.8 %copy-start.5 = (f32[1,1,16,1024]{3,2,1,0:T(8,128)S(1)}, f32[1,1,16,1024]{3,2,1,0:T(8,128)}, u32[]{:S(2)}) copy-start(f32[1,1,16,1024]{3,2,1,0:T(8,128)} %param.17) | copy-start | bytes 196612
  6.3 0.8 %copy-start.8 = (s32[1,1,16,1024]{3,2,1,0:T(8,128)S(1)}, s32[1,1,16,1024]{3,2,1,0:T(8,128)}, u32[]{:S(2)}) copy-start(s32[1,1,16,1024]{3,2,1,0:T(8,128)} %param.19) | copy-start | bytes 196612
  7.3 9.4 %collective-permute-start.2 = (f32[7,24,128]{2,1,0:T(8,128)S(1)}, f32[7,24,128]{2,1,0:T(8,128)S(1)}, u32[]{:S(2)}, u32[]{:S(2)}) collective-permute-start(f32[7,24,128]{2,1,0:T(8,128)S(1)} %get-tuple-element.46.to_west), channel_id=1, source_target_pairs={{0,248},{8,0},{16,8},{24,16},{32,24},{40,32},{48,40},{56,48},{64,5... | collective-permute-start | bytes 258056 | tf_op jit(solution)/shard_map/ppermute | solution.py:695
  15.2 6.7 %collective-permute-start.3 = (f32[7,24,128]{2,1,0:T(8,128)S(1)}, f32[7,24,128]{2,1,0:T(8,128)S(1)}, u32[]{:S(2)}, u32[]{:S(2)}) collective-permute-start(f32[7,24,128]{2,1,0:T(8,128)S(1)} %get-tuple-element.47.to_east), channel_id=1, source_target_pairs={{0,8},{8,16},{16,24},{24,32},{32,40},{40,48},{48,56},{56,64},{64,7... | collective-permute-start | bytes 258056 | tf_op jit(solution)/shard_map/ppermute | solution.py:696
  15.8 36.9 %copy-start.1 = (f32[24,16,128]{2,1,0:T(8,128)S(1)}, f32[24,16,128]{2,1,0:T(8,128)}, u32[]{:S(2)}) copy-start(f32[24,16,128]{2,1,0:T(8,128)} %theta.1) | copy-start | bytes 589828
  15.8 36.9 %copy-start.2 = (f32[24,16,128]{2,1,0:T(8,128)S(1)}, f32[24,16,128]{2,1,0:T(8,128)}, u32[]{:S(2)}) copy-start(f32[24,16,128]{2,1,0:T(8,128)} %humidity.1) | copy-start | bytes 589828
  15.8 36.9 %copy-start.3 = (f32[24,16,128]{2,1,0:T(8,128)S(1)}, f32[24,16,128]{2,1,0:T(8,128)}, u32[]{:S(2)}) copy-start(f32[24,16,128]{2,1,0:T(8,128)} %zonal.1) | copy-start | bytes 589828
  15.8 36.9 %copy-start.4 = (f32[24,16,128]{2,1,0:T(8,128)S(1)}, f32[24,16,128]{2,1,0:T(8,128)}, u32[]{:S(2)}) copy-start(f32[24,16,128]{2,1,0:T(8,128)} %vertical.1) | copy-start | bytes 589828
  15.8 36.9 %copy-start.10 = (s32[1,1,8]{2,1,0:T(1,128)S(1)}, s32[1,1,8]{2,1,0:T(1,128)}, u32[]{:S(2)}) copy-start(s32[1,1,8]{2,1,0:T(1,128)} %param.15) | copy-start | bytes 100
  52.7 15.4 %copy-start.6 = (f32[1,1,16,1024]{3,2,1,0:T(8,128)S(1)}, f32[1,1,16,1024]{3,2,1,0:T(8,128)}, u32[]{:S(2)}) copy-start(f32[1,1,16,1024]{3,2,1,0:T(8,128)} %param.17) | copy-start | bytes 196612
